TPU v7x, 32 devices: a whole 2x2x4 slice. The times are simulated.
32 devices in a mesh: groups: 2 (over y), expert: 4 (over z), dp: 4 (over x, core).
Axes of the slice: x: 2, y: 2, z: 4, core: 2. Of those that a mesh axis runs over, the one named last changes fastest.
Arguments:
- tokens: bfloat16 [16384, 1024], P(('groups', 'expert', 'dp')), parts along dimension 0, may hold values from -100 to 100
- routes: int32 [16384, 2], P(('groups', 'expert', 'dp')), parts along dimension 0, may hold values from 0 to 3, all different within a row; in each aligned block of 512 rows (0 to 511, 512 to 1023, ...) at most 320 rows name the same one
- w_orig: float32 [4, 512, 1024], P('expert', 'dp'), may hold values from -6 to 6
- mask: int32 [4, 512, 1024], P('expert', 'dp'), may hold values from 0 to 1, as said below
Outputs:
- w_pruned: float32 [8, 512, 1024], P(('groups', 'expert'), 'dp'), parts along dimension 0
There are 2 independent parts, one for each index of `groups`. A program takes and returns all parts, laid end to end along the dimension named above; an argument that names none is the same for every part. Nothing has to cross between parts.
Inputs may be any that keep to these rules, and one draw needn't show every extreme that they name: `routes`: in the rows of one device each expert is named by at most 320 rows, a bound that some block reaches; the 2 experts of a token differ. `mask`: each aligned group of four consecutive entries along the last dimension holds exactly two ones.
All inputs are finite; a program needn't handle non-finite values.
Results may differ from a plain program's by a relative error of at most 0.0008.
Values may be sent and summed in bfloat16 or wider, within the bound.
No kernel may reach another device: no remote copies, remote signals or barrier semaphores. Data moves between devices by JAX's collectives and lax.ppermute only.
A program may use at most 64 MiB of HBM per device.

v0:
```python
import jax
import jax.numpy as jnp
from jax import lax
from jax.sharding import PartitionSpec as P

STEPS = 3


step_scale = 1.5


def full_product(rows):
    return lax.dot_general(rows, rows, (((0,), (0,)), ((), ())), preferred_element_type=jnp.float32)


def local(tokens, routes, w_orig, mask):
    experts_n = lax.axis_size("expert")
    tok_rows, topk_count = routes.shape
    width = tokens.shape[1]
    capacity = max(2, min(tok_rows, 5 * tok_rows * topk_count // (4 * experts_n)))
    flat_routes = routes.reshape(-1)
    onehot = (flat_routes[:, None] == jnp.arange(experts_n, dtype=jnp.int32)[None, :]).astype(
        jnp.int32
    )
    before = jnp.cumsum(onehot, axis=0) - onehot
    slot_index = jnp.sum(before * onehot, axis=1)
    target = flat_routes * capacity + slot_index
    source = jnp.arange(flat_routes.shape[0], dtype=jnp.int32) // topk_count
    buffer = jnp.zeros((experts_n * capacity, width), jnp.bfloat16).at[target].set(tokens[source])
    outgoing = buffer.reshape(experts_n, capacity, width)
    arrived = lax.all_to_all(outgoing, "expert", split_axis=0, concat_axis=0, tiled=True).reshape(
        experts_n * capacity, width
    )
    local_terms = full_product(arrived)
    gram_matrix = lax.psum(local_terms.astype(jnp.bfloat16), "dp").astype(jnp.float32)
    frobenius = jnp.sqrt(jnp.sum(gram_matrix * gram_matrix) + 1e-06)
    rate_value = step_scale / frobenius
    dense_copy = w_orig[0]
    keep_mask = mask[0].astype(jnp.float32)
    weights = keep_mask * dense_copy
    for section in range(STEPS):
        change = weights - dense_copy
        gradient = jnp.dot(
            change, gram_matrix, precision=lax.Precision.HIGHEST, preferred_element_type=jnp.float32
        )
        weights = keep_mask * (weights - rate_value * gradient)
    return weights[None]


def solution(mesh):
    placed = (
        P(("groups", "expert", "dp"), None),
        P(("groups", "expert", "dp"), None),
        P("expert", "dp", None),
        P("expert", "dp", None),
    )
    return jax.shard_map(
        local,
        mesh=mesh,
        in_specs=placed,
        out_specs=P(("groups", "expert"), "dp", None),
        check_vma=False,
    )
```

profile of v0, /device:TPU:1, one launch (start us, length us, event | category | flops | bytes accessed | tf_op | source)
XLA Modules:
  0.0 161.7 jit_solution(4249164424961093475)
XLA Ops:
  6.5 0.0 copy-start
  6.5 0.0 all-reduce.2.cloned.1.call-start
  6.6 0.8 broadcast_multiply_fusion
  7.3 0.8 copy.6
  8.2 0.2 eq.29
  8.3 0.2 eq.25
  8.5 0.1 copy.5
  8.7 0.2 mul.51
  8.9 1.1 reduce-window.6
  10.0 0.2 slice_reduce_fusion
  10.2 0.2 reduce-window.9
  10.4 0.1 add_bitcast_fusion
  10.5 0.0 copy-done
  10.5 14.5 %scatter_custom_fusion = bf16[1280,1024]{1,0:T(8,128)(2,1)} fusion(s32[1024]{0:T(1024)S(1)} %bitcast.58, bf16[512,1024]{1,0:T(8,128)(2,1)S(1)} %copy-done, s32[1024]{0:T(1024)S(1)} %broadcast_clamp_fusion, bf16[]{:T(256)} %constant.27.clone.1), kind=kCustom, calls=%fused_computation.4 | custom fusion | bytes 2621442 | tf_op jit(solution)/shard_map/scatter | solution.py:29
  25.0 64.0 %all_to_all.5 = bf16[4,320,1024]{2,1,0:T(8,128)(2,1)S(1)} all-to-all(bf16[4,320,1024]{2,1,0:T(8,128)(2,1)} %bitcast.54), channel_id=1, replica_groups=mesh['groups'=2,'expert'=4,'dp'=4] {'expert'}, dimensions={0} | all-to-all | bytes 5242880 | tf_op jit(solution)/shard_map/all_to_all | solution.py:31
  89.0 4.2 %bitcast_convert_fusion = bf16[1024,1024]{1,0:T(8,128)(2,1)} fusion(bf16[4,320,1024]{2,1,0:T(8,128)(2,1)S(1)} %all_to_all.5), kind=kOutput, calls=%fused_computation.2 | convolution fusion | flops 2685403136 | bytes 4718592 | tf_op jit(solution)/shard_map/dot_general | solution.py:13
  93.2 0.0 all-reduce.2.cloned.1.call-update
  93.2 51.9 %all-reduce.2.cloned.1.call-done = bf16[1024,1024]{1,0:T(8,128)(2,1)} async-done(((bf16[1024,1024]{1,0:T(8,128)(2,1)}), bf16[1024,1024]{1,0:T(8,128)(2,1)}) %all-reduce.2.cloned.1.call-update) | async-done | bytes 2097168 | tf_op jit(solution)/shard_map/psum | solution.py:35
  145.1 0.0 copy-start.1
  145.1 3.4 %multiply_reduce_fusion = f32[]{:T(128)} fusion(bf16[1024,1024]{1,0:T(8,128)(2,1)} %all-reduce.2.cloned.1.call-done), kind=kLoop, calls=%fused_computation.3 | loop fusion | flops 3145727 | bytes 2097156 | tf_op jit(solution)/shard_map/reduce_sum | solution.py:36
  149.2 0.0 copy-done.1
  149.2 0.0 copy-start.2
  149.2 0.0 copy-start.3
  149.2 2.7 %fusion.9 = f32[128,1024]{1,0:T(8,128)S(1)} fusion(bf16[1024,1024]{1,0:T(8,128)(2,1)S(1)} %copy-done.1, f32[1,128,1024]{2,1,0:T(8,128)} %param.6, s32[1,128,1024]{2,1,0:T(8,128)} %param.7, f32[]{:T(128)S(6)} %div.10), kind=kOutput, calls=%fused_computation.16 | convolution fusion | flops 1611661312 | bytes 3670020 | tf_op jit(solution)/shard_map/dot_general | solution.py:43
  151.9 0.0 copy-done.2
  151.9 0.0 copy-done.3
  151.9 1.1 fusion.7
  153.0 1.9 %fusion.5 = f32[1,128,1024]{2,1,0:T(8,128)} fusion(f32[128,1024]{1,0:T(8,128)S(1)} %fusion.7, bf16[1024,1024]{1,0:T(8,128)(2,1)S(1)} %copy-done.1, f32[1,128,1024]{2,1,0:T(8,128)S(1)} %copy-done.2, s32[1,128,1024]{2,1,0:T(8,128)S(1)} %copy-done.3, f32[]{:T(128)S(6)} %div.10), kind=kOutput, calls=%fused_computation.10 | convolution fusion | flops 1611268096 | bytes 4194308 | tf_op jit(solution)/shard_map/dot_general | solution.py:43
  (5 shorter events, 0.1 us)
Async XLA Ops:
  6.5 4.0 %copy-start = (bf16[512,1024]{1,0:T(8,128)(2,1)S(1)}, bf16[512,1024]{1,0:T(8,128)(2,1)}, u32[]{:S(2)}) copy-start(bf16[512,1024]{1,0:T(8,128)(2,1)} %param.4) | copy-start | bytes 3145732
  6.5 138.5 %all-reduce.2.cloned.1.call-start = ((), (), s32[]{:S(2)}) async-start(), calls=%async_computation.1 | async-start | bytes 4194304 | tf_op jit(solution)/shard_map/psum | solution.py:35
  145.1 4.1 %copy-start.1 = (bf16[1024,1024]{1,0:T(8,128)(2,1)S(1)}, bf16[1024,1024]{1,0:T(8,128)(2,1)}, u32[]{:S(2)}) copy-start(bf16[1024,1024]{1,0:T(8,128)(2,1)} %all-reduce.2.cloned.1.call-done) | copy-start | bytes 6291460
  149.2 2.7 %copy-start.2 = (f32[1,128,1024]{2,1,0:T(8,128)S(1)}, f32[1,128,1024]{2,1,0:T(8,128)}, u32[]{:S(2)}) copy-start(f32[1,128,1024]{2,1,0:T(8,128)} %param.6) | copy-start | bytes 1572868
  149.2 2.7 %copy-start.3 = (s32[1,128,1024]{2,1,0:T(8,128)S(1)}, s32[1,128,1024]{2,1,0:T(8,128)}, u32[]{:S(2)}) copy-start(s32[1,128,1024]{2,1,0:T(8,128)} %param.7) | copy-start | bytes 1572868
Sparse Core Ops, SparseCore 0:
  93.3 51.6 all-reduce.1
where the time goes:
time: 163 us; the launch traced here: 162 us
  blocking collectives  64 us (39%)
  waiting for transfers between devices  51.9 us (32%)
  local copies, waits for them, and re-layouts  16.2 us (10%)
  between operations  14.2 us (9%)
  matrix products  9.75 us (6%)
  other arithmetic  5.66 us (3%)
    all_to_all x1, blocking collectives, local(): lax.all_to_all(outgoing, 'expert', split_axis=0, concat_axis=0, tiled=True)  64 us
    psum x1, waiting for transfers between devices, local(): lax.psum(local_terms.astype(jnp.bfloat16), 'dp').astype(jnp.float32)  51.9 us
    scatter x1, local copies, waits for them, and re-layouts, local(): jnp.zeros((experts_n * capacity, width), jnp.bfloat16).at[target]  14.5 us
    dot_general x3, matrix products, local(): jnp.dot(change, gram_matrix, precision=lax.Precision.HIGHEST, preferred_e...  5.59 us
    dot_general x1, matrix products, full_product(): lax.dot_general(rows, rows, (((0,), (0,)), ((), ())), preferred_element_t...  4.16 us
    reduce_sum x1, other arithmetic, local(): frobenius = jnp.sqrt(jnp.sum(gram_matrix * gram_matrix) + 1e-06)  3.42 us
  transfers between devices with their start and end apart: 1, of which 1 were waited for; matrix products, arithmetic and copies ran while one was open for 0% of the time, Pallas kernels for 0%

commit v1 on v0

--- a/solution.py
+++ b/solution.py
@@ -1,19 +1,28 @@
+import functools
+
 import jax
 import jax.numpy as jnp
 from jax import lax
+from jax.experimental import pallas as pl
+from jax.experimental.pallas import tpu as pltpu
 from jax.sharding import PartitionSpec as P
 
 STEPS = 3
 
 
 step_scale = 1.5
+
+BLK = 128
+PIECE = 32
+VMEM = pl.BlockSpec(memory_space=pltpu.VMEM)
+SMEM = pl.BlockSpec(memory_space=pltpu.SMEM)
 
 
 def full_product(rows):
     return lax.dot_general(rows, rows, (((0,), (0,)), ((), ())), preferred_element_type=jnp.float32)
 
 
-def local(tokens, routes, w_orig, mask):
+def local_rows(tokens, routes, w_orig, mask):
     experts_n = lax.axis_size("expert")
     tok_rows, topk_count = routes.shape
     width = tokens.shape[1]
@@ -47,6 +56,156 @@
     return weights[None]
 
 
+def turn_kernel(where, tokens, routes_t, out):
+    width = tokens.shape[1]
+    out[0:width, :] = tokens[...].T
+    experts = lax.broadcasted_iota(jnp.int32, (16, tokens.shape[0]), 0) ^ where[0]
+    named = experts == routes_t[0:1, :]
+    for k in range(1, routes_t.shape[0]):
+        named = named | (experts == routes_t[k : k + 1, :])
+    out[width : width + 16, :] = named.astype(jnp.float32).astype(jnp.bfloat16)
+
+
+def gram_kernel(panels, experts, where, mine, other, keep, send, lhs):
+    width = mine.shape[0] - 16
+    toks = mine.shape[1]
+    group = 2 * experts * PIECE
+    row = 64 * where[2]
+    at_keep = row + PIECE * where[1]
+    at_send = row + PIECE * (1 - where[1])
+    blocks = 2 * max(panels) + 2
+    for half, source in enumerate((mine, other)):
+        flags = source[width : width + 16, :]
+        lanes = slice(half * toks, (half + 1) * toks)
+        for k in range(blocks):
+            for s, at in enumerate((at_keep, at_send)):
+                rows = source[pl.ds(pl.multiple_of(at + BLK * k, PIECE), PIECE), :]
+                for e in range(experts):
+                    first = group * k + experts * PIECE * s + PIECE * e
+                    lhs[first : first + PIECE, lanes] = rows * flags[e : e + 1, :]
+    base = 0
+    for j in panels:
+        used = lhs[0 : group * (2 * j + 2), :]
+        total = lax.dot_general(
+            used[:, 0:toks], mine[256 * j : 256 * j + 256, :], (((1,), (1,)), ((), ())),
+            preferred_element_type=jnp.float32)
+        total = total + lax.dot_general(
+            used[:, toks:], other[256 * j : 256 * j + 256, :], (((1,), (1,)), ((), ())),
+            preferred_element_type=jnp.float32)
+        for side in range(2):
+            for k in range(2 * j + side + 1):
+                for s, out in enumerate((keep, send)):
+                    for e in range(experts):
+                        first = group * k + experts * PIECE * s + PIECE * e
+                        out[e, base + PIECE * k : base + PIECE * (k + 1), :] = total[
+                            first : first + PIECE, BLK * side : BLK * (side + 1)].astype(out.dtype)
+            base += PIECE * (2 * j + side + 1)
+
+
+def pair_kernel(keep, got, own, *outs):
+    for e, out in enumerate((own,) + outs):
+        out[...] = (keep[e] + got[e].astype(jnp.float32)).astype(out.dtype)
+
+
+def sum_kernel(own, *refs):
+    total = own[...]
+    for ref in refs[:-1]:
+        total = total + ref[...].astype(jnp.float32)
+    refs[-1][...] = total.astype(jnp.bfloat16)
+
+
+def steps_kernel(chunks, where, w_ref, mask_ref, *refs):
+    pieces, (out, gram) = refs[:-2], refs[-2:]
+    width = w_ref.shape[1]
+    core, x = where[2], where[1]
+    ats = (64 * core + PIECE * x, 64 * (1 - core) + PIECE * x,
+           64 * core + PIECE * (1 - x), 64 * (1 - core) + PIECE * (1 - x))
+    square = jnp.zeros((PIECE, BLK), jnp.float32)
+    n = 0
+    for panels in chunks:
+        for at in ats:
+            piece, base = pieces[n], 0
+            n += 1
+            for j in panels:
+                for c in (2 * j, 2 * j + 1):
+                    for k in range(c + 1):
+                        block = piece[base : base + PIECE, :]
+                        base += PIECE
+                        gram[pl.ds(pl.multiple_of(at + BLK * k, PIECE), PIECE), BLK * c : BLK * (c + 1)] = block
+                        value = block.astype(jnp.float32)
+                        square = square + value * value * (1.0 if k == c else 2.0)
+    for c in range(width // BLK):
+        for k in range(c):
+            gram[BLK * c : BLK * (c + 1), BLK * k : BLK * (k + 1)] = gram[
+                BLK * k : BLK * (k + 1), BLK * c : BLK * (c + 1)].T
+    rate = step_scale / jnp.sqrt(jnp.sum(square) + 1e-06)
+    dense = w_ref[...]
+    keep = mask_ref[...].astype(jnp.float32)
+    weights = keep * dense
+    rows = dense.shape[0]
+    for section in range(STEPS):
+        change = weights - dense
+        high = change.astype(jnp.bfloat16)
+        low = (change - high.astype(jnp.float32)).astype(jnp.bfloat16)
+        both = jnp.dot(jnp.concatenate([high, low], axis=0), gram[...], preferred_element_type=jnp.float32)
+        weights = keep * (weights - rate * (both[0:rows] + both[rows:]))
+    out[...] = weights
+
+
+def params(mib=48):
+    return pltpu.CompilerParams(vmem_limit_bytes=mib << 20)
+
+
+def local_grams(chunks, tokens, routes, w_orig, mask):
+    toks, width = tokens.shape
+    experts = lax.axis_size("expert")
+    z, dp = lax.axis_index("expert"), lax.axis_index("dp")
+    where = jnp.stack([z, dp // 2, dp % 2]).astype(jnp.int32)
+    over_core = [(d, d ^ 1) for d in range(4)]
+    over_x = [(d, d ^ 2) for d in range(4)]
+    bf16, f32 = jnp.bfloat16, jnp.float32
+    turned = pl.pallas_call(
+        turn_kernel, in_specs=[SMEM, VMEM, VMEM], out_specs=VMEM,
+        out_shape=jax.ShapeDtypeStruct((width + 16, toks), bf16), compiler_params=params(),
+    )(where, tokens, routes.T)
+    other = lax.ppermute(turned, "dp", over_core)
+    pieces = []
+    for panels in chunks:
+        rows = PIECE * sum(4 * j + 3 for j in panels)
+        keep, send = pl.pallas_call(
+            functools.partial(gram_kernel, panels, experts),
+            in_specs=[SMEM, VMEM, VMEM], out_specs=[VMEM, VMEM],
+            out_shape=[jax.ShapeDtypeStruct((experts, rows, BLK), f32),
+                       jax.ShapeDtypeStruct((experts, rows, BLK), bf16)],
+            scratch_shapes=[pltpu.VMEM((2 * experts * PIECE * (2 * max(panels) + 2), 2 * toks), bf16)],
+            compiler_params=params(),
+        )(where, turned, other)
+        got = lax.ppermute(send, "dp", over_x)
+        own, *away = pl.pallas_call(
+            pair_kernel, in_specs=[VMEM] * 2, out_specs=[VMEM] * experts,
+            out_shape=[jax.ShapeDtypeStruct((rows, BLK), f32)]
+            + [jax.ShapeDtypeStruct((rows, BLK), bf16)] * (experts - 1),
+            compiler_params=params(),
+        )(keep, got)
+        came = [lax.ppermute(a, "expert", [(i, i ^ (s + 1)) for i in range(experts)])
+                for s, a in enumerate(away)]
+        final = pl.pallas_call(
+            sum_kernel, in_specs=[VMEM] * experts, out_specs=VMEM,
+            out_shape=jax.ShapeDtypeStruct((rows, BLK), bf16), compiler_params=params(),
+        )(own, *came)
+        by_core = lax.ppermute(final, "dp", over_core)
+        by_x = lax.ppermute(final, "dp", over_x)
+        by_both = lax.ppermute(by_x, "dp", over_core)
+        pieces += [final, by_core, by_x, by_both]
+    out = pl.pallas_call(
+        functools.partial(steps_kernel, chunks),
+        in_specs=[SMEM] + [VMEM] * (2 + len(pieces)), out_specs=VMEM,
+        out_shape=jax.ShapeDtypeStruct(w_orig.shape[1:], f32),
+        scratch_shapes=[pltpu.VMEM((width, width), bf16)], compiler_params=params(),
+    )(where, w_orig[0], mask[0], *pieces)
+    return out[None]
+
+
 def solution(mesh):
     placed = (
         P(("groups", "expert", "dp"), None),
@@ -54,6 +213,8 @@
         P("expert", "dp", None),
         P("expert", "dp", None),
     )
+    few = mesh.shape["expert"] == 4 and mesh.shape["dp"] == 4
+    local = functools.partial(local_grams, ((3,), (2,), (0, 1))) if few else local_rows
     return jax.shard_map(
         local,
         mesh=mesh,

time: 163 us -> 63.8 us (0.39)
  blocking collectives: 64 us -> 0 us
  waiting for transfers between devices: 51.9 us -> 28.4 us
  starting transfers between devices: 0.01 us -> 22.7 us
  local copies, waits for them, and re-layouts: 16.2 us -> 1.92 us
  between operations: 14.2 us -> 0.12 us
  Pallas kernels: 0 us -> 10.1 us
  matrix products: 9.75 us -> 0 us
  other arithmetic: 5.66 us -> 0.08 us
    all_to_all x1 -> x0, blocking collectives: 64 us -> none  [local(): lax.all_to_all(outgoing, 'expert', split_axis=0, concat_axis=0, tiled=True)]
    psum x1 -> x0, waiting for transfers between devices: 51.9 us -> none  [local(): lax.psum(local_terms.astype(jnp.bfloat16), 'dp').astype(jnp.float32)]
    ppermute x0 -> x22, waiting for transfers between devices: none -> 28.4 us  [the longest x3 16.3 us: local_grams(): got = lax.ppermute(send, 'dp', over_x)]
    ppermute x0 -> x22, starting transfers between devices: none -> 22.7 us  [the longest x9 11.8 us: local_grams(): lax.ppermute(a, 'expert', [(i, i ^ s + 1) for i in range(experts)])]
    scatter x1 -> x0, local copies, waits for them, and re-layouts: 14.5 us -> none  [local(): jnp.zeros((experts_n * capacity, width), jnp.bfloat16).at[target]]
    pallas_call x0 -> x11, Pallas kernels: none -> 10.1 us  [the longest x3 4.94 us: local_grams(): pl.pallas_call(functools.partial(gram_kernel, panels, experts), in_specs=...]
    dot_general x4 -> x0, matrix products: 9.75 us -> none  [the longest x3 5.59 us: local(): jnp.dot(change, gram_matrix, precision=lax.Precision.HIGHEST, preferred_e...]
    reduce_sum x2 -> x0, other arithmetic: 3.45 us -> none  [the longest x1 3.42 us: local(): frobenius = jnp.sqrt(jnp.sum(gram_matrix * gram_matrix) + 1e-06)]
  transfers between devices with their start and end apart: 1 -> 22, of which waited for: 1 -> 7; matrix products, arithmetic and copies ran while one was open for 0% -> 0% of each run, Pallas kernels for 0% -> 5%
where the time goes in v1:
time: 63.8 us; the launch traced here: 63.3 us
  waiting for transfers between devices  28.4 us (45%)
  starting transfers between devices  22.7 us (36%)
  Pallas kernels  10.1 us (16%)
  local copies, waits for them, and re-layouts  1.92 us (3%)
    ppermute x3, waiting for transfers between devices, local_grams(): got = lax.ppermute(send, 'dp', over_x)  16.3 us
    ppermute x9, starting transfers between devices, local_grams(): lax.ppermute(a, 'expert', [(i, i ^ s + 1) for i in range(experts)])  11.8 us
    ppermute x9, waiting for transfers between devices, local_grams(): lax.ppermute(a, 'expert', [(i, i ^ s + 1) for i in range(experts)])  6.79 us
    pallas_call x3, Pallas kernels, local_grams(): pl.pallas_call(functools.partial(gram_kernel, panels, experts), in_specs=...  4.94 us
    ppermute x3, starting transfers between devices, local_grams(): got = lax.ppermute(send, 'dp', over_x)  3.99 us
    pallas_call x1, Pallas kernels, local_grams(): pl.pallas_call(functools.partial(steps_kernel, chunks), in_specs=[SMEM] +...  3.94 us
    ppermute x3, starting transfers between devices, local_grams(): by_x = lax.ppermute(final, 'dp', over_x)  3.33 us
    ppermute x1, waiting for transfers between devices, local_grams(): other = lax.ppermute(turned, 'dp', over_core)  2.63 us
  transfers between devices with their start and end apart: 22, of which 7 were waited for; matrix products, arithmetic and copies ran while one was open for 0% of the time, Pallas kernels for 5%

profile of v1, /device:TPU:1, one launch (start us, length us, event | category | flops | bytes accessed | tf_op | source)
XLA Modules:
  0.0 63.3 jit_solution(700304265041223798)
XLA Ops:
  0.0 0.1 pad_add_fusion.where
  0.1 0.0 copy-start
  0.1 1.2 %copy-done = bf16[512,1024]{1,0:T(8,128)(2,1)S(1)} copy-done((bf16[512,1024]{1,0:T(8,128)(2,1)S(1)}, bf16[512,1024]{1,0:T(8,128)(2,1)}, u32[]{:S(2)}) %copy-start) | copy-done | bytes 1048600
  1.3 0.0 copy-start.3
  1.3 0.7 %copy-done.3 = s32[512,2]{0,1:T(2,128)S(1)} copy-done((s32[512,2]{0,1:T(2,128)S(1)}, s32[512,2]{0,1:T(2,128)}, u32[]{:S(2)}) %copy-start.3) | copy-done | bytes 4120
  2.0 0.9 %shard_map.46.mine = bf16[1040,512]{1,0:T(8,128)(2,1)S(1)} custom-call(s32[3]{0:T(128)S(1)} %pad_add_fusion.where, bf16[512,1024]{1,0:T(8,128)(2,1)S(1)} %copy-done, s32[2,512]{1,0:T(2,128)S(1)} %bitcast.9), custom_call_target="tpu_custom_call" | custom-call | tf_op jit(solution)/shard_map/pallas_call | solution.py:167
  2.9 0.1 collective-permute-start
  3.0 2.6 %collective-permute-done.other = bf16[1040,512]{1,0:T(8,128)(2,1)S(1)} collective-permute-done((bf16[1040,512]{1,0:T(8,128)(2,1)S(1)}, bf16[1040,512]{1,0:T(8,128)(2,1)S(1)}, u32[]{:S(2)}, u32[]{:S(2)}) %collective-permute-start) | collective-permute-done | bytes 1064992 | tf_op jit(solution)/shard_map/ppermute | solution.py:171
  5.6 1.8 %shard_map.47 = (f32[4,480,128]{2,1,0:T(8,128)S(1)}, bf16[4,480,128]{2,1,0:T(8,128)(2,1)S(1)}) custom-call(s32[3]{0:T(128)S(1)} %pad_add_fusion.where, bf16[1040,512]{1,0:T(8,128)(2,1)S(1)} %shard_map.46.mine, bf16[1040,512]{1,0:T(8,128)(2,1)S(1)} %collective-permute-done.other), custom_call_target="tpu_custom_call" | custom-call | tf_op jit(solution)/shard_map/pallas_call | solution.py:175
  7.4 2.4 %collective-permute-start.1 = (bf16[4,480,128]{2,1,0:T(8,128)(2,1)S(1)}, bf16[4,480,128]{2,1,0:T(8,128)(2,1)S(1)}, u32[]{:S(2)}, u32[]{:S(2)}) collective-permute-start(bf16[4,480,128]{2,1,0:T(8,128)(2,1)S(1)} %get-tuple-element.24), channel_id=1, source_target_pairs={{0,2},{1,3},{2,0},{3,1},{4,6},{5,7},{6,4},{7,5},{8,10},{9,11},{10,... | collective-permute-start | bytes 1474568 | tf_op jit(solution)/shard_map/ppermute | solution.py:183
  9.8 1.6 %shard_map.50 = (f32[4,352,128]{2,1,0:T(8,128)S(1)}, bf16[4,352,128]{2,1,0:T(8,128)(2,1)S(1)}) custom-call(s32[3]{0:T(128)S(1)} %pad_add_fusion.where, bf16[1040,512]{1,0:T(8,128)(2,1)S(1)} %shard_map.46.mine, bf16[1040,512]{1,0:T(8,128)(2,1)S(1)} %collective-permute-done.other), custom_call_target="tpu_custom_call" | custom-call | tf_op jit(solution)/shard_map/pallas_call | solution.py:175
  11.4 0.1 collective-permute-start.8
  11.5 1.6 %shard_map.53 = (f32[4,320,128]{2,1,0:T(8,128)S(1)}, bf16[4,320,128]{2,1,0:T(8,128)(2,1)S(1)}) custom-call(s32[3]{0:T(128)S(1)} %pad_add_fusion.where, bf16[1040,512]{1,0:T(8,128)(2,1)S(1)} %shard_map.46.mine, bf16[1040,512]{1,0:T(8,128)(2,1)S(1)} %collective-permute-done.other), custom_call_target="tpu_custom_call" | custom-call | tf_op jit(solution)/shard_map/pallas_call | solution.py:175
  13.1 1.5 %collective-permute-start.15 = (bf16[4,320,128]{2,1,0:T(8,128)(2,1)S(1)}, bf16[4,320,128]{2,1,0:T(8,128)(2,1)S(1)}, u32[]{:S(2)}, u32[]{:S(2)}) collective-permute-start(bf16[4,320,128]{2,1,0:T(8,128)(2,1)S(1)} %get-tuple-element.36), channel_id=1, source_target_pairs={{0,2},{1,3},{2,0},{3,1},{4,6},{5,7},{6,4},{7,5},{8,10},{9,11},{10,... | collective-permute-start | bytes 983048 | tf_op jit(solution)/shard_map/ppermute | solution.py:183
  14.6 6.6 %collective-permute-done.1.got = bf16[4,480,128]{2,1,0:T(8,128)(2,1)S(1)} collective-permute-done((bf16[4,480,128]{2,1,0:T(8,128)(2,1)S(1)}, bf16[4,480,128]{2,1,0:T(8,128)(2,1)S(1)}, u32[]{:S(2)}, u32[]{:S(2)}) %collective-permute-start.1) | collective-permute-done | bytes 491552 | tf_op jit(solution)/shard_map/ppermute | solution.py:183
  21.1 0.1 shard_map.48
  21.2 1.3 %collective-permute-start.2 = (bf16[480,128]{1,0:T(8,128)(2,1)S(1)}, bf16[480,128]{1,0:T(8,128)(2,1)S(1)}, u32[]{:S(2)}, u32[]{:S(2)}) collective-permute-start(bf16[480,128]{1,0:T(8,128)(2,1)S(1)} %get-tuple-element.26), channel_id=1, source_target_pairs={{0,4},{4,0},{8,12},{12,8},{1,5},{5,1},{9,13},{13,9},{2,6},{6,2},{1... | collective-permute-start | bytes 368648 | tf_op jit(solution)/shard_map/ppermute | solution.py:190
  22.5 2.3 %collective-permute-start.3 = (bf16[480,128]{1,0:T(8,128)(2,1)S(1)}, bf16[480,128]{1,0:T(8,128)(2,1)S(1)}, u32[]{:S(2)}, u32[]{:S(2)}) collective-permute-start(bf16[480,128]{1,0:T(8,128)(2,1)S(1)} %get-tuple-element.27), channel_id=1, source_target_pairs={{0,8},{4,12},{8,0},{12,4},{1,9},{5,13},{9,1},{13,5},{2,10},{6,14},... | collective-permute-start | bytes 368648 | tf_op jit(solution)/shard_map/ppermute | solution.py:190
  24.8 0.0 collective-permute-start.4
  24.8 4.0 %collective-permute-done.8.got = bf16[4,352,128]{2,1,0:T(8,128)(2,1)S(1)} collective-permute-done((bf16[4,352,128]{2,1,0:T(8,128)(2,1)S(1)}, bf16[4,352,128]{2,1,0:T(8,128)(2,1)S(1)}, u32[]{:S(2)}, u32[]{:S(2)}) %collective-permute-start.8) | collective-permute-done | bytes 360480 | tf_op jit(solution)/shard_map/ppermute | solution.py:183
  28.9 0.1 shard_map.51
  28.9 1.3 %collective-permute-start.9 = (bf16[352,128]{1,0:T(8,128)(2,1)S(1)}, bf16[352,128]{1,0:T(8,128)(2,1)S(1)}, u32[]{:S(2)}, u32[]{:S(2)}) collective-permute-start(bf16[352,128]{1,0:T(8,128)(2,1)S(1)} %get-tuple-element.32), channel_id=1, source_target_pairs={{0,4},{4,0},{8,12},{12,8},{1,5},{5,1},{9,13},{13,9},{2,6},{6,2},{1... | collective-permute-start | bytes 270344 | tf_op jit(solution)/shard_map/ppermute | solution.py:190
  30.2 5.7 %collective-permute-done.15.got = bf16[4,320,128]{2,1,0:T(8,128)(2,1)S(1)} collective-permute-done((bf16[4,320,128]{2,1,0:T(8,128)(2,1)S(1)}, bf16[4,320,128]{2,1,0:T(8,128)(2,1)S(1)}, u32[]{:S(2)}, u32[]{:S(2)}) %collective-permute-start.15) | collective-permute-done | bytes 327712 | tf_op jit(solution)/shard_map/ppermute | solution.py:183
  35.9 2.2 %collective-permute-start.10 = (bf16[352,128]{1,0:T(8,128)(2,1)S(1)}, bf16[352,128]{1,0:T(8,128)(2,1)S(1)}, u32[]{:S(2)}, u32[]{:S(2)}) collective-permute-start(bf16[352,128]{1,0:T(8,128)(2,1)S(1)} %get-tuple-element.33), channel_id=1, source_target_pairs={{0,8},{4,12},{8,0},{12,4},{1,9},{5,13},{9,1},{13,5},{2,10},{6,14},... | collective-permute-start | bytes 270344 | tf_op jit(solution)/shard_map/ppermute | solution.py:190
  38.1 0.0 collective-permute-done.9.refs_0_
  38.1 1.1 %collective-permute-start.11 = (bf16[352,128]{1,0:T(8,128)(2,1)S(1)}, bf16[352,128]{1,0:T(8,128)(2,1)S(1)}, u32[]{:S(2)}, u32[]{:S(2)}) collective-permute-start(bf16[352,128]{1,0:T(8,128)(2,1)S(1)} %get-tuple-element.34), channel_id=1, source_target_pairs={{0,12},{4,8},{8,4},{12,0},{1,13},{5,9},{9,5},{13,1},{2,14},{6,10},... | collective-permute-start | bytes 270344 | tf_op jit(solution)/shard_map/ppermute | solution.py:190
  39.2 0.1 shard_map.54
  39.3 0.0 copy-start.1
  39.3 0.0 copy-start.2
  39.3 0.0 collective-permute-done.2.refs_0_
  39.3 0.3 collective-permute-start.16
  39.6 0.0 collective-permute-done.3.refs_1_
  39.6 2.2 %collective-permute-start.17 = (bf16[320,128]{1,0:T(8,128)(2,1)S(1)}, bf16[320,128]{1,0:T(8,128)(2,1)S(1)}, u32[]{:S(2)}, u32[]{:S(2)}) collective-permute-start(bf16[320,128]{1,0:T(8,128)(2,1)S(1)} %get-tuple-element.39), channel_id=1, source_target_pairs={{0,8},{4,12},{8,0},{12,4},{1,9},{5,13},{9,1},{13,5},{2,10},{6,14},... | collective-permute-start | bytes 245768 | tf_op jit(solution)/shard_map/ppermute | solution.py:190
  41.8 0.0 collective-permute-done.4.refs_2_
  41.8 1.1 %collective-permute-start.18 = (bf16[320,128]{1,0:T(8,128)(2,1)S(1)}, bf16[320,128]{1,0:T(8,128)(2,1)S(1)}, u32[]{:S(2)}, u32[]{:S(2)}) collective-permute-start(bf16[320,128]{1,0:T(8,128)(2,1)S(1)} %get-tuple-element.40), channel_id=1, source_target_pairs={{0,12},{4,8},{8,4},{12,0},{1,13},{5,9},{9,5},{13,1},{2,14},{6,10},... | collective-permute-start | bytes 245768 | tf_op jit(solution)/shard_map/ppermute | solution.py:190
  42.9 0.1 shard_map.49.refs_0_
  43.0 0.0 collective-permute-done.10.refs_1_
  43.0 1.3 %collective-permute-start.6 = (bf16[480,128]{1,0:T(8,128)(2,1)S(1)}, bf16[480,128]{1,0:T(8,128)(2,1)S(1)}, u32[]{:S(2)}, u32[]{:S(2)}) collective-permute-start(bf16[480,128]{1,0:T(8,128)(2,1)S(1)} %shard_map.49.refs_0_), channel_id=1, source_target_pairs={{0,2},{1,3},{2,0},{3,1},{4,6},{5,7},{6,4},{7,5},{8,10},{9,11},{10,... | collective-permute-start | bytes 368648 | tf_op jit(solution)/shard_map/ppermute | solution.py:197
  44.3 0.0 collective-permute-done.11.refs_2_
  44.3 0.8 %collective-permute-start.13 = (bf16[352,128]{1,0:T(8,128)(2,1)S(1)}, bf16[352,128]{1,0:T(8,128)(2,1)S(1)}, u32[]{:S(2)}, u32[]{:S(2)}) collective-permute-start(bf16[352,128]{1,0:T(8,128)(2,1)S(1)} %shard_map.52.refs_4_), channel_id=1, source_target_pairs={{0,2},{1,3},{2,0},{3,1},{4,6},{5,7},{6,4},{7,5},{8,10},{9,11},{10,... | collective-permute-start | bytes 270344 | tf_op jit(solution)/shard_map/ppermute | solution.py:197
  45.2 0.0 collective-permute-done.16.refs_0_
  45.2 6.8 %collective-permute-done.17.refs_1_ = bf16[320,128]{1,0:T(8,128)(2,1)S(1)} collective-permute-done((bf16[320,128]{1,0:T(8,128)(2,1)S(1)}, bf16[320,128]{1,0:T(8,128)(2,1)S(1)}, u32[]{:S(2)}, u32[]{:S(2)}) %collective-permute-start.17) | collective-permute-done | bytes 81952 | tf_op jit(solution)/shard_map/ppermute | solution.py:190
  51.9 0.0 collective-permute-done.18.refs_2_
  52.0 1.6 %collective-permute-start.19 = (bf16[320,128]{1,0:T(8,128)(2,1)S(1)}, bf16[320,128]{1,0:T(8,128)(2,1)S(1)}, u32[]{:S(2)}, u32[]{:S(2)}) collective-permute-start(bf16[320,128]{1,0:T(8,128)(2,1)S(1)} %shard_map.55.refs_8_), channel_id=1, source_target_pairs={{0,1},{1,0},{2,3},{3,2},{4,5},{5,4},{6,7},{7,6},{8,9},{9,8},{10,11... | collective-permute-start | bytes 245768 | tf_op jit(solution)/shard_map/ppermute | solution.py:196
  53.5 1.2 %collective-permute-start.20 = (bf16[320,128]{1,0:T(8,128)(2,1)S(1)}, bf16[320,128]{1,0:T(8,128)(2,1)S(1)}, u32[]{:S(2)}, u32[]{:S(2)}) collective-permute-start(bf16[320,128]{1,0:T(8,128)(2,1)S(1)} %shard_map.55.refs_8_), channel_id=1, source_target_pairs={{0,2},{1,3},{2,0},{3,1},{4,6},{5,7},{6,4},{7,5},{8,10},{9,11},{10,... | collective-permute-start | bytes 245768 | tf_op jit(solution)/shard_map/ppermute | solution.py:197
  54.8 0.3 collective-permute-start.5
  55.1 0.0 collective-permute-done.6.refs_2_
  55.1 0.2 collective-permute-start.7
  55.3 0.0 collective-permute-done.19.refs_9_
  55.3 0.3 collective-permute-start.12
  55.6 0.0 collective-permute-done.13.refs_6_
  55.6 0.2 collective-permute-start.14
  55.8 1.8 %collective-permute-done.20.refs_10_ = bf16[320,128]{1,0:T(8,128)(2,1)S(1)} collective-permute-done((bf16[320,128]{1,0:T(8,128)(2,1)S(1)}, bf16[320,128]{1,0:T(8,128)(2,1)S(1)}, u32[]{:S(2)}, u32[]{:S(2)}) %collective-permute-start.20) | collective-permute-done | bytes 81952 | tf_op jit(solution)/shard_map/ppermute | solution.py:197
  57.6 0.8 %collective-permute-start.21 = (bf16[320,128]{1,0:T(8,128)(2,1)S(1)}, bf16[320,128]{1,0:T(8,128)(2,1)S(1)}, u32[]{:S(2)}, u32[]{:S(2)}) collective-permute-start(bf16[320,128]{1,0:T(8,128)(2,1)S(1)} %collective-permute-done.20.refs_10_), channel_id=1, source_target_pairs={{0,1},{1,0},{2,3},{3,2},{4,5},{5,4},{6,7},{7,6},{8,9},{9,8},{10,11... | collective-permute-start | bytes 245768 | tf_op jit(solution)/shard_map/ppermute | solution.py:198
  58.4 0.0 collective-permute-done.12.refs_5_
  58.4 0.9 %collective-permute-done.21.refs_11_ = bf16[320,128]{1,0:T(8,128)(2,1)S(1)} collective-permute-done((bf16[320,128]{1,0:T(8,128)(2,1)S(1)}, bf16[320,128]{1,0:T(8,128)(2,1)S(1)}, u32[]{:S(2)}, u32[]{:S(2)}) %collective-permute-start.21) | collective-permute-done | bytes 81952 | tf_op jit(solution)/shard_map/ppermute | solution.py:198
  59.3 0.0 collective-permute-done.14.refs_7_
  59.3 0.0 collective-permute-done.5.refs_1_
  59.3 0.0 collective-permute-done.7.refs_3_
  59.4 0.0 copy-done.1
  59.4 0.0 copy-done.2
  59.4 3.9 %shard_map.56 = f32[128,1024]{1,0:T(8,128)} custom-call(s32[3]{0:T(128)S(1)} %pad_add_fusion.where, f32[128,1024]{1,0:T(8,128)S(1)} %bitcast.7, s32[128,1024]{1,0:T(8,128)S(1)} %bitcast.8, bf16[480,128]{1,0:T(8,128)(2,1)S(1)} %shard_map.49.refs_0_, bf16[480,128]{1,0:T(8,128)(2,1)S(1)} %collective-permute-done.5.refs_1_, ...), custom_call_target="tpu_custom_call" | custom-call | tf_op jit(solution)/shard_map/pallas_call | solution.py:200
  (2 shorter events, 0.1 us)
Async XLA Ops:
  0.1 1.2 %copy-start = (bf16[512,1024]{1,0:T(8,128)(2,1)S(1)}, bf16[512,1024]{1,0:T(8,128)(2,1)}, u32[]{:S(2)}) copy-start(bf16[512,1024]{1,0:T(8,128)(2,1)} %tokens.1) | copy-start | bytes 3145732
  1.3 0.7 %copy-start.3 = (s32[512,2]{0,1:T(2,128)S(1)}, s32[512,2]{0,1:T(2,128)}, u32[]{:S(2)}) copy-start(s32[512,2]{0,1:T(2,128)} %param.5) | copy-start | bytes 12292
  2.9 2.7 %collective-permute-start = (bf16[1040,512]{1,0:T(8,128)(2,1)S(1)}, bf16[1040,512]{1,0:T(8,128)(2,1)S(1)}, u32[]{:S(2)}, u32[]{:S(2)}) collective-permute-start(bf16[1040,512]{1,0:T(8,128)(2,1)S(1)} %shard_map.46.mine), channel_id=1, source_target_pairs={{0,1},{1,0},{2,3},{3,2},{4,5},{5,4},{6,7},{7,6},{8,9},{9,8},{10,11... | collective-permute-start | bytes 3194888 | tf_op jit(solution)/shard_map/ppermute | solution.py:171
  7.4 13.7 %collective-permute-start.1 = (bf16[4,480,128]{2,1,0:T(8,128)(2,1)S(1)}, bf16[4,480,128]{2,1,0:T(8,128)(2,1)S(1)}, u32[]{:S(2)}, u32[]{:S(2)}) collective-permute-start(bf16[4,480,128]{2,1,0:T(8,128)(2,1)S(1)} %get-tuple-element.24), channel_id=1, source_target_pairs={{0,2},{1,3},{2,0},{3,1},{4,6},{5,7},{6,4},{7,5},{8,10},{9,11},{10,... | collective-permute-start | bytes 1474568 | tf_op jit(solution)/shard_map/ppermute | solution.py:183
  11.4 17.5 %collective-permute-start.8 = (bf16[4,352,128]{2,1,0:T(8,128)(2,1)S(1)}, bf16[4,352,128]{2,1,0:T(8,128)(2,1)S(1)}, u32[]{:S(2)}, u32[]{:S(2)}) collective-permute-start(bf16[4,352,128]{2,1,0:T(8,128)(2,1)S(1)} %get-tuple-element.30), channel_id=1, source_target_pairs={{0,2},{1,3},{2,0},{3,1},{4,6},{5,7},{6,4},{7,5},{8,10},{9,11},{10,... | collective-permute-start | bytes 1081352 | tf_op jit(solution)/shard_map/ppermute | solution.py:183
  13.1 22.8 %collective-permute-start.15 = (bf16[4,320,128]{2,1,0:T(8,128)(2,1)S(1)}, bf16[4,320,128]{2,1,0:T(8,128)(2,1)S(1)}, u32[]{:S(2)}, u32[]{:S(2)}) collective-permute-start(bf16[4,320,128]{2,1,0:T(8,128)(2,1)S(1)} %get-tuple-element.36), channel_id=1, source_target_pairs={{0,2},{1,3},{2,0},{3,1},{4,6},{5,7},{6,4},{7,5},{8,10},{9,11},{10,... | collective-permute-start | bytes 983048 | tf_op jit(solution)/shard_map/ppermute | solution.py:183
  21.2 18.1 %collective-permute-start.2 = (bf16[480,128]{1,0:T(8,128)(2,1)S(1)}, bf16[480,128]{1,0:T(8,128)(2,1)S(1)}, u32[]{:S(2)}, u32[]{:S(2)}) collective-permute-start(bf16[480,128]{1,0:T(8,128)(2,1)S(1)} %get-tuple-element.26), channel_id=1, source_target_pairs={{0,4},{4,0},{8,12},{12,8},{1,5},{5,1},{9,13},{13,9},{2,6},{6,2},{1... | collective-permute-start | bytes 368648 | tf_op jit(solution)/shard_map/ppermute | solution.py:190
  22.5 17.1 %collective-permute-start.3 = (bf16[480,128]{1,0:T(8,128)(2,1)S(1)}, bf16[480,128]{1,0:T(8,128)(2,1)S(1)}, u32[]{:S(2)}, u32[]{:S(2)}) collective-permute-start(bf16[480,128]{1,0:T(8,128)(2,1)S(1)} %get-tuple-element.27), channel_id=1, source_target_pairs={{0,8},{4,12},{8,0},{12,4},{1,9},{5,13},{9,1},{13,5},{2,10},{6,14},... | collective-permute-start | bytes 368648 | tf_op jit(solution)/shard_map/ppermute | solution.py:190
  24.8 17.0 %collective-permute-start.4 = (bf16[480,128]{1,0:T(8,128)(2,1)S(1)}, bf16[480,128]{1,0:T(8,128)(2,1)S(1)}, u32[]{:S(2)}, u32[]{:S(2)}) collective-permute-start(bf16[480,128]{1,0:T(8,128)(2,1)S(1)} %get-tuple-element.28), channel_id=1, source_target_pairs={{0,12},{4,8},{8,4},{12,0},{1,13},{5,9},{9,5},{13,1},{2,14},{6,10},... | collective-permute-start | bytes 368648 | tf_op jit(solution)/shard_map/ppermute | solution.py:190
  28.9 9.2 %collective-permute-start.9 = (bf16[352,128]{1,0:T(8,128)(2,1)S(1)}, bf16[352,128]{1,0:T(8,128)(2,1)S(1)}, u32[]{:S(2)}, u32[]{:S(2)}) collective-permute-start(bf16[352,128]{1,0:T(8,128)(2,1)S(1)} %get-tuple-element.32), channel_id=1, source_target_pairs={{0,4},{4,0},{8,12},{12,8},{1,5},{5,1},{9,13},{13,9},{2,6},{6,2},{1... | collective-permute-start | bytes 270344 | tf_op jit(solution)/shard_map/ppermute | solution.py:190
  35.9 7.1 %collective-permute-start.10 = (bf16[352,128]{1,0:T(8,128)(2,1)S(1)}, bf16[352,128]{1,0:T(8,128)(2,1)S(1)}, u32[]{:S(2)}, u32[]{:S(2)}) collective-permute-start(bf16[352,128]{1,0:T(8,128)(2,1)S(1)} %get-tuple-element.33), channel_id=1, source_target_pairs={{0,8},{4,12},{8,0},{12,4},{1,9},{5,13},{9,1},{13,5},{2,10},{6,14},... | collective-permute-start | bytes 270344 | tf_op jit(solution)/shard_map/ppermute | solution.py:190
  38.1 6.1 %collective-permute-start.11 = (bf16[352,128]{1,0:T(8,128)(2,1)S(1)}, bf16[352,128]{1,0:T(8,128)(2,1)S(1)}, u32[]{:S(2)}, u32[]{:S(2)}) collective-permute-start(bf16[352,128]{1,0:T(8,128)(2,1)S(1)} %get-tuple-element.34), channel_id=1, source_target_pairs={{0,12},{4,8},{8,4},{12,0},{1,13},{5,9},{9,5},{13,1},{2,14},{6,10},... | collective-permute-start | bytes 270344 | tf_op jit(solution)/shard_map/ppermute | solution.py:190
  39.3 20.1 %copy-start.1 = (f32[1,128,1024]{2,1,0:T(8,128)S(1)}, f32[1,128,1024]{2,1,0:T(8,128)}, u32[]{:S(2)}) copy-start(f32[1,128,1024]{2,1,0:T(8,128)} %param.6) | copy-start | bytes 1572868
  39.3 20.1 %copy-start.2 = (s32[1,128,1024]{2,1,0:T(8,128)S(1)}, s32[1,128,1024]{2,1,0:T(8,128)}, u32[]{:S(2)}) copy-start(s32[1,128,1024]{2,1,0:T(8,128)} %param.7) | copy-start | bytes 1572868
  39.3 5.9 %collective-permute-start.16 = (bf16[320,128]{1,0:T(8,128)(2,1)S(1)}, bf16[320,128]{1,0:T(8,128)(2,1)S(1)}, u32[]{:S(2)}, u32[]{:S(2)}) collective-permute-start(bf16[320,128]{1,0:T(8,128)(2,1)S(1)} %get-tuple-element.38), channel_id=1, source_target_pairs={{0,4},{4,0},{8,12},{12,8},{1,5},{5,1},{9,13},{13,9},{2,6},{6,2},{1... | collective-permute-start | bytes 245768 | tf_op jit(solution)/shard_map/ppermute | solution.py:190
  39.6 12.3 %collective-permute-start.17 = (bf16[320,128]{1,0:T(8,128)(2,1)S(1)}, bf16[320,128]{1,0:T(8,128)(2,1)S(1)}, u32[]{:S(2)}, u32[]{:S(2)}) collective-permute-start(bf16[320,128]{1,0:T(8,128)(2,1)S(1)} %get-tuple-element.39), channel_id=1, source_target_pairs={{0,8},{4,12},{8,0},{12,4},{1,9},{5,13},{9,1},{13,5},{2,10},{6,14},... | collective-permute-start | bytes 245768 | tf_op jit(solution)/shard_map/ppermute | solution.py:190
  41.8 10.1 %collective-permute-start.18 = (bf16[320,128]{1,0:T(8,128)(2,1)S(1)}, bf16[320,128]{1,0:T(8,128)(2,1)S(1)}, u32[]{:S(2)}, u32[]{:S(2)}) collective-permute-start(bf16[320,128]{1,0:T(8,128)(2,1)S(1)} %get-tuple-element.40), channel_id=1, source_target_pairs={{0,12},{4,8},{8,4},{12,0},{1,13},{5,9},{9,5},{13,1},{2,14},{6,10},... | collective-permute-start | bytes 245768 | tf_op jit(solution)/shard_map/ppermute | solution.py:190
  43.0 12.1 %collective-permute-start.6 = (bf16[480,128]{1,0:T(8,128)(2,1)S(1)}, bf16[480,128]{1,0:T(8,128)(2,1)S(1)}, u32[]{:S(2)}, u32[]{:S(2)}) collective-permute-start(bf16[480,128]{1,0:T(8,128)(2,1)S(1)} %shard_map.49.refs_0_), channel_id=1, source_target_pairs={{0,2},{1,3},{2,0},{3,1},{4,6},{5,7},{6,4},{7,5},{8,10},{9,11},{10,... | collective-permute-start | bytes 368648 | tf_op jit(solution)/shard_map/ppermute | solution.py:197
  44.3 11.3 %collective-permute-start.13 = (bf16[352,128]{1,0:T(8,128)(2,1)S(1)}, bf16[352,128]{1,0:T(8,128)(2,1)S(1)}, u32[]{:S(2)}, u32[]{:S(2)}) collective-permute-start(bf16[352,128]{1,0:T(8,128)(2,1)S(1)} %shard_map.52.refs_4_), channel_id=1, source_target_pairs={{0,2},{1,3},{2,0},{3,1},{4,6},{5,7},{6,4},{7,5},{8,10},{9,11},{10,... | collective-permute-start | bytes 270344 | tf_op jit(solution)/shard_map/ppermute | solution.py:197
  52.0 3.3 %collective-permute-start.19 = (bf16[320,128]{1,0:T(8,128)(2,1)S(1)}, bf16[320,128]{1,0:T(8,128)(2,1)S(1)}, u32[]{:S(2)}, u32[]{:S(2)}) collective-permute-start(bf16[320,128]{1,0:T(8,128)(2,1)S(1)} %shard_map.55.refs_8_), channel_id=1, source_target_pairs={{0,1},{1,0},{2,3},{3,2},{4,5},{5,4},{6,7},{7,6},{8,9},{9,8},{10,11... | collective-permute-start | bytes 245768 | tf_op jit(solution)/shard_map/ppermute | solution.py:196
  53.5 4.0 %collective-permute-start.20 = (bf16[320,128]{1,0:T(8,128)(2,1)S(1)}, bf16[320,128]{1,0:T(8,128)(2,1)S(1)}, u32[]{:S(2)}, u32[]{:S(2)}) collective-permute-start(bf16[320,128]{1,0:T(8,128)(2,1)S(1)} %shard_map.55.refs_8_), channel_id=1, source_target_pairs={{0,2},{1,3},{2,0},{3,1},{4,6},{5,7},{6,4},{7,5},{8,10},{9,11},{10,... | collective-permute-start | bytes 245768 | tf_op jit(solution)/shard_map/ppermute | solution.py:197
  54.8 4.6 %collective-permute-start.5 = (bf16[480,128]{1,0:T(8,128)(2,1)S(1)}, bf16[480,128]{1,0:T(8,128)(2,1)S(1)}, u32[]{:S(2)}, u32[]{:S(2)}) collective-permute-start(bf16[480,128]{1,0:T(8,128)(2,1)S(1)} %shard_map.49.refs_0_), channel_id=1, source_target_pairs={{0,1},{1,0},{2,3},{3,2},{4,5},{5,4},{6,7},{7,6},{8,9},{9,8},{10,11... | collective-permute-start | bytes 368648 | tf_op jit(solution)/shard_map/ppermute | solution.py:196
  55.1 4.2 %collective-permute-start.7 = (bf16[480,128]{1,0:T(8,128)(2,1)S(1)}, bf16[480,128]{1,0:T(8,128)(2,1)S(1)}, u32[]{:S(2)}, u32[]{:S(2)}) collective-permute-start(bf16[480,128]{1,0:T(8,128)(2,1)S(1)} %collective-permute-done.6.refs_2_), channel_id=1, source_target_pairs={{0,1},{1,0},{2,3},{3,2},{4,5},{5,4},{6,7},{7,6},{8,9},{9,8},{10,11... | collective-permute-start | bytes 368648 | tf_op jit(solution)/shard_map/ppermute | solution.py:198
  55.3 3.1 %collective-permute-start.12 = (bf16[352,128]{1,0:T(8,128)(2,1)S(1)}, bf16[352,128]{1,0:T(8,128)(2,1)S(1)}, u32[]{:S(2)}, u32[]{:S(2)}) collective-permute-start(bf16[352,128]{1,0:T(8,128)(2,1)S(1)} %shard_map.52.refs_4_), channel_id=1, source_target_pairs={{0,1},{1,0},{2,3},{3,2},{4,5},{5,4},{6,7},{7,6},{8,9},{9,8},{10,11... | collective-permute-start | bytes 270344 | tf_op jit(solution)/shard_map/ppermute | solution.py:196
  55.6 3.7 %collective-permute-start.14 = (bf16[352,128]{1,0:T(8,128)(2,1)S(1)}, bf16[352,128]{1,0:T(8,128)(2,1)S(1)}, u32[]{:S(2)}, u32[]{:S(2)}) collective-permute-start(bf16[352,128]{1,0:T(8,128)(2,1)S(1)} %collective-permute-done.13.refs_6_), channel_id=1, source_target_pairs={{0,1},{1,0},{2,3},{3,2},{4,5},{5,4},{6,7},{7,6},{8,9},{9,8},{10,11... | collective-permute-start | bytes 270344 | tf_op jit(solution)/shard_map/ppermute | solution.py:198
  57.6 1.8 %collective-permute-start.21 = (bf16[320,128]{1,0:T(8,128)(2,1)S(1)}, bf16[320,128]{1,0:T(8,128)(2,1)S(1)}, u32[]{:S(2)}, u32[]{:S(2)}) collective-permute-start(bf16[320,128]{1,0:T(8,128)(2,1)S(1)} %collective-permute-done.20.refs_10_), channel_id=1, source_target_pairs={{0,1},{1,0},{2,3},{3,2},{4,5},{5,4},{6,7},{7,6},{8,9},{9,8},{10,11... | collective-permute-start | bytes 245768 | tf_op jit(solution)/shard_map/ppermute | solution.py:198

commit v2 on v0

--- a/solution.py
+++ b/solution.py
@@ -1,19 +1,28 @@
+import functools
+
 import jax
 import jax.numpy as jnp
 from jax import lax
+from jax.experimental import pallas as pl
+from jax.experimental.pallas import tpu as pltpu
 from jax.sharding import PartitionSpec as P
 
 STEPS = 3
 
 
 step_scale = 1.5
+
+BLK = 128
+PIECE = 32
+VMEM = pl.BlockSpec(memory_space=pltpu.VMEM)
+SMEM = pl.BlockSpec(memory_space=pltpu.SMEM)
 
 
 def full_product(rows):
     return lax.dot_general(rows, rows, (((0,), (0,)), ((), ())), preferred_element_type=jnp.float32)
 
 
-def local(tokens, routes, w_orig, mask):
+def local_rows(tokens, routes, w_orig, mask):
     experts_n = lax.axis_size("expert")
     tok_rows, topk_count = routes.shape
     width = tokens.shape[1]
@@ -47,6 +56,200 @@
     return weights[None]
 
 
+def count(panels):
+    return sum(4 * j + 3 for j in panels)
+
+
+def blocks_of(panels):
+    return [(k, c) for j in panels for c in (2 * j, 2 * j + 1) for k in range(c + 1)]
+
+
+def lift_kernel(experts, where, tokens, routes_t, out, turned):
+    toks, width = tokens.shape
+    turned[...] = tokens[...].T
+    numbers = lax.broadcasted_iota(jnp.int32, (16, toks), 0) ^ where[0]
+    named = numbers == routes_t[0:1, :]
+    for k in range(1, routes_t.shape[0]):
+        named = named | (numbers == routes_t[k : k + 1, :])
+    flags = named.astype(jnp.float32).astype(jnp.bfloat16)
+    row = 64 * where[2]
+    ats = (row + PIECE * where[1], row + PIECE * (1 - where[1]))
+    first = 0
+    for k in range(width // BLK):
+        for at in ats:
+            rows = turned[pl.ds(pl.multiple_of(at + BLK * k, PIECE), PIECE), :]
+            for e in range(experts):
+                out[first : first + PIECE, :] = rows * flags[e : e + 1, :]
+                first += PIECE
+
+
+def gram_kernel(panels, mode, experts, where, lhs_a, tok_a, lhs_b, tok_b, keep, send):
+    group = 2 * experts * PIECE
+    halves = (PIECE * where[1], PIECE * (1 - where[1]))
+    base = 0
+    for j in panels:
+        used, cols = slice(0, group * (2 * j + 2)), slice(256 * j, 256 * j + 256)
+        total = jnp.dot(lhs_a[used, :], tok_a[:, cols], preferred_element_type=jnp.float32)
+        total = total + jnp.dot(lhs_b[used, :], tok_b[:, cols], preferred_element_type=jnp.float32)
+        for side in range(2):
+            for k in range(2 * j + side + 1):
+                for s in range(2):
+                    for e in range(experts):
+                        first = group * k + experts * PIECE * s + PIECE * e
+                        value = total[first : first + PIECE, BLK * side : BLK * (side + 1)]
+                        if mode == "z":
+                            out = keep if e % 2 == 0 else send
+                            at = pl.multiple_of(halves[s] + base, PIECE)
+                            out[e // 2, pl.ds(at, PIECE), :] = value.astype(out.dtype)
+                        else:
+                            out = (keep, send)[s]
+                            out[e, base : base + PIECE, :] = value.astype(out.dtype)
+                base += 2 * PIECE if mode == "z" else PIECE
+
+
+def pair_kernel(keep, got, own, *outs):
+    for e, out in enumerate((own,) + outs):
+        out[...] = (keep[e] + got[e].astype(jnp.float32)).astype(out.dtype)
+
+
+def split_kernel(keep, got, own, out):
+    for e in range(4):
+        to = (own, out)[e % 2]
+        to[e // 2] = (keep[e] + got[e].astype(jnp.float32)).astype(to.dtype)
+
+
+def sum_kernel(*refs):
+    total = refs[0][...].astype(jnp.float32)
+    for ref in refs[1:-1]:
+        total = total + ref[...].astype(jnp.float32)
+    refs[-1][...] = total.astype(refs[-1].dtype)
+
+
+def put_pieces(chunk, gram, where):
+    panels, size, pieces = chunk
+    core, x = where[2], where[1]
+    if size == PIECE:
+        ats = [64 * a + PIECE * b for b in (x, 1 - x) for a in (core, 1 - core)]
+    else:
+        ats = [64 * a for a in (core, 1 - core)]
+    square = jnp.zeros((PIECE, BLK), jnp.float32)
+    for at, piece in zip(ats, pieces):
+        base = 0
+        for k, c in blocks_of(panels):
+            gram[pl.ds(pl.multiple_of(at + BLK * k, PIECE), size), BLK * c : BLK * (c + 1)] = piece[
+                base : base + size, :]
+            for part in range(0, size, PIECE):
+                value = piece[base + part : base + part + PIECE, :].astype(jnp.float32)
+                square = square + value * value * (1.0 if k == c else 2.0)
+            base += size
+    for k, c in blocks_of(panels):
+        if k < c:
+            gram[BLK * c : BLK * (c + 1), BLK * k : BLK * (k + 1)] = gram[
+                BLK * k : BLK * (k + 1), BLK * c : BLK * (c + 1)].T
+    return square
+
+
+def unflatten(shape, refs):
+    refs, out = list(refs), []
+    for panels, size, pieces in shape:
+        out.append((panels, size, refs[:pieces]))
+        refs = refs[pieces:]
+    return out
+
+
+def early_kernel(shape, where, *refs):
+    gram, square = refs[-2:]
+    square[...] = sum(put_pieces(chunk, gram, where) for chunk in unflatten(shape, refs[:-2]))
+
+
+def steps_kernel(shape, where, w_ref, mask_ref, old, square, *refs):
+    pieces, (out, gram) = refs[:-2], refs[-2:]
+    total = square[...] + sum(put_pieces(chunk, gram, where) for chunk in unflatten(shape, pieces))
+    rate = step_scale / jnp.sqrt(jnp.sum(total) + 1e-06)
+    dense = w_ref[...]
+    keep = mask_ref[...].astype(jnp.float32)
+    weights = keep * dense
+    rows = dense.shape[0]
+    for section in range(STEPS):
+        change = weights - dense
+        high = change.astype(jnp.bfloat16)
+        low = (change - high.astype(jnp.float32)).astype(jnp.bfloat16)
+        both = jnp.dot(jnp.concatenate([high, low], axis=0), gram[...], preferred_element_type=jnp.float32)
+        weights = keep * (weights - rate * (both[0:rows] + both[rows:]))
+    out[...] = weights
+
+
+def call(kernel, outs, *args, scratch=(), smem=True, aliases={}):
+    return pl.pallas_call(
+        kernel, in_specs=[SMEM if smem and i == 0 else VMEM for i in range(len(args))],
+        out_specs=[VMEM] * len(outs),
+        out_shape=[jax.ShapeDtypeStruct(s, d) for s, d in outs],
+        scratch_shapes=list(scratch), input_output_aliases=aliases,
+        compiler_params=pltpu.CompilerParams(vmem_limit_bytes=16 << 20),
+    )(*args)
+
+
+def over(axis, bit):
+    return lambda a: lax.ppermute(a, axis, [(i, i ^ bit) for i in range(4)])
+
+
+def local_grams(plan, tokens, routes, w_orig, mask):
+    toks, width = tokens.shape
+    experts = lax.axis_size("expert")
+    z, dp = lax.axis_index("expert"), lax.axis_index("dp")
+    where = jnp.stack([z, dp // 2, dp % 2]).astype(jnp.int32)
+    over_core, over_x = over("dp", 1), over("dp", 2)
+    bf16, f32 = jnp.bfloat16, jnp.float32
+
+    def lift(tok, routes_t):
+        return call(functools.partial(lift_kernel, experts), [((2 * width, toks), bf16)],
+                    where, tok, routes_t, scratch=[pltpu.VMEM((width, toks), bf16)])[0]
+
+    other, other_routes = over_core(tokens), over_core(routes.T)
+    lhs = lift(tokens, routes.T)
+    other_lhs = lift(other, other_routes)
+    shape, found = [], []
+    for panels, mode in plan:
+        blocks = count(panels)
+        first = mode == "z"
+        dims = (2, 2 * PIECE * blocks, BLK) if first else (experts, PIECE * blocks, BLK)
+        keep, send = call(functools.partial(gram_kernel, panels, mode, experts),
+                          [(dims, f32), (dims, bf16)], where, lhs, tokens, other_lhs, other)
+        size = 2 * PIECE if first else PIECE
+        flat = (size * blocks, BLK)
+        if not first:
+            got = over_x(send)
+        if mode == "direct":
+            own, *away = call(pair_kernel, [(flat, f32)] + [(flat, bf16)] * (experts - 1), keep, got, smem=False)
+            came = [over("expert", s + 1)(a) for s, a in enumerate(away)]
+            final = call(sum_kernel, [(flat, bf16)], own, *came, smem=False)[0]
+        else:
+            if not first:
+                keep, send = call(split_kernel, [((2,) + flat, f32), ((2,) + flat, bf16)], keep, got, smem=False)
+            near = over("expert", 1)(send)
+            own, away = call(pair_kernel, [(flat, f32), (flat, bf16)], keep, near, smem=False)
+            far = over("expert", 2)(away)
+            final = call(sum_kernel, [(flat, bf16)], own, far, smem=False)[0]
+        if first:
+            final = call(sum_kernel, [(flat, bf16)], final, over_x(final), smem=False)[0]
+            pieces = [final, over_core(final)]
+        else:
+            by_x = over_x(final)
+            pieces = [final, over_core(final), by_x, over_core(by_x)]
+        shape.append((panels, size, len(pieces)))
+        found.append(pieces)
+    gram, square = call(functools.partial(early_kernel, tuple(shape[:-1])),
+                        [((width, width), bf16), ((PIECE, BLK), f32)],
+                        where, *[p for pieces in found[:-1] for p in pieces])
+    out, _ = call(functools.partial(steps_kernel, tuple(shape[-1:])),
+                  [(w_orig.shape[1:], f32), ((width, width), bf16)],
+                  where, w_orig[0], mask[0], gram, square, *found[-1], aliases={3: 1})
+    return out[None]
+
+
+PLAN = (((2,), "z"), ((3,), "direct"), ((0, 1), "direct"))
+
+
 def solution(mesh):
     placed = (
         P(("groups", "expert", "dp"), None),
@@ -54,6 +257,8 @@
         P("expert", "dp", None),
         P("expert", "dp", None),
     )
+    few = mesh.shape["expert"] == 4 and mesh.shape["dp"] == 4
+    local = functools.partial(local_grams, PLAN) if few else local_rows
     return jax.shard_map(
         local,
         mesh=mesh,

time: 163 us -> 56.4 us (0.35)
  blocking collectives: 64 us -> 0 us
  waiting for transfers between devices: 51.9 us -> 11 us
  starting transfers between devices: 0.01 us -> 30.9 us
  local copies, waits for them, and re-layouts: 16.2 us -> 2.11 us
  between operations: 14.2 us -> 0.15 us
  Pallas kernels: 0 us -> 12 us
  matrix products: 9.75 us -> 0 us
  other arithmetic: 5.66 us -> 0.08 us
    all_to_all x1 -> x0, blocking collectives: 64 us -> none  [local(): lax.all_to_all(outgoing, 'expert', split_axis=0, concat_axis=0, tiled=True)]
    psum x1 -> x0, waiting for transfers between devices: 51.9 us -> none  [local(): lax.psum(local_terms.astype(jnp.bfloat16), 'dp').astype(jnp.float32)]
    ppermute x0 -> x20, starting transfers between devices: none -> 30.9 us  [over(): return lambda a: lax.ppermute(a, axis, [(i, i ^ bit) for i in range(4)])]
    scatter x1 -> x0, local copies, waits for them, and re-layouts: 14.5 us -> none  [local(): jnp.zeros((experts_n * capacity, width), jnp.bfloat16).at[target]]
    pallas_call x0 -> x14, Pallas kernels: none -> 12 us  [call(): pl.pallas_call(kernel, in_specs=[SMEM if smem and i == 0 else VMEM for i...]
    ppermute x0 -> x20, waiting for transfers between devices: none -> 11 us  [over(): return lambda a: lax.ppermute(a, axis, [(i, i ^ bit) for i in range(4)])]
    dot_general x4 -> x0, matrix products: 9.75 us -> none  [the longest x3 5.59 us: local(): jnp.dot(change, gram_matrix, precision=lax.Precision.HIGHEST, preferred_e...]
    reduce_sum x2 -> x0, other arithmetic: 3.45 us -> none  [the longest x1 3.42 us: local(): frobenius = jnp.sqrt(jnp.sum(gram_matrix * gram_matrix) + 1e-06)]
  transfers between devices with their start and end apart: 1 -> 20, of which waited for: 1 -> 5; matrix products, arithmetic and copies ran while one was open for 0% -> 0% of each run, Pallas kernels for 0% -> 11%
where the time goes in v2:
time: 56.4 us; the launch traced here: 56.2 us
  starting transfers between devices  30.9 us (55%)
  Pallas kernels  12 us (21%)
  waiting for transfers between devices  11 us (20%)
  local copies, waits for them, and re-layouts  2.11 us (4%)
    ppermute x20, starting transfers between devices, over(): return lambda a: lax.ppermute(a, axis, [(i, i ^ bit) for i in range(4)])  30.9 us
    pallas_call x14, Pallas kernels, call(): pl.pallas_call(kernel, in_specs=[SMEM if smem and i == 0 else VMEM for i...  12 us
    ppermute x20, waiting for transfers between devices, over(): return lambda a: lax.ppermute(a, axis, [(i, i ^ bit) for i in range(4)])  11 us
    unnamed x10, local copies, waits for them, and re-layouts  2.11 us
  transfers between devices with their start and end apart: 20, of which 5 were waited for; matrix products, arithmetic and copies ran while one was open for 0% of the time, Pallas kernels for 11%

profile of v2, /device:TPU:1, one launch (start us, length us, event | category | flops | bytes accessed | tf_op | source)
XLA Modules:
  0.0 56.2 jit_solution(884962603271711295)
XLA Ops:
  0.0 0.1 collective-permute-start
  0.1 0.5 collective-permute-start.1
  0.5 0.1 pad_add_fusion.where
  0.6 0.0 copy-start
  0.6 1.2 %copy-done = bf16[512,1024]{1,0:T(8,128)(2,1)S(1)} copy-done((bf16[512,1024]{1,0:T(8,128)(2,1)S(1)}, bf16[512,1024]{1,0:T(8,128)(2,1)}, u32[]{:S(2)}) %copy-start) | copy-done | bytes 1048600
  1.8 0.0 copy-start.4
  1.8 0.7 %copy-done.4 = s32[512,2]{0,1:T(2,128)S(1)} copy-done((s32[512,2]{0,1:T(2,128)S(1)}, s32[512,2]{0,1:T(2,128)}, u32[]{:S(2)}) %copy-start.4) | copy-done | bytes 4120
  2.5 1.0 %shard_map.46.lhs_a = bf16[2048,512]{1,0:T(8,128)(2,1)S(1)} custom-call(s32[3]{0:T(128)S(1)} %pad_add_fusion.where, bf16[512,1024]{1,0:T(8,128)(2,1)S(1)} %copy-done, s32[2,512]{1,0:T(2,128)S(1)} %bitcast.10), custom_call_target="tpu_custom_call" | custom-call | tf_op jit(solution)/shard_map/pallas_call | solution.py:183
  3.5 0.0 copy-start.1
  3.5 0.0 collective-permute-done.1.routes_t
  3.5 0.0 collective-permute-done.tokens.tok_b
  3.5 1.0 %shard_map.47.lhs_b = bf16[2048,512]{1,0:T(8,128)(2,1)S(1)} custom-call(s32[3]{0:T(128)S(1)} %pad_add_fusion.where, bf16[512,1024]{1,0:T(8,128)(2,1)S(1)} %collective-permute-done.tokens.tok_b, s32[2,512]{1,0:T(2,128)S(1)} %collective-permute-done.1.routes_t), custom_call_target="tpu_custom_call" | custom-call | tf_op jit(solution)/shard_map/pallas_call | solution.py:183
  4.5 0.2 copy-done.1
  4.7 1.5 %shard_map.48 = (f32[2,704,128]{2,1,0:T(8,128)S(1)}, bf16[2,704,128]{2,1,0:T(8,128)(2,1)S(1)}) custom-call(s32[3]{0:T(128)S(1)} %pad_add_fusion.where, bf16[2048,512]{1,0:T(8,128)(2,1)S(1)} %shard_map.46.lhs_a, bf16[512,1024]{1,0:T(8,128)(2,1)S(1)} %copy-done.1, bf16[2048,512]{1,0:T(8,128)(2,1)S(1)} %shard_map.47.lhs_b, ...), custom_call_target="tpu_custom_call" | custom-call | tf_op jit(solution)/shard_map/pallas_call | solution.py:183
  6.3 2.4 %collective-permute-start.2 = (bf16[2,704,128]{2,1,0:T(8,128)(2,1)S(1)}, bf16[2,704,128]{2,1,0:T(8,128)(2,1)S(1)}, u32[]{:S(2)}, u32[]{:S(2)}) collective-permute-start(bf16[2,704,128]{2,1,0:T(8,128)(2,1)S(1)} %get-tuple-element.25), channel_id=1, source_target_pairs={{0,4},{4,0},{8,12},{12,8},{1,5},{5,1},{9,13},{13,9},{2,6},{6,2},{1... | collective-permute-start | bytes 1081352 | tf_op jit(solution)/shard_map/ppermute | solution.py:193
  8.6 1.8 %shard_map.52 = (f32[4,480,128]{2,1,0:T(8,128)S(1)}, bf16[4,480,128]{2,1,0:T(8,128)(2,1)S(1)}) custom-call(s32[3]{0:T(128)S(1)} %pad_add_fusion.where, bf16[2048,512]{1,0:T(8,128)(2,1)S(1)} %shard_map.46.lhs_a, bf16[512,1024]{1,0:T(8,128)(2,1)S(1)} %copy-done.1, bf16[2048,512]{1,0:T(8,128)(2,1)S(1)} %shard_map.47.lhs_b, ...), custom_call_target="tpu_custom_call" | custom-call | tf_op jit(solution)/shard_map/pallas_call | solution.py:183
  10.5 1.3 %collective-permute-start.6 = (bf16[4,480,128]{2,1,0:T(8,128)(2,1)S(1)}, bf16[4,480,128]{2,1,0:T(8,128)(2,1)S(1)}, u32[]{:S(2)}, u32[]{:S(2)}) collective-permute-start(bf16[4,480,128]{2,1,0:T(8,128)(2,1)S(1)} %get-tuple-element.29), channel_id=1, source_target_pairs={{0,2},{1,3},{2,0},{3,1},{4,6},{5,7},{6,4},{7,5},{8,10},{9,11},{10,... | collective-permute-start | bytes 1474568 | tf_op jit(solution)/shard_map/ppermute | solution.py:193
  11.8 1.5 %shard_map.56 = (f32[4,320,128]{2,1,0:T(8,128)S(1)}, bf16[4,320,128]{2,1,0:T(8,128)(2,1)S(1)}) custom-call(s32[3]{0:T(128)S(1)} %pad_add_fusion.where, bf16[2048,512]{1,0:T(8,128)(2,1)S(1)} %shard_map.46.lhs_a, bf16[512,1024]{1,0:T(8,128)(2,1)S(1)} %copy-done.1, bf16[2048,512]{1,0:T(8,128)(2,1)S(1)} %shard_map.47.lhs_b, ...), custom_call_target="tpu_custom_call" | custom-call | tf_op jit(solution)/shard_map/pallas_call | solution.py:183
  13.3 0.3 collective-permute-start.13
  13.6 3.3 %collective-permute-done.2.got = bf16[2,704,128]{2,1,0:T(8,128)(2,1)S(1)} collective-permute-done((bf16[2,704,128]{2,1,0:T(8,128)(2,1)S(1)}, bf16[2,704,128]{2,1,0:T(8,128)(2,1)S(1)}, u32[]{:S(2)}, u32[]{:S(2)}) %collective-permute-start.2) | collective-permute-done | bytes 360480 | tf_op jit(solution)/shard_map/ppermute | solution.py:193
  17.0 0.1 shard_map.49
  17.1 2.2 %collective-permute-start.3 = (bf16[704,128]{1,0:T(8,128)(2,1)S(1)}, bf16[704,128]{1,0:T(8,128)(2,1)S(1)}, u32[]{:S(2)}, u32[]{:S(2)}) collective-permute-start(bf16[704,128]{1,0:T(8,128)(2,1)S(1)} %get-tuple-element.27), channel_id=1, source_target_pairs={{0,8},{4,12},{8,0},{12,4},{1,9},{5,13},{9,1},{13,5},{2,10},{6,14},... | collective-permute-start | bytes 540680 | tf_op jit(solution)/shard_map/ppermute | solution.py:193
  19.3 3.2 %collective-permute-done.6.got = bf16[4,480,128]{2,1,0:T(8,128)(2,1)S(1)} collective-permute-done((bf16[4,480,128]{2,1,0:T(8,128)(2,1)S(1)}, bf16[4,480,128]{2,1,0:T(8,128)(2,1)S(1)}, u32[]{:S(2)}, u32[]{:S(2)}) %collective-permute-start.6) | collective-permute-done | bytes 491552 | tf_op jit(solution)/shard_map/ppermute | solution.py:193
  22.5 0.1 shard_map.53
  22.6 0.4 collective-permute-start.7
  23.1 2.1 %collective-permute-start.8 = (bf16[480,128]{1,0:T(8,128)(2,1)S(1)}, bf16[480,128]{1,0:T(8,128)(2,1)S(1)}, u32[]{:S(2)}, u32[]{:S(2)}) collective-permute-start(bf16[480,128]{1,0:T(8,128)(2,1)S(1)} %get-tuple-element.32), channel_id=1, source_target_pairs={{0,8},{4,12},{8,0},{12,4},{1,9},{5,13},{9,1},{13,5},{2,10},{6,14},... | collective-permute-start | bytes 368648 | tf_op jit(solution)/shard_map/ppermute | solution.py:193
  25.2 1.1 %collective-permute-start.9 = (bf16[480,128]{1,0:T(8,128)(2,1)S(1)}, bf16[480,128]{1,0:T(8,128)(2,1)S(1)}, u32[]{:S(2)}, u32[]{:S(2)}) collective-permute-start(bf16[480,128]{1,0:T(8,128)(2,1)S(1)} %get-tuple-element.33), channel_id=1, source_target_pairs={{0,12},{4,8},{8,4},{12,0},{1,13},{5,9},{9,5},{13,1},{2,14},{6,10},... | collective-permute-start | bytes 368648 | tf_op jit(solution)/shard_map/ppermute | solution.py:193
  26.3 1.2 %collective-permute-done.3.refs_1_ = bf16[704,128]{1,0:T(8,128)(2,1)S(1)} collective-permute-done((bf16[704,128]{1,0:T(8,128)(2,1)S(1)}, bf16[704,128]{1,0:T(8,128)(2,1)S(1)}, u32[]{:S(2)}, u32[]{:S(2)}) %collective-permute-start.3) | collective-permute-done | bytes 180256 | tf_op jit(solution)/shard_map/ppermute | solution.py:193
  27.5 0.0 copy-start.2
  27.5 0.0 copy-start.3
  27.5 1.0 %collective-permute-start.4 = (bf16[704,128]{1,0:T(8,128)(2,1)S(1)}, bf16[704,128]{1,0:T(8,128)(2,1)S(1)}, u32[]{:S(2)}, u32[]{:S(2)}) collective-permute-start(bf16[704,128]{1,0:T(8,128)(2,1)S(1)} %shard_map.50.refs_0_), channel_id=1, source_target_pairs={{0,2},{1,3},{2,0},{3,1},{4,6},{5,7},{6,4},{7,5},{8,10},{9,11},{10,... | collective-permute-start | bytes 540680 | tf_op jit(solution)/shard_map/ppermute | solution.py:193
  28.5 1.0 %collective-permute-done.13.got = bf16[4,320,128]{2,1,0:T(8,128)(2,1)S(1)} collective-permute-done((bf16[4,320,128]{2,1,0:T(8,128)(2,1)S(1)}, bf16[4,320,128]{2,1,0:T(8,128)(2,1)S(1)}, u32[]{:S(2)}, u32[]{:S(2)}) %collective-permute-start.13) | collective-permute-done | bytes 327712 | tf_op jit(solution)/shard_map/ppermute | solution.py:193
  29.6 0.1 shard_map.57
  29.6 5.7 %collective-permute-start.14 = (bf16[320,128]{1,0:T(8,128)(2,1)S(1)}, bf16[320,128]{1,0:T(8,128)(2,1)S(1)}, u32[]{:S(2)}, u32[]{:S(2)}) collective-permute-start(bf16[320,128]{1,0:T(8,128)(2,1)S(1)} %get-tuple-element.39), channel_id=1, source_target_pairs={{0,4},{4,0},{8,12},{12,8},{1,5},{5,1},{9,13},{13,9},{2,6},{6,2},{1... | collective-permute-start | bytes 245768 | tf_op jit(solution)/shard_map/ppermute | solution.py:193
  35.3 0.0 collective-permute-done.7.refs_1_
  35.3 3.2 %collective-permute-start.15 = (bf16[320,128]{1,0:T(8,128)(2,1)S(1)}, bf16[320,128]{1,0:T(8,128)(2,1)S(1)}, u32[]{:S(2)}, u32[]{:S(2)}) collective-permute-start(bf16[320,128]{1,0:T(8,128)(2,1)S(1)} %get-tuple-element.40), channel_id=1, source_target_pairs={{0,8},{4,12},{8,0},{12,4},{1,9},{5,13},{9,1},{13,5},{2,10},{6,14},... | collective-permute-start | bytes 245768 | tf_op jit(solution)/shard_map/ppermute | solution.py:193
  38.5 0.0 collective-permute-done.8.refs_2_
  38.5 0.0 collective-permute-done.9.refs_3_
  38.5 0.1 shard_map.54.refs_2_
  38.6 0.3 collective-permute-start.11
  38.9 1.8 %collective-permute-start.16 = (bf16[320,128]{1,0:T(8,128)(2,1)S(1)}, bf16[320,128]{1,0:T(8,128)(2,1)S(1)}, u32[]{:S(2)}, u32[]{:S(2)}) collective-permute-start(bf16[320,128]{1,0:T(8,128)(2,1)S(1)} %get-tuple-element.41), channel_id=1, source_target_pairs={{0,12},{4,8},{8,4},{12,0},{1,13},{5,9},{9,5},{13,1},{2,14},{6,10},... | collective-permute-start | bytes 245768 | tf_op jit(solution)/shard_map/ppermute | solution.py:193
  40.8 0.0 collective-permute-done.4.refs_1_
  40.8 1.2 %collective-permute-start.5 = (bf16[704,128]{1,0:T(8,128)(2,1)S(1)}, bf16[704,128]{1,0:T(8,128)(2,1)S(1)}, u32[]{:S(2)}, u32[]{:S(2)}) collective-permute-start(bf16[704,128]{1,0:T(8,128)(2,1)S(1)} %shard_map.51.refs_0_), channel_id=1, source_target_pairs={{0,1},{1,0},{2,3},{3,2},{4,5},{5,4},{6,7},{7,6},{8,9},{9,8},{10,11... | collective-permute-start | bytes 540680 | tf_op jit(solution)/shard_map/ppermute | solution.py:193
  42.0 0.0 collective-permute-done.14.refs_1_
  42.0 0.0 collective-permute-done.15.refs_2_
  42.0 2.0 %collective-permute-done.16.refs_3_ = bf16[320,128]{1,0:T(8,128)(2,1)S(1)} collective-permute-done((bf16[320,128]{1,0:T(8,128)(2,1)S(1)}, bf16[320,128]{1,0:T(8,128)(2,1)S(1)}, u32[]{:S(2)}, u32[]{:S(2)}) %collective-permute-start.16) | collective-permute-done | bytes 81952 | tf_op jit(solution)/shard_map/ppermute | solution.py:193
  44.1 1.3 %collective-permute-start.18 = (bf16[320,128]{1,0:T(8,128)(2,1)S(1)}, bf16[320,128]{1,0:T(8,128)(2,1)S(1)}, u32[]{:S(2)}, u32[]{:S(2)}) collective-permute-start(bf16[320,128]{1,0:T(8,128)(2,1)S(1)} %shard_map.58.refs_0_), channel_id=1, source_target_pairs={{0,2},{1,3},{2,0},{3,1},{4,6},{5,7},{6,4},{7,5},{8,10},{9,11},{10,... | collective-permute-start | bytes 245768 | tf_op jit(solution)/shard_map/ppermute | solution.py:193
  45.4 3.0 %collective-permute-start.10 = (bf16[480,128]{1,0:T(8,128)(2,1)S(1)}, bf16[480,128]{1,0:T(8,128)(2,1)S(1)}, u32[]{:S(2)}, u32[]{:S(2)}) collective-permute-start(bf16[480,128]{1,0:T(8,128)(2,1)S(1)} %shard_map.54.refs_2_), channel_id=1, source_target_pairs={{0,1},{1,0},{2,3},{3,2},{4,5},{5,4},{6,7},{7,6},{8,9},{9,8},{10,11... | collective-permute-start | bytes 368648 | tf_op jit(solution)/shard_map/ppermute | solution.py:193
  48.5 0.0 collective-permute-done.11.refs_4_
  48.5 0.0 collective-permute-start.12
  48.5 0.5 collective-permute-start.17
  49.0 0.0 collective-permute-done.18.refs_2_
  49.0 2.5 %collective-permute-start.19 = (bf16[320,128]{1,0:T(8,128)(2,1)S(1)}, bf16[320,128]{1,0:T(8,128)(2,1)S(1)}, u32[]{:S(2)}, u32[]{:S(2)}) collective-permute-start(bf16[320,128]{1,0:T(8,128)(2,1)S(1)} %collective-permute-done.18.refs_2_), channel_id=1, source_target_pairs={{0,1},{1,0},{2,3},{3,2},{4,5},{5,4},{6,7},{7,6},{8,9},{9,8},{10,11... | collective-permute-start | bytes 245768 | tf_op jit(solution)/shard_map/ppermute | solution.py:193
  51.5 0.0 collective-permute-done.10.refs_3_
  51.5 0.0 collective-permute-done.12.refs_5_
  51.5 0.0 collective-permute-done.5.refs_1_
  51.5 1.2 %shard_map.55 = (bf16[1024,1024]{1,0:T(8,128)(2,1)S(1)}, f32[32,128]{1,0:T(8,128)S(1)}) custom-call(s32[3]{0:T(128)S(1)} %pad_add_fusion.where, bf16[704,128]{1,0:T(8,128)(2,1)S(1)} %shard_map.51.refs_0_, bf16[704,128]{1,0:T(8,128)(2,1)S(1)} %collective-permute-done.5.refs_1_, bf16[480,128]{1,0:T(8,128)(2,1)S(1)} %shard_map.54.refs_2_, ...), custom_call_target="tpu_custom_call" | custom-call | tf_op jit(solution)/shard_map/pallas_call | solution.py:183
  52.8 0.0 collective-permute-done.17.refs_1_
  52.8 0.0 collective-permute-done.19.refs_3_
  52.8 0.0 copy-done.2
  52.8 0.0 copy-done.3
  52.8 3.4 %shard_map.59 = (f32[128,1024]{1,0:T(8,128)}, bf16[1024,1024]{1,0:T(8,128)(2,1)S(1)}) custom-call(s32[3]{0:T(128)S(1)} %pad_add_fusion.where, f32[128,1024]{1,0:T(8,128)S(1)} %bitcast.7, s32[128,1024]{1,0:T(8,128)S(1)} %bitcast.8, bf16[1024,1024]{1,0:T(8,128)(2,1)S(1)} %get-tuple-element.34.old, ...), custom_call_target="tpu_custom_call", output_to_operand_aliasing={{1}: (3, {})} | custom-call | tf_op jit(solution)/shard_map/pallas_call | solution.py:183
  (3 shorter events, 0.1 us)
Async XLA Ops:
  0.0 3.5 %collective-permute-start = (bf16[512,1024]{1,0:T(8,128)(2,1)}, bf16[512,1024]{1,0:T(8,128)(2,1)S(1)}, u32[]{:S(2)}, u32[]{:S(2)}) collective-permute-start(bf16[512,1024]{1,0:T(8,128)(2,1)} %tok_a.5), channel_id=1, source_target_pairs={{0,1},{1,0},{2,3},{3,2},{4,5},{5,4},{6,7},{7,6},{8,9},{9,8},{10,11... | collective-permute-start | bytes 3145736 | tf_op jit(solution)/shard_map/ppermute | solution.py:193
  0.1 3.5 %collective-permute-start.1 = (s32[2,512]{1,0:T(2,128)}, s32[2,512]{1,0:T(2,128)S(1)}, u32[]{:S(2)}, u32[]{:S(2)}) collective-permute-start(s32[2,512]{1,0:T(2,128)} %bitcast.9), channel_id=1, source_target_pairs={{0,1},{1,0},{2,3},{3,2},{4,5},{5,4},{6,7},{7,6},{8,9},{9,8},{10,11... | collective-permute-start | bytes 12296 | tf_op jit(solution)/shard_map/ppermute | solution.py:193
  0.6 1.2 %copy-start = (bf16[512,1024]{1,0:T(8,128)(2,1)S(1)}, bf16[512,1024]{1,0:T(8,128)(2,1)}, u32[]{:S(2)}) copy-start(bf16[512,1024]{1,0:T(8,128)(2,1)} %tok_a.5) | copy-start | bytes 3145732
  1.8 0.7 %copy-start.4 = (s32[512,2]{0,1:T(2,128)S(1)}, s32[512,2]{0,1:T(2,128)}, u32[]{:S(2)}) copy-start(s32[512,2]{0,1:T(2,128)} %param.5) | copy-start | bytes 12292
  3.5 1.2 %copy-start.1 = (bf16[512,1024]{1,0:T(8,128)(2,1)S(1)}, bf16[512,1024]{1,0:T(8,128)(2,1)}, u32[]{:S(2)}) copy-start(bf16[512,1024]{1,0:T(8,128)(2,1)} %tok_a.5) | copy-start | bytes 3145732
  6.3 10.7 %collective-permute-start.2 = (bf16[2,704,128]{2,1,0:T(8,128)(2,1)S(1)}, bf16[2,704,128]{2,1,0:T(8,128)(2,1)S(1)}, u32[]{:S(2)}, u32[]{:S(2)}) collective-permute-start(bf16[2,704,128]{2,1,0:T(8,128)(2,1)S(1)} %get-tuple-element.25), channel_id=1, source_target_pairs={{0,4},{4,0},{8,12},{12,8},{1,5},{5,1},{9,13},{13,9},{2,6},{6,2},{1... | collective-permute-start | bytes 1081352 | tf_op jit(solution)/shard_map/ppermute | solution.py:193
  10.5 12.0 %collective-permute-start.6 = (bf16[4,480,128]{2,1,0:T(8,128)(2,1)S(1)}, bf16[4,480,128]{2,1,0:T(8,128)(2,1)S(1)}, u32[]{:S(2)}, u32[]{:S(2)}) collective-permute-start(bf16[4,480,128]{2,1,0:T(8,128)(2,1)S(1)} %get-tuple-element.29), channel_id=1, source_target_pairs={{0,2},{1,3},{2,0},{3,1},{4,6},{5,7},{6,4},{7,5},{8,10},{9,11},{10,... | collective-permute-start | bytes 1474568 | tf_op jit(solution)/shard_map/ppermute | solution.py:193
  13.3 16.2 %collective-permute-start.13 = (bf16[4,320,128]{2,1,0:T(8,128)(2,1)S(1)}, bf16[4,320,128]{2,1,0:T(8,128)(2,1)S(1)}, u32[]{:S(2)}, u32[]{:S(2)}) collective-permute-start(bf16[4,320,128]{2,1,0:T(8,128)(2,1)S(1)} %get-tuple-element.37), channel_id=1, source_target_pairs={{0,2},{1,3},{2,0},{3,1},{4,6},{5,7},{6,4},{7,5},{8,10},{9,11},{10,... | collective-permute-start | bytes 983048 | tf_op jit(solution)/shard_map/ppermute | solution.py:193
  17.1 10.4 %collective-permute-start.3 = (bf16[704,128]{1,0:T(8,128)(2,1)S(1)}, bf16[704,128]{1,0:T(8,128)(2,1)S(1)}, u32[]{:S(2)}, u32[]{:S(2)}) collective-permute-start(bf16[704,128]{1,0:T(8,128)(2,1)S(1)} %get-tuple-element.27), channel_id=1, source_target_pairs={{0,8},{4,12},{8,0},{12,4},{1,9},{5,13},{9,1},{13,5},{2,10},{6,14},... | collective-permute-start | bytes 540680 | tf_op jit(solution)/shard_map/ppermute | solution.py:193
  22.6 12.6 %collective-permute-start.7 = (bf16[480,128]{1,0:T(8,128)(2,1)S(1)}, bf16[480,128]{1,0:T(8,128)(2,1)S(1)}, u32[]{:S(2)}, u32[]{:S(2)}) collective-permute-start(bf16[480,128]{1,0:T(8,128)(2,1)S(1)} %get-tuple-element.31), channel_id=1, source_target_pairs={{0,4},{4,0},{8,12},{12,8},{1,5},{5,1},{9,13},{13,9},{2,6},{6,2},{1... | collective-permute-start | bytes 368648 | tf_op jit(solution)/shard_map/ppermute | solution.py:193
  23.1 15.5 %collective-permute-start.8 = (bf16[480,128]{1,0:T(8,128)(2,1)S(1)}, bf16[480,128]{1,0:T(8,128)(2,1)S(1)}, u32[]{:S(2)}, u32[]{:S(2)}) collective-permute-start(bf16[480,128]{1,0:T(8,128)(2,1)S(1)} %get-tuple-element.32), channel_id=1, source_target_pairs={{0,8},{4,12},{8,0},{12,4},{1,9},{5,13},{9,1},{13,5},{2,10},{6,14},... | collective-permute-start | bytes 368648 | tf_op jit(solution)/shard_map/ppermute | solution.py:193
  25.2 13.3 %collective-permute-start.9 = (bf16[480,128]{1,0:T(8,128)(2,1)S(1)}, bf16[480,128]{1,0:T(8,128)(2,1)S(1)}, u32[]{:S(2)}, u32[]{:S(2)}) collective-permute-start(bf16[480,128]{1,0:T(8,128)(2,1)S(1)} %get-tuple-element.33), channel_id=1, source_target_pairs={{0,12},{4,8},{8,4},{12,0},{1,13},{5,9},{9,5},{13,1},{2,14},{6,10},... | collective-permute-start | bytes 368648 | tf_op jit(solution)/shard_map/ppermute | solution.py:193
  27.5 25.3 %copy-start.2 = (f32[1,128,1024]{2,1,0:T(8,128)S(1)}, f32[1,128,1024]{2,1,0:T(8,128)}, u32[]{:S(2)}) copy-start(f32[1,128,1024]{2,1,0:T(8,128)} %param.6) | copy-start | bytes 1572868
  27.5 25.3 %copy-start.3 = (s32[1,128,1024]{2,1,0:T(8,128)S(1)}, s32[1,128,1024]{2,1,0:T(8,128)}, u32[]{:S(2)}) copy-start(s32[1,128,1024]{2,1,0:T(8,128)} %param.7) | copy-start | bytes 1572868
  27.5 13.2 %collective-permute-start.4 = (bf16[704,128]{1,0:T(8,128)(2,1)S(1)}, bf16[704,128]{1,0:T(8,128)(2,1)S(1)}, u32[]{:S(2)}, u32[]{:S(2)}) collective-permute-start(bf16[704,128]{1,0:T(8,128)(2,1)S(1)} %shard_map.50.refs_0_), channel_id=1, source_target_pairs={{0,2},{1,3},{2,0},{3,1},{4,6},{5,7},{6,4},{7,5},{8,10},{9,11},{10,... | collective-permute-start | bytes 540680 | tf_op jit(solution)/shard_map/ppermute | solution.py:193
  29.6 12.4 %collective-permute-start.14 = (bf16[320,128]{1,0:T(8,128)(2,1)S(1)}, bf16[320,128]{1,0:T(8,128)(2,1)S(1)}, u32[]{:S(2)}, u32[]{:S(2)}) collective-permute-start(bf16[320,128]{1,0:T(8,128)(2,1)S(1)} %get-tuple-element.39), channel_id=1, source_target_pairs={{0,4},{4,0},{8,12},{12,8},{1,5},{5,1},{9,13},{13,9},{2,6},{6,2},{1... | collective-permute-start | bytes 245768 | tf_op jit(solution)/shard_map/ppermute | solution.py:193
  35.3 6.7 %collective-permute-start.15 = (bf16[320,128]{1,0:T(8,128)(2,1)S(1)}, bf16[320,128]{1,0:T(8,128)(2,1)S(1)}, u32[]{:S(2)}, u32[]{:S(2)}) collective-permute-start(bf16[320,128]{1,0:T(8,128)(2,1)S(1)} %get-tuple-element.40), channel_id=1, source_target_pairs={{0,8},{4,12},{8,0},{12,4},{1,9},{5,13},{9,1},{13,5},{2,10},{6,14},... | collective-permute-start | bytes 245768 | tf_op jit(solution)/shard_map/ppermute | solution.py:193
  38.6 9.9 %collective-permute-start.11 = (bf16[480,128]{1,0:T(8,128)(2,1)S(1)}, bf16[480,128]{1,0:T(8,128)(2,1)S(1)}, u32[]{:S(2)}, u32[]{:S(2)}) collective-permute-start(bf16[480,128]{1,0:T(8,128)(2,1)S(1)} %shard_map.54.refs_2_), channel_id=1, source_target_pairs={{0,2},{1,3},{2,0},{3,1},{4,6},{5,7},{6,4},{7,5},{8,10},{9,11},{10,... | collective-permute-start | bytes 368648 | tf_op jit(solution)/shard_map/ppermute | solution.py:193
  38.9 5.2 %collective-permute-start.16 = (bf16[320,128]{1,0:T(8,128)(2,1)S(1)}, bf16[320,128]{1,0:T(8,128)(2,1)S(1)}, u32[]{:S(2)}, u32[]{:S(2)}) collective-permute-start(bf16[320,128]{1,0:T(8,128)(2,1)S(1)} %get-tuple-element.41), channel_id=1, source_target_pairs={{0,12},{4,8},{8,4},{12,0},{1,13},{5,9},{9,5},{13,1},{2,14},{6,10},... | collective-permute-start | bytes 245768 | tf_op jit(solution)/shard_map/ppermute | solution.py:193
  40.8 10.7 %collective-permute-start.5 = (bf16[704,128]{1,0:T(8,128)(2,1)S(1)}, bf16[704,128]{1,0:T(8,128)(2,1)S(1)}, u32[]{:S(2)}, u32[]{:S(2)}) collective-permute-start(bf16[704,128]{1,0:T(8,128)(2,1)S(1)} %shard_map.51.refs_0_), channel_id=1, source_target_pairs={{0,1},{1,0},{2,3},{3,2},{4,5},{5,4},{6,7},{7,6},{8,9},{9,8},{10,11... | collective-permute-start | bytes 540680 | tf_op jit(solution)/shard_map/ppermute | solution.py:193
  44.1 4.9 %collective-permute-start.18 = (bf16[320,128]{1,0:T(8,128)(2,1)S(1)}, bf16[320,128]{1,0:T(8,128)(2,1)S(1)}, u32[]{:S(2)}, u32[]{:S(2)}) collective-permute-start(bf16[320,128]{1,0:T(8,128)(2,1)S(1)} %shard_map.58.refs_0_), channel_id=1, source_target_pairs={{0,2},{1,3},{2,0},{3,1},{4,6},{5,7},{6,4},{7,5},{8,10},{9,11},{10,... | collective-permute-start | bytes 245768 | tf_op jit(solution)/shard_map/ppermute | solution.py:193
  45.4 6.1 %collective-permute-start.10 = (bf16[480,128]{1,0:T(8,128)(2,1)S(1)}, bf16[480,128]{1,0:T(8,128)(2,1)S(1)}, u32[]{:S(2)}, u32[]{:S(2)}) collective-permute-start(bf16[480,128]{1,0:T(8,128)(2,1)S(1)} %shard_map.54.refs_2_), channel_id=1, source_target_pairs={{0,1},{1,0},{2,3},{3,2},{4,5},{5,4},{6,7},{7,6},{8,9},{9,8},{10,11... | collective-permute-start | bytes 368648 | tf_op jit(solution)/shard_map/ppermute | solution.py:193
  48.5 3.0 %collective-permute-start.12 = (bf16[480,128]{1,0:T(8,128)(2,1)S(1)}, bf16[480,128]{1,0:T(8,128)(2,1)S(1)}, u32[]{:S(2)}, u32[]{:S(2)}) collective-permute-start(bf16[480,128]{1,0:T(8,128)(2,1)S(1)} %collective-permute-done.11.refs_4_), channel_id=1, source_target_pairs={{0,1},{1,0},{2,3},{3,2},{4,5},{5,4},{6,7},{7,6},{8,9},{9,8},{10,11... | collective-permute-start | bytes 368648 | tf_op jit(solution)/shard_map/ppermute | solution.py:193
  48.5 4.3 %collective-permute-start.17 = (bf16[320,128]{1,0:T(8,128)(2,1)S(1)}, bf16[320,128]{1,0:T(8,128)(2,1)S(1)}, u32[]{:S(2)}, u32[]{:S(2)}) collective-permute-start(bf16[320,128]{1,0:T(8,128)(2,1)S(1)} %shard_map.58.refs_0_), channel_id=1, source_target_pairs={{0,1},{1,0},{2,3},{3,2},{4,5},{5,4},{6,7},{7,6},{8,9},{9,8},{10,11... | collective-permute-start | bytes 245768 | tf_op jit(solution)/shard_map/ppermute | solution.py:193
  49.0 3.8 %collective-permute-start.19 = (bf16[320,128]{1,0:T(8,128)(2,1)S(1)}, bf16[320,128]{1,0:T(8,128)(2,1)S(1)}, u32[]{:S(2)}, u32[]{:S(2)}) collective-permute-start(bf16[320,128]{1,0:T(8,128)(2,1)S(1)} %collective-permute-done.18.refs_2_), channel_id=1, source_target_pairs={{0,1},{1,0},{2,3},{3,2},{4,5},{5,4},{6,7},{7,6},{8,9},{9,8},{10,11... | collective-permute-start | bytes 245768 | tf_op jit(solution)/shard_map/ppermute | solution.py:193

commit v3 on v2

--- a/solution.py
+++ b/solution.py
@@ -208,46 +208,63 @@
     other, other_routes = over_core(tokens), over_core(routes.T)
     lhs = lift(tokens, routes.T)
     other_lhs = lift(other, other_routes)
-    shape, found = [], []
-    for panels, mode in plan:
+    def gram(panels, mode, at):
         blocks = count(panels)
-        first = mode == "z"
-        dims = (2, 2 * PIECE * blocks, BLK) if first else (experts, PIECE * blocks, BLK)
-        keep, send = call(functools.partial(gram_kernel, panels, mode, experts),
-                          [(dims, f32), (dims, bf16)], where, lhs, tokens, other_lhs, other)
-        size = 2 * PIECE if first else PIECE
-        flat = (size * blocks, BLK)
-        if not first:
-            got = over_x(send)
-        if mode == "direct":
-            own, *away = call(pair_kernel, [(flat, f32)] + [(flat, bf16)] * (experts - 1), keep, got, smem=False)
-            came = [over("expert", s + 1)(a) for s, a in enumerate(away)]
-            final = call(sum_kernel, [(flat, bf16)], own, *came, smem=False)[0]
-        else:
-            if not first:
-                keep, send = call(split_kernel, [((2,) + flat, f32), ((2,) + flat, bf16)], keep, got, smem=False)
-            near = over("expert", 1)(send)
-            own, away = call(pair_kernel, [(flat, f32), (flat, bf16)], keep, near, smem=False)
-            far = over("expert", 2)(away)
-            final = call(sum_kernel, [(flat, bf16)], own, far, smem=False)[0]
-        if first:
-            final = call(sum_kernel, [(flat, bf16)], final, over_x(final), smem=False)[0]
-            pieces = [final, over_core(final)]
-        else:
-            by_x = over_x(final)
-            pieces = [final, over_core(final), by_x, over_core(by_x)]
-        shape.append((panels, size, len(pieces)))
-        found.append(pieces)
-    gram, square = call(functools.partial(early_kernel, tuple(shape[:-1])),
+        dims = (2, 2 * PIECE * blocks, BLK) if mode == "z" else (experts, PIECE * blocks, BLK)
+        return call(functools.partial(gram_kernel, panels, mode, experts),
+                    [(dims, f32), (dims, bf16)], at, lhs, tokens, other_lhs, other)
+
+    def flat(panels, mode=""):
+        return ((2 if mode == "z" else 1) * PIECE * count(panels), BLK)
+
+    def summed(*parts):
+        return call(sum_kernel, [(parts[0].shape, bf16)], *parts, smem=False)[0]
+
+    over_z = [over("expert", bit) for bit in range(4)]
+    chunk_a, chunk_z, chunk_b = plan
+    keep_a, send_a = gram(chunk_a, "x", where)
+    got_a = over_x(send_a)
+    keep_z, send_z = gram(chunk_z, "z", after(where, send_a))
+    near_z = over_z[1](send_z)
+    keep_b, send_b = gram(chunk_b, "x", after(where, send_z))
+    got_b = over_x(send_b)
+    own_z, send_z = call(pair_kernel, [(flat(chunk_z, "z"), f32), (flat(chunk_z, "z"), bf16)],
+                         keep_z, after(near_z, send_b), smem=False)
+    far_z = over_z[2](send_z)
+
+    def first_hop(panels, keep, got):
+        keep, send = call(split_kernel, [((2,) + flat(panels), f32), ((2,) + flat(panels), bf16)],
+                          keep, got, smem=False)
+        return keep, over_z[1](send)
+
+    def second_hop(panels, keep, near):
+        own, send = call(pair_kernel, [(flat(panels), f32), (flat(panels), bf16)], keep, near, smem=False)
+        return summed(own, over_z[2](send))
+
+    own_a, near_a = first_hop(chunk_a, keep_a, after(got_a, send_b))
+    own_b, near_b = first_hop(chunk_b, keep_b, got_b)
+    part_z = summed(own_z, far_z)
+    both_z = summed(part_z, over_x(part_z))
+    final_a = second_hop(chunk_a, own_a, near_a)
+    final_b = second_hop(chunk_b, own_b, near_b)
+    x_a = over_x(final_a)
+    x_b = over_x(final_b)
+    shape = ((chunk_z, 2 * PIECE, 2), (chunk_a, PIECE, 4), (chunk_b, PIECE, 4))
+    gram_early, square = call(functools.partial(early_kernel, shape[:2]),
                         [((width, width), bf16), ((PIECE, BLK), f32)],
-                        where, *[p for pieces in found[:-1] for p in pieces])
-    out, _ = call(functools.partial(steps_kernel, tuple(shape[-1:])),
+                        where, both_z, over_core(both_z), final_a, over_core(final_a), x_a, over_core(x_a))
+    last = [final_b, over_core(final_b), x_b, over_core(x_b)]
+    out, _ = call(functools.partial(steps_kernel, shape[2:]),
                   [(w_orig.shape[1:], f32), ((width, width), bf16)],
-                  where, w_orig[0], mask[0], gram, square, *found[-1], aliases={3: 1})
+                  where, w_orig[0], mask[0], gram_early, square, *last, aliases={3: 1})
     return out[None]
 
 
-PLAN = (((2,), "z"), ((3,), "direct"), ((0, 1), "direct"))
+def after(value, earlier):
+    return lax.optimization_barrier((value, earlier))[0]
+
+
+PLAN = ((3,), (2,), (0, 1))
 
 
 def solution(mesh):

time: 56.4 us -> 53.6 us (0.950)
  starting transfers between devices: 30.9 us -> 25.8 us
  waiting for transfers between devices: 11 us -> 13.2 us
    ppermute x20 -> x18, starting transfers between devices: 30.9 us -> 25.8 us  [over(): return lambda a: lax.ppermute(a, axis, [(i, i ^ bit) for i in range(4)])]
    ppermute x20 -> x18, waiting for transfers between devices: 11 us -> 13.2 us  [over(): return lambda a: lax.ppermute(a, axis, [(i, i ^ bit) for i in range(4)])]
    pallas_call x14 -> x16, Pallas kernels: 12 us -> 12 us  [call(): pl.pallas_call(kernel, in_specs=[SMEM if smem and i == 0 else VMEM for i...]
  transfers between devices with their start and end apart: 20 -> 18, of which waited for: 5 -> 4; matrix products, arithmetic and copies ran while one was open for 0% -> 0% of each run, Pallas kernels for 11% -> 11%
where the time goes in v3:
time: 53.6 us; the launch traced here: 53.3 us
  starting transfers between devices  25.8 us (48%)
  waiting for transfers between devices  13.2 us (25%)
  Pallas kernels  12 us (22%)
  local copies, waits for them, and re-layouts  2.12 us (4%)
    ppermute x18, starting transfers between devices, over(): return lambda a: lax.ppermute(a, axis, [(i, i ^ bit) for i in range(4)])  25.8 us
    ppermute x18, waiting for transfers between devices, over(): return lambda a: lax.ppermute(a, axis, [(i, i ^ bit) for i in range(4)])  13.2 us
    pallas_call x16, Pallas kernels, call(): pl.pallas_call(kernel, in_specs=[SMEM if smem and i == 0 else VMEM for i...  12 us
    unnamed x10, local copies, waits for them, and re-layouts  2.12 us
  transfers between devices with their start and end apart: 18, of which 4 were waited for; matrix products, arithmetic and copies ran while one was open for 0% of the time, Pallas kernels for 11%

profile of v3, /device:TPU:1, one launch (start us, length us, event | category | flops | bytes accessed | tf_op | source)
XLA Modules:
  0.0 53.3 jit_solution(13384452804553659975)
XLA Ops:
  0.0 0.1 collective-permute-start
  0.1 0.5 collective-permute-start.1
  0.5 0.1 pad_add_fusion.where
  0.6 0.0 copy-start
  0.6 1.2 %copy-done = bf16[512,1024]{1,0:T(8,128)(2,1)S(1)} copy-done((bf16[512,1024]{1,0:T(8,128)(2,1)S(1)}, bf16[512,1024]{1,0:T(8,128)(2,1)}, u32[]{:S(2)}) %copy-start) | copy-done | bytes 1048600
  1.8 0.0 copy-start.4
  1.8 0.7 %copy-done.4 = s32[512,2]{0,1:T(2,128)S(1)} copy-done((s32[512,2]{0,1:T(2,128)S(1)}, s32[512,2]{0,1:T(2,128)}, u32[]{:S(2)}) %copy-start.4) | copy-done | bytes 4120
  2.5 1.0 %shard_map.46.lhs_a = bf16[2048,512]{1,0:T(8,128)(2,1)S(1)} custom-call(s32[3]{0:T(128)S(1)} %pad_add_fusion.where, bf16[512,1024]{1,0:T(8,128)(2,1)S(1)} %copy-done, s32[2,512]{1,0:T(2,128)S(1)} %bitcast.10), custom_call_target="tpu_custom_call" | custom-call | tf_op jit(solution)/shard_map/pallas_call | solution.py:183
  3.5 0.0 copy-start.1
  3.5 0.0 collective-permute-done.1.routes_t
  3.5 0.0 collective-permute-done.tokens.tok_b
  3.5 1.0 %shard_map.47.lhs_b = bf16[2048,512]{1,0:T(8,128)(2,1)S(1)} custom-call(s32[3]{0:T(128)S(1)} %pad_add_fusion.where, bf16[512,1024]{1,0:T(8,128)(2,1)S(1)} %collective-permute-done.tokens.tok_b, s32[2,512]{1,0:T(2,128)S(1)} %collective-permute-done.1.routes_t), custom_call_target="tpu_custom_call" | custom-call | tf_op jit(solution)/shard_map/pallas_call | solution.py:183
  4.5 0.2 copy-done.1
  4.7 1.8 %shard_map.48 = (f32[4,480,128]{2,1,0:T(8,128)S(1)}, bf16[4,480,128]{2,1,0:T(8,128)(2,1)S(1)}) custom-call(s32[3]{0:T(128)S(1)} %pad_add_fusion.where, bf16[2048,512]{1,0:T(8,128)(2,1)S(1)} %shard_map.46.lhs_a, bf16[512,1024]{1,0:T(8,128)(2,1)S(1)} %copy-done.1, bf16[2048,512]{1,0:T(8,128)(2,1)S(1)} %shard_map.47.lhs_b, ...), custom_call_target="tpu_custom_call" | custom-call | tf_op jit(solution)/shard_map/pallas_call | solution.py:183
  6.6 2.3 %collective-permute-start.6 = (bf16[4,480,128]{2,1,0:T(8,128)(2,1)S(1)}, bf16[4,480,128]{2,1,0:T(8,128)(2,1)S(1)}, u32[]{:S(2)}, u32[]{:S(2)}) collective-permute-start(bf16[4,480,128]{2,1,0:T(8,128)(2,1)S(1)} %get-tuple-element.28), channel_id=1, source_target_pairs={{0,2},{1,3},{2,0},{3,1},{4,6},{5,7},{6,4},{7,5},{8,10},{9,11},{10,... | collective-permute-start | bytes 1474568 | tf_op jit(solution)/shard_map/ppermute | solution.py:193
  8.9 1.5 %shard_map.49 = (f32[2,704,128]{2,1,0:T(8,128)S(1)}, bf16[2,704,128]{2,1,0:T(8,128)(2,1)S(1)}) custom-call(s32[3]{0:T(128)S(1)} %pad_add_fusion.where, bf16[2048,512]{1,0:T(8,128)(2,1)S(1)} %shard_map.46.lhs_a, bf16[512,1024]{1,0:T(8,128)(2,1)S(1)} %copy-done.1, bf16[2048,512]{1,0:T(8,128)(2,1)S(1)} %shard_map.47.lhs_b, ...), custom_call_target="tpu_custom_call" | custom-call | tf_op jit(solution)/shard_map/pallas_call | solution.py:183
  10.4 1.4 %collective-permute-start.2 = (bf16[2,704,128]{2,1,0:T(8,128)(2,1)S(1)}, bf16[2,704,128]{2,1,0:T(8,128)(2,1)S(1)}, u32[]{:S(2)}, u32[]{:S(2)}) collective-permute-start(bf16[2,704,128]{2,1,0:T(8,128)(2,1)S(1)} %get-tuple-element.31), channel_id=1, source_target_pairs={{0,4},{4,0},{8,12},{12,8},{1,5},{5,1},{9,13},{13,9},{2,6},{6,2},{1... | collective-permute-start | bytes 1081352 | tf_op jit(solution)/shard_map/ppermute | solution.py:193
  11.8 1.5 %shard_map.50 = (f32[4,320,128]{2,1,0:T(8,128)S(1)}, bf16[4,320,128]{2,1,0:T(8,128)(2,1)S(1)}) custom-call(s32[3]{0:T(128)S(1)} %pad_add_fusion.where, bf16[2048,512]{1,0:T(8,128)(2,1)S(1)} %shard_map.46.lhs_a, bf16[512,1024]{1,0:T(8,128)(2,1)S(1)} %copy-done.1, bf16[2048,512]{1,0:T(8,128)(2,1)S(1)} %shard_map.47.lhs_b, ...), custom_call_target="tpu_custom_call" | custom-call | tf_op jit(solution)/shard_map/pallas_call | solution.py:183
  13.3 0.3 collective-permute-start.12
  13.6 6.4 %collective-permute-done.6.got = bf16[4,480,128]{2,1,0:T(8,128)(2,1)S(1)} collective-permute-done((bf16[4,480,128]{2,1,0:T(8,128)(2,1)S(1)}, bf16[4,480,128]{2,1,0:T(8,128)(2,1)S(1)}, u32[]{:S(2)}, u32[]{:S(2)}) %collective-permute-start.6) | collective-permute-done | bytes 491552 | tf_op jit(solution)/shard_map/ppermute | solution.py:193
  20.0 0.1 shard_map.54
  20.1 1.3 %collective-permute-start.7 = (bf16[2,480,128]{2,1,0:T(8,128)(2,1)S(1)}, bf16[2,480,128]{2,1,0:T(8,128)(2,1)S(1)}, u32[]{:S(2)}, u32[]{:S(2)}) collective-permute-start(bf16[2,480,128]{2,1,0:T(8,128)(2,1)S(1)} %get-tuple-element.40), channel_id=1, source_target_pairs={{0,4},{4,0},{8,12},{12,8},{1,5},{5,1},{9,13},{13,9},{2,6},{6,2},{1... | collective-permute-start | bytes 737288 | tf_op jit(solution)/shard_map/ppermute | solution.py:193
  21.4 0.0 collective-permute-done.2.got
  21.4 0.1 shard_map.51
  21.5 2.4 %collective-permute-start.3 = (bf16[704,128]{1,0:T(8,128)(2,1)S(1)}, bf16[704,128]{1,0:T(8,128)(2,1)S(1)}, u32[]{:S(2)}, u32[]{:S(2)}) collective-permute-start(bf16[704,128]{1,0:T(8,128)(2,1)S(1)} %get-tuple-element.36), channel_id=1, source_target_pairs={{0,8},{4,12},{8,0},{12,4},{1,9},{5,13},{9,1},{13,5},{2,10},{6,14},... | collective-permute-start | bytes 540680 | tf_op jit(solution)/shard_map/ppermute | solution.py:193
  23.8 3.2 %collective-permute-done.12.got = bf16[4,320,128]{2,1,0:T(8,128)(2,1)S(1)} collective-permute-done((bf16[4,320,128]{2,1,0:T(8,128)(2,1)S(1)}, bf16[4,320,128]{2,1,0:T(8,128)(2,1)S(1)}, u32[]{:S(2)}, u32[]{:S(2)}) %collective-permute-start.12) | collective-permute-done | bytes 327712 | tf_op jit(solution)/shard_map/ppermute | solution.py:193
  27.0 0.1 shard_map.58
  27.1 0.0 copy-start.2
  27.1 0.0 copy-start.3
  27.1 1.3 %collective-permute-start.13 = (bf16[2,320,128]{2,1,0:T(8,128)(2,1)S(1)}, bf16[2,320,128]{2,1,0:T(8,128)(2,1)S(1)}, u32[]{:S(2)}, u32[]{:S(2)}) collective-permute-start(bf16[2,320,128]{2,1,0:T(8,128)(2,1)S(1)} %get-tuple-element.47), channel_id=1, source_target_pairs={{0,4},{4,0},{8,12},{12,8},{1,5},{5,1},{9,13},{13,9},{2,6},{6,2},{1... | collective-permute-start | bytes 491528 | tf_op jit(solution)/shard_map/ppermute | solution.py:193
  28.4 0.0 collective-permute-done.7.got
  28.4 3.2 %collective-permute-start.8 = (bf16[480,128]{1,0:T(8,128)(2,1)S(1)}, bf16[480,128]{1,0:T(8,128)(2,1)S(1)}, u32[]{:S(2)}, u32[]{:S(2)}) collective-permute-start(bf16[480,128]{1,0:T(8,128)(2,1)S(1)} %get-tuple-element.42), channel_id=1, source_target_pairs={{0,8},{4,12},{8,0},{12,4},{1,9},{5,13},{9,1},{13,5},{2,10},{6,14},... | collective-permute-start | bytes 368648 | tf_op jit(solution)/shard_map/ppermute | solution.py:193
  31.7 0.0 collective-permute-done.3.refs_1_
  31.7 1.3 %collective-permute-start.4 = (bf16[704,128]{1,0:T(8,128)(2,1)S(1)}, bf16[704,128]{1,0:T(8,128)(2,1)S(1)}, u32[]{:S(2)}, u32[]{:S(2)}) collective-permute-start(bf16[704,128]{1,0:T(8,128)(2,1)S(1)} %shard_map.52.refs_0_), channel_id=1, source_target_pairs={{0,2},{1,3},{2,0},{3,1},{4,6},{5,7},{6,4},{7,5},{8,10},{9,11},{10,... | collective-permute-start | bytes 540680 | tf_op jit(solution)/shard_map/ppermute | solution.py:193
  33.0 2.8 %collective-permute-done.13.got = bf16[2,320,128]{2,1,0:T(8,128)(2,1)S(1)} collective-permute-done((bf16[2,320,128]{2,1,0:T(8,128)(2,1)S(1)}, bf16[2,320,128]{2,1,0:T(8,128)(2,1)S(1)}, u32[]{:S(2)}, u32[]{:S(2)}) %collective-permute-start.13) | collective-permute-done | bytes 163872 | tf_op jit(solution)/shard_map/ppermute | solution.py:193
  35.9 0.1 collective-permute-start.14
  36.0 0.0 collective-permute-done.8.refs_1_
  36.0 1.2 %collective-permute-start.10 = (bf16[480,128]{1,0:T(8,128)(2,1)S(1)}, bf16[480,128]{1,0:T(8,128)(2,1)S(1)}, u32[]{:S(2)}, u32[]{:S(2)}) collective-permute-start(bf16[480,128]{1,0:T(8,128)(2,1)S(1)} %shard_map.56.refs_2_), channel_id=1, source_target_pairs={{0,2},{1,3},{2,0},{3,1},{4,6},{5,7},{6,4},{7,5},{8,10},{9,11},{10,... | collective-permute-start | bytes 368648 | tf_op jit(solution)/shard_map/ppermute | solution.py:193
  37.3 0.0 collective-permute-done.4.refs_1_
  37.3 6.1 %collective-permute-start.5 = (bf16[704,128]{1,0:T(8,128)(2,1)S(1)}, bf16[704,128]{1,0:T(8,128)(2,1)S(1)}, u32[]{:S(2)}, u32[]{:S(2)}) collective-permute-start(bf16[704,128]{1,0:T(8,128)(2,1)S(1)} %shard_map.53.refs_0_), channel_id=1, source_target_pairs={{0,1},{1,0},{2,3},{3,2},{4,5},{5,4},{6,7},{7,6},{8,9},{9,8},{10,11... | collective-permute-start | bytes 540680 | tf_op jit(solution)/shard_map/ppermute | solution.py:193
  43.5 0.0 collective-permute-done.14.refs_1_
  43.5 1.6 %collective-permute-start.16 = (bf16[320,128]{1,0:T(8,128)(2,1)S(1)}, bf16[320,128]{1,0:T(8,128)(2,1)S(1)}, u32[]{:S(2)}, u32[]{:S(2)}) collective-permute-start(bf16[320,128]{1,0:T(8,128)(2,1)S(1)} %shard_map.60.refs_0_), channel_id=1, source_target_pairs={{0,2},{1,3},{2,0},{3,1},{4,6},{5,7},{6,4},{7,5},{8,10},{9,11},{10,... | collective-permute-start | bytes 245768 | tf_op jit(solution)/shard_map/ppermute | solution.py:193
  45.0 0.8 %collective-permute-start.9 = (bf16[480,128]{1,0:T(8,128)(2,1)S(1)}, bf16[480,128]{1,0:T(8,128)(2,1)S(1)}, u32[]{:S(2)}, u32[]{:S(2)}) collective-permute-start(bf16[480,128]{1,0:T(8,128)(2,1)S(1)} %shard_map.56.refs_2_), channel_id=1, source_target_pairs={{0,1},{1,0},{2,3},{3,2},{4,5},{5,4},{6,7},{7,6},{8,9},{9,8},{10,11... | collective-permute-start | bytes 368648 | tf_op jit(solution)/shard_map/ppermute | solution.py:193
  45.8 0.0 collective-permute-done.10.refs_4_
  45.8 1.1 %collective-permute-start.11 = (bf16[480,128]{1,0:T(8,128)(2,1)S(1)}, bf16[480,128]{1,0:T(8,128)(2,1)S(1)}, u32[]{:S(2)}, u32[]{:S(2)}) collective-permute-start(bf16[480,128]{1,0:T(8,128)(2,1)S(1)} %collective-permute-done.10.refs_4_), channel_id=1, source_target_pairs={{0,1},{1,0},{2,3},{3,2},{4,5},{5,4},{6,7},{7,6},{8,9},{9,8},{10,11... | collective-permute-start | bytes 368648 | tf_op jit(solution)/shard_map/ppermute | solution.py:193
  47.0 0.0 collective-permute-start.15
  47.0 0.7 %collective-permute-done.16.refs_2_ = bf16[320,128]{1,0:T(8,128)(2,1)S(1)} collective-permute-done((bf16[320,128]{1,0:T(8,128)(2,1)S(1)}, bf16[320,128]{1,0:T(8,128)(2,1)S(1)}, u32[]{:S(2)}, u32[]{:S(2)}) %collective-permute-start.16) | collective-permute-done | bytes 81952 | tf_op jit(solution)/shard_map/ppermute | solution.py:193
  47.7 0.9 %collective-permute-start.17 = (bf16[320,128]{1,0:T(8,128)(2,1)S(1)}, bf16[320,128]{1,0:T(8,128)(2,1)S(1)}, u32[]{:S(2)}, u32[]{:S(2)}) collective-permute-start(bf16[320,128]{1,0:T(8,128)(2,1)S(1)} %collective-permute-done.16.refs_2_), channel_id=1, source_target_pairs={{0,1},{1,0},{2,3},{3,2},{4,5},{5,4},{6,7},{7,6},{8,9},{9,8},{10,11... | collective-permute-start | bytes 245768 | tf_op jit(solution)/shard_map/ppermute | solution.py:193
  48.6 0.0 collective-permute-done.5.refs_1_
  48.6 0.0 collective-permute-done.9.refs_3_
  48.6 0.0 collective-permute-done.11.refs_5_
  48.6 1.2 %shard_map.57 = (bf16[1024,1024]{1,0:T(8,128)(2,1)S(1)}, f32[32,128]{1,0:T(8,128)S(1)}) custom-call(s32[3]{0:T(128)S(1)} %pad_add_fusion.where, bf16[704,128]{1,0:T(8,128)(2,1)S(1)} %shard_map.53.refs_0_, bf16[704,128]{1,0:T(8,128)(2,1)S(1)} %collective-permute-done.5.refs_1_, bf16[480,128]{1,0:T(8,128)(2,1)S(1)} %shard_map.56.refs_2_, ...), custom_call_target="tpu_custom_call" | custom-call | tf_op jit(solution)/shard_map/pallas_call | solution.py:183
  49.9 0.0 collective-permute-done.15.refs_1_
  49.9 0.0 collective-permute-done.17.refs_3_
  49.9 0.0 copy-done.2
  49.9 0.0 copy-done.3
  49.9 3.4 %shard_map.61 = (f32[128,1024]{1,0:T(8,128)}, bf16[1024,1024]{1,0:T(8,128)(2,1)S(1)}) custom-call(s32[3]{0:T(128)S(1)} %pad_add_fusion.where, f32[128,1024]{1,0:T(8,128)S(1)} %bitcast.7, s32[128,1024]{1,0:T(8,128)S(1)} %bitcast.8, bf16[1024,1024]{1,0:T(8,128)(2,1)S(1)} %get-tuple-element.43.old, ...), custom_call_target="tpu_custom_call", output_to_operand_aliasing={{1}: (3, {})} | custom-call | tf_op jit(solution)/shard_map/pallas_call | solution.py:183
  (6 shorter events, 0.2 us)
Async XLA Ops:
  0.0 3.5 %collective-permute-start = (bf16[512,1024]{1,0:T(8,128)(2,1)}, bf16[512,1024]{1,0:T(8,128)(2,1)S(1)}, u32[]{:S(2)}, u32[]{:S(2)}) collective-permute-start(bf16[512,1024]{1,0:T(8,128)(2,1)} %tok_a.5), channel_id=1, source_target_pairs={{0,1},{1,0},{2,3},{3,2},{4,5},{5,4},{6,7},{7,6},{8,9},{9,8},{10,11... | collective-permute-start | bytes 3145736 | tf_op jit(solution)/shard_map/ppermute | solution.py:193
  0.1 3.5 %collective-permute-start.1 = (s32[2,512]{1,0:T(2,128)}, s32[2,512]{1,0:T(2,128)S(1)}, u32[]{:S(2)}, u32[]{:S(2)}) collective-permute-start(s32[2,512]{1,0:T(2,128)} %bitcast.9), channel_id=1, source_target_pairs={{0,1},{1,0},{2,3},{3,2},{4,5},{5,4},{6,7},{7,6},{8,9},{9,8},{10,11... | collective-permute-start | bytes 12296 | tf_op jit(solution)/shard_map/ppermute | solution.py:193
  0.6 1.2 %copy-start = (bf16[512,1024]{1,0:T(8,128)(2,1)S(1)}, bf16[512,1024]{1,0:T(8,128)(2,1)}, u32[]{:S(2)}) copy-start(bf16[512,1024]{1,0:T(8,128)(2,1)} %tok_a.5) | copy-start | bytes 3145732
  1.8 0.7 %copy-start.4 = (s32[512,2]{0,1:T(2,128)S(1)}, s32[512,2]{0,1:T(2,128)}, u32[]{:S(2)}) copy-start(s32[512,2]{0,1:T(2,128)} %param.5) | copy-start | bytes 12292
  3.5 1.2 %copy-start.1 = (bf16[512,1024]{1,0:T(8,128)(2,1)S(1)}, bf16[512,1024]{1,0:T(8,128)(2,1)}, u32[]{:S(2)}) copy-start(bf16[512,1024]{1,0:T(8,128)(2,1)} %tok_a.5) | copy-start | bytes 3145732
  6.6 13.4 %collective-permute-start.6 = (bf16[4,480,128]{2,1,0:T(8,128)(2,1)S(1)}, bf16[4,480,128]{2,1,0:T(8,128)(2,1)S(1)}, u32[]{:S(2)}, u32[]{:S(2)}) collective-permute-start(bf16[4,480,128]{2,1,0:T(8,128)(2,1)S(1)} %get-tuple-element.28), channel_id=1, source_target_pairs={{0,2},{1,3},{2,0},{3,1},{4,6},{5,7},{6,4},{7,5},{8,10},{9,11},{10,... | collective-permute-start | bytes 1474568 | tf_op jit(solution)/shard_map/ppermute | solution.py:193
  10.4 11.0 %collective-permute-start.2 = (bf16[2,704,128]{2,1,0:T(8,128)(2,1)S(1)}, bf16[2,704,128]{2,1,0:T(8,128)(2,1)S(1)}, u32[]{:S(2)}, u32[]{:S(2)}) collective-permute-start(bf16[2,704,128]{2,1,0:T(8,128)(2,1)S(1)} %get-tuple-element.31), channel_id=1, source_target_pairs={{0,4},{4,0},{8,12},{12,8},{1,5},{5,1},{9,13},{13,9},{2,6},{6,2},{1... | collective-permute-start | bytes 1081352 | tf_op jit(solution)/shard_map/ppermute | solution.py:193
  13.3 13.7 %collective-permute-start.12 = (bf16[4,320,128]{2,1,0:T(8,128)(2,1)S(1)}, bf16[4,320,128]{2,1,0:T(8,128)(2,1)S(1)}, u32[]{:S(2)}, u32[]{:S(2)}) collective-permute-start(bf16[4,320,128]{2,1,0:T(8,128)(2,1)S(1)} %get-tuple-element.33), channel_id=1, source_target_pairs={{0,2},{1,3},{2,0},{3,1},{4,6},{5,7},{6,4},{7,5},{8,10},{9,11},{10,... | collective-permute-start | bytes 983048 | tf_op jit(solution)/shard_map/ppermute | solution.py:193
  20.1 8.3 %collective-permute-start.7 = (bf16[2,480,128]{2,1,0:T(8,128)(2,1)S(1)}, bf16[2,480,128]{2,1,0:T(8,128)(2,1)S(1)}, u32[]{:S(2)}, u32[]{:S(2)}) collective-permute-start(bf16[2,480,128]{2,1,0:T(8,128)(2,1)S(1)} %get-tuple-element.40), channel_id=1, source_target_pairs={{0,4},{4,0},{8,12},{12,8},{1,5},{5,1},{9,13},{13,9},{2,6},{6,2},{1... | collective-permute-start | bytes 737288 | tf_op jit(solution)/shard_map/ppermute | solution.py:193
  21.5 10.2 %collective-permute-start.3 = (bf16[704,128]{1,0:T(8,128)(2,1)S(1)}, bf16[704,128]{1,0:T(8,128)(2,1)S(1)}, u32[]{:S(2)}, u32[]{:S(2)}) collective-permute-start(bf16[704,128]{1,0:T(8,128)(2,1)S(1)} %get-tuple-element.36), channel_id=1, source_target_pairs={{0,8},{4,12},{8,0},{12,4},{1,9},{5,13},{9,1},{13,5},{2,10},{6,14},... | collective-permute-start | bytes 540680 | tf_op jit(solution)/shard_map/ppermute | solution.py:193
  27.1 22.8 %copy-start.2 = (f32[1,128,1024]{2,1,0:T(8,128)S(1)}, f32[1,128,1024]{2,1,0:T(8,128)}, u32[]{:S(2)}) copy-start(f32[1,128,1024]{2,1,0:T(8,128)} %param.6) | copy-start | bytes 1572868
  27.1 22.8 %copy-start.3 = (s32[1,128,1024]{2,1,0:T(8,128)S(1)}, s32[1,128,1024]{2,1,0:T(8,128)}, u32[]{:S(2)}) copy-start(s32[1,128,1024]{2,1,0:T(8,128)} %param.7) | copy-start | bytes 1572868
  27.1 8.7 %collective-permute-start.13 = (bf16[2,320,128]{2,1,0:T(8,128)(2,1)S(1)}, bf16[2,320,128]{2,1,0:T(8,128)(2,1)S(1)}, u32[]{:S(2)}, u32[]{:S(2)}) collective-permute-start(bf16[2,320,128]{2,1,0:T(8,128)(2,1)S(1)} %get-tuple-element.47), channel_id=1, source_target_pairs={{0,4},{4,0},{8,12},{12,8},{1,5},{5,1},{9,13},{13,9},{2,6},{6,2},{1... | collective-permute-start | bytes 491528 | tf_op jit(solution)/shard_map/ppermute | solution.py:193
  28.4 7.5 %collective-permute-start.8 = (bf16[480,128]{1,0:T(8,128)(2,1)S(1)}, bf16[480,128]{1,0:T(8,128)(2,1)S(1)}, u32[]{:S(2)}, u32[]{:S(2)}) collective-permute-start(bf16[480,128]{1,0:T(8,128)(2,1)S(1)} %get-tuple-element.42), channel_id=1, source_target_pairs={{0,8},{4,12},{8,0},{12,4},{1,9},{5,13},{9,1},{13,5},{2,10},{6,14},... | collective-permute-start | bytes 368648 | tf_op jit(solution)/shard_map/ppermute | solution.py:193
  31.7 5.5 %collective-permute-start.4 = (bf16[704,128]{1,0:T(8,128)(2,1)S(1)}, bf16[704,128]{1,0:T(8,128)(2,1)S(1)}, u32[]{:S(2)}, u32[]{:S(2)}) collective-permute-start(bf16[704,128]{1,0:T(8,128)(2,1)S(1)} %shard_map.52.refs_0_), channel_id=1, source_target_pairs={{0,2},{1,3},{2,0},{3,1},{4,6},{5,7},{6,4},{7,5},{8,10},{9,11},{10,... | collective-permute-start | bytes 540680 | tf_op jit(solution)/shard_map/ppermute | solution.py:193
  35.9 7.6 %collective-permute-start.14 = (bf16[320,128]{1,0:T(8,128)(2,1)S(1)}, bf16[320,128]{1,0:T(8,128)(2,1)S(1)}, u32[]{:S(2)}, u32[]{:S(2)}) collective-permute-start(bf16[320,128]{1,0:T(8,128)(2,1)S(1)} %get-tuple-element.49), channel_id=1, source_target_pairs={{0,8},{4,12},{8,0},{12,4},{1,9},{5,13},{9,1},{13,5},{2,10},{6,14},... | collective-permute-start | bytes 245768 | tf_op jit(solution)/shard_map/ppermute | solution.py:193
  36.0 9.8 %collective-permute-start.10 = (bf16[480,128]{1,0:T(8,128)(2,1)S(1)}, bf16[480,128]{1,0:T(8,128)(2,1)S(1)}, u32[]{:S(2)}, u32[]{:S(2)}) collective-permute-start(bf16[480,128]{1,0:T(8,128)(2,1)S(1)} %shard_map.56.refs_2_), channel_id=1, source_target_pairs={{0,2},{1,3},{2,0},{3,1},{4,6},{5,7},{6,4},{7,5},{8,10},{9,11},{10,... | collective-permute-start | bytes 368648 | tf_op jit(solution)/shard_map/ppermute | solution.py:193
  37.3 11.3 %collective-permute-start.5 = (bf16[704,128]{1,0:T(8,128)(2,1)S(1)}, bf16[704,128]{1,0:T(8,128)(2,1)S(1)}, u32[]{:S(2)}, u32[]{:S(2)}) collective-permute-start(bf16[704,128]{1,0:T(8,128)(2,1)S(1)} %shard_map.53.refs_0_), channel_id=1, source_target_pairs={{0,1},{1,0},{2,3},{3,2},{4,5},{5,4},{6,7},{7,6},{8,9},{9,8},{10,11... | collective-permute-start | bytes 540680 | tf_op jit(solution)/shard_map/ppermute | solution.py:193
  43.5 4.2 %collective-permute-start.16 = (bf16[320,128]{1,0:T(8,128)(2,1)S(1)}, bf16[320,128]{1,0:T(8,128)(2,1)S(1)}, u32[]{:S(2)}, u32[]{:S(2)}) collective-permute-start(bf16[320,128]{1,0:T(8,128)(2,1)S(1)} %shard_map.60.refs_0_), channel_id=1, source_target_pairs={{0,2},{1,3},{2,0},{3,1},{4,6},{5,7},{6,4},{7,5},{8,10},{9,11},{10,... | collective-permute-start | bytes 245768 | tf_op jit(solution)/shard_map/ppermute | solution.py:193
  45.0 3.6 %collective-permute-start.9 = (bf16[480,128]{1,0:T(8,128)(2,1)S(1)}, bf16[480,128]{1,0:T(8,128)(2,1)S(1)}, u32[]{:S(2)}, u32[]{:S(2)}) collective-permute-start(bf16[480,128]{1,0:T(8,128)(2,1)S(1)} %shard_map.56.refs_2_), channel_id=1, source_target_pairs={{0,1},{1,0},{2,3},{3,2},{4,5},{5,4},{6,7},{7,6},{8,9},{9,8},{10,11... | collective-permute-start | bytes 368648 | tf_op jit(solution)/shard_map/ppermute | solution.py:193
  45.8 2.8 %collective-permute-start.11 = (bf16[480,128]{1,0:T(8,128)(2,1)S(1)}, bf16[480,128]{1,0:T(8,128)(2,1)S(1)}, u32[]{:S(2)}, u32[]{:S(2)}) collective-permute-start(bf16[480,128]{1,0:T(8,128)(2,1)S(1)} %collective-permute-done.10.refs_4_), channel_id=1, source_target_pairs={{0,1},{1,0},{2,3},{3,2},{4,5},{5,4},{6,7},{7,6},{8,9},{9,8},{10,11... | collective-permute-start | bytes 368648 | tf_op jit(solution)/shard_map/ppermute | solution.py:193
  47.0 2.9 %collective-permute-start.15 = (bf16[320,128]{1,0:T(8,128)(2,1)S(1)}, bf16[320,128]{1,0:T(8,128)(2,1)S(1)}, u32[]{:S(2)}, u32[]{:S(2)}) collective-permute-start(bf16[320,128]{1,0:T(8,128)(2,1)S(1)} %shard_map.60.refs_0_), channel_id=1, source_target_pairs={{0,1},{1,0},{2,3},{3,2},{4,5},{5,4},{6,7},{7,6},{8,9},{9,8},{10,11... | collective-permute-start | bytes 245768 | tf_op jit(solution)/shard_map/ppermute | solution.py:193
  47.7 2.1 %collective-permute-start.17 = (bf16[320,128]{1,0:T(8,128)(2,1)S(1)}, bf16[320,128]{1,0:T(8,128)(2,1)S(1)}, u32[]{:S(2)}, u32[]{:S(2)}) collective-permute-start(bf16[320,128]{1,0:T(8,128)(2,1)S(1)} %collective-permute-done.16.refs_2_), channel_id=1, source_target_pairs={{0,1},{1,0},{2,3},{3,2},{4,5},{5,4},{6,7},{7,6},{8,9},{9,8},{10,11... | collective-permute-start | bytes 245768 | tf_op jit(solution)/shard_map/ppermute | solution.py:193

commit v4 on v3

--- a/solution.py
+++ b/solution.py
@@ -64,23 +64,59 @@
     return [(k, c) for j in panels for c in (2 * j, 2 * j + 1) for k in range(c + 1)]
 
 
-def lift_kernel(experts, where, tokens, routes_t, out, turned):
-    toks, width = tokens.shape
-    turned[...] = tokens[...].T
-    numbers = lax.broadcasted_iota(jnp.int32, (16, toks), 0) ^ where[0]
-    named = numbers == routes_t[0:1, :]
-    for k in range(1, routes_t.shape[0]):
-        named = named | (numbers == routes_t[k : k + 1, :])
-    flags = named.astype(jnp.float32).astype(jnp.bfloat16)
+def flags_of(z, routes):
+    numbers = jnp.arange(16, dtype=jnp.int32) ^ z
+    return jnp.any(numbers[:, None, None] == routes.T[None], axis=1).astype(jnp.bfloat16)
+
+
+def lift(where, experts, turned, flags, out, lanes):
     row = 64 * where[2]
     ats = (row + PIECE * where[1], row + PIECE * (1 - where[1]))
     first = 0
-    for k in range(width // BLK):
+    for k in range(turned.shape[0] // BLK):
         for at in ats:
-            rows = turned[pl.ds(pl.multiple_of(at + BLK * k, PIECE), PIECE), :]
+            rows = turned[pl.ds(pl.multiple_of(at + BLK * k, PIECE), PIECE), lanes]
             for e in range(experts):
-                out[first : first + PIECE, :] = rows * flags[e : e + 1, :]
+                out[first : first + PIECE, lanes] = rows * flags[e : e + 1, lanes]
                 first += PIECE
+
+
+def own_kernel(panel, experts, where, tok, flags, lhs, part, turned):
+    for i in range(tok.shape[0] // BLK):
+        lanes = slice(BLK * i, BLK * (i + 1))
+        turned[:, lanes] = tok[lanes, :].T
+        lift(where, experts, turned, flags, lhs, lanes)
+    part[...] = jnp.dot(lhs[0 : part.shape[0], :], tok[:, 256 * panel : 256 * panel + 256],
+                        preferred_element_type=jnp.float32)
+
+
+def pack(total, j, base, mode, experts, halves, keep, send):
+    group = 2 * experts * PIECE
+    for side in range(2):
+        for k in range(2 * j + side + 1):
+            for s in range(2):
+                for e in range(experts):
+                    first = group * k + experts * PIECE * s + PIECE * e
+                    value = total[first : first + PIECE, BLK * side : BLK * (side + 1)]
+                    if mode == "z":
+                        out = keep if e % 2 == 0 else send
+                        at = pl.multiple_of(halves[s] + base, PIECE)
+                        out[e // 2, pl.ds(at, PIECE), :] = value.astype(out.dtype)
+                    else:
+                        out = (keep, send)[s]
+                        out[e, base : base + PIECE, :] = value.astype(out.dtype)
+            base += 2 * PIECE if mode == "z" else PIECE
+    return base
+
+
+def first_kernel(panel, experts, where, tok_b, flags, part, keep, send, lhs_b, turned):
+    for i in range(tok_b.shape[0] // BLK):
+        lanes = slice(BLK * i, BLK * (i + 1))
+        turned[:, lanes] = tok_b[lanes, :].T
+        lift(where, experts, turned, flags, lhs_b, lanes)
+    total = part[...] + jnp.dot(lhs_b[0 : part.shape[0], :], tok_b[:, 256 * panel : 256 * panel + 256],
+                                preferred_element_type=jnp.float32)
+    pack(total, panel, 0, "x", experts, None, keep, send)
 
 
 def gram_kernel(panels, mode, experts, where, lhs_a, tok_a, lhs_b, tok_b, keep, send):
@@ -91,20 +127,7 @@
         used, cols = slice(0, group * (2 * j + 2)), slice(256 * j, 256 * j + 256)
         total = jnp.dot(lhs_a[used, :], tok_a[:, cols], preferred_element_type=jnp.float32)
         total = total + jnp.dot(lhs_b[used, :], tok_b[:, cols], preferred_element_type=jnp.float32)
-        for side in range(2):
-            for k in range(2 * j + side + 1):
-                for s in range(2):
-                    for e in range(experts):
-                        first = group * k + experts * PIECE * s + PIECE * e
-                        value = total[first : first + PIECE, BLK * side : BLK * (side + 1)]
-                        if mode == "z":
-                            out = keep if e % 2 == 0 else send
-                            at = pl.multiple_of(halves[s] + base, PIECE)
-                            out[e // 2, pl.ds(at, PIECE), :] = value.astype(out.dtype)
-                        else:
-                            out = (keep, send)[s]
-                            out[e, base : base + PIECE, :] = value.astype(out.dtype)
-                base += 2 * PIECE if mode == "z" else PIECE
+        base = pack(total, j, base, mode, experts, halves, keep, send)
 
 
 def pair_kernel(keep, got, own, *outs):
@@ -201,13 +224,23 @@
     over_core, over_x = over("dp", 1), over("dp", 2)
     bf16, f32 = jnp.bfloat16, jnp.float32
 
-    def lift(tok, routes_t):
-        return call(functools.partial(lift_kernel, experts), [((2 * width, toks), bf16)],
-                    where, tok, routes_t, scratch=[pltpu.VMEM((width, toks), bf16)])[0]
-
-    other, other_routes = over_core(tokens), over_core(routes.T)
-    lhs = lift(tokens, routes.T)
-    other_lhs = lift(other, other_routes)
+    over_z = [over("expert", bit) for bit in range(4)]
+    chunk_a, chunk_z, chunk_b = plan
+    panel, = chunk_a
+    lifted, turned = ((2 * width, toks), bf16), pltpu.VMEM((width, toks), bf16)
+    dims = (experts, PIECE * count(chunk_a), BLK)
+    flags = flags_of(z, routes)
+    other, other_flags = over_core(tokens), over_core(flags)
+    lhs, part = call(
+        functools.partial(own_kernel, panel, experts),
+        [lifted, ((4 * experts * PIECE * (panel + 1), 256), f32)],
+        where, tokens, flags, scratch=[turned])
+    keep_a, send_a, other_lhs = call(
+        functools.partial(first_kernel, panel, experts), [(dims, f32), (dims, bf16), lifted],
+        where, other, other_flags, part, scratch=[turned])
+    got_a = over_x(send_a)
+
+
     def gram(panels, mode, at):
         blocks = count(panels)
         dims = (2, 2 * PIECE * blocks, BLK) if mode == "z" else (experts, PIECE * blocks, BLK)
@@ -220,10 +253,6 @@
     def summed(*parts):
         return call(sum_kernel, [(parts[0].shape, bf16)], *parts, smem=False)[0]
 
-    over_z = [over("expert", bit) for bit in range(4)]
-    chunk_a, chunk_z, chunk_b = plan
-    keep_a, send_a = gram(chunk_a, "x", where)
-    got_a = over_x(send_a)
     keep_z, send_z = gram(chunk_z, "z", after(where, send_a))
     near_z = over_z[1](send_z)
     keep_b, send_b = gram(chunk_b, "x", after(where, send_z))
@@ -250,9 +279,10 @@
     x_a = over_x(final_a)
     x_b = over_x(final_b)
     shape = ((chunk_z, 2 * PIECE, 2), (chunk_a, PIECE, 4), (chunk_b, PIECE, 4))
-    gram_early, square = call(functools.partial(early_kernel, shape[:2]),
-                        [((width, width), bf16), ((PIECE, BLK), f32)],
-                        where, both_z, over_core(both_z), final_a, over_core(final_a), x_a, over_core(x_a))
+    outs = [((width, width), bf16), ((PIECE, BLK), f32)]
+    of_z = [both_z, over_core(both_z)]
+    of_a = [final_a, over_core(final_a), x_a, over_core(x_a)]
+    gram_early, square = call(functools.partial(early_kernel, shape[:2]), outs, where, *of_z, *of_a)
     last = [final_b, over_core(final_b), x_b, over_core(x_b)]
     out, _ = call(functools.partial(steps_kernel, shape[2:]),
                   [(w_orig.shape[1:], f32), ((width, width), bf16)],

time: 53.6 us -> 53.2 us (level)
  local copies, waits for them, and re-layouts: 2.12 us -> 1.24 us
  other arithmetic: 0.08 us -> 0.85 us
    unnamed x10 -> x8, local copies, waits for them, and re-layouts: 2.12 us -> 1.24 us
    reduce_or x0 -> x1, other arithmetic: none -> 0.76 us  [flags_of(): jnp.any(numbers[:, None, None] == routes.T[None], axis=1)]
    pallas_call x16 -> x15, Pallas kernels: 12 us -> 11.6 us  [call(): pl.pallas_call(kernel, in_specs=[SMEM if smem and i == 0 else VMEM for i...]
  transfers between devices with their start and end apart: 18 -> 18, of which waited for: 4 -> 5; matrix products, arithmetic and copies ran while one was open for 0% -> 2% of each run, Pallas kernels for 11% -> 12%
where the time goes in v4:
time: 53.2 us; the launch traced here: 53 us
  starting transfers between devices  26 us (49%)
  waiting for transfers between devices  13.1 us (25%)
  Pallas kernels  11.6 us (22%)
  local copies, waits for them, and re-layouts  1.24 us (2%)
  other arithmetic  0.85 us (2%)
    ppermute x18, starting transfers between devices, over(): return lambda a: lax.ppermute(a, axis, [(i, i ^ bit) for i in range(4)])  26 us
    ppermute x18, waiting for transfers between devices, over(): return lambda a: lax.ppermute(a, axis, [(i, i ^ bit) for i in range(4)])  13.1 us
    pallas_call x15, Pallas kernels, call(): pl.pallas_call(kernel, in_specs=[SMEM if smem and i == 0 else VMEM for i...  11.6 us
    unnamed x8, local copies, waits for them, and re-layouts  1.24 us
  transfers between devices with their start and end apart: 18, of which 5 were waited for; matrix products, arithmetic and copies ran while one was open for 2% of the time, Pallas kernels for 12%

profile of v4, /device:TPU:1, one launch (start us, length us, event | category | flops | bytes accessed | tf_op | source)
XLA Modules:
  0.0 53.0 jit_solution(4307273995152893206)
XLA Ops:
  0.0 0.1 collective-permute-start
  0.1 0.8 %compare_reduce_fusion = pred[16,512]{1,0:T(8,128)(4,1)S(1)} fusion(s32[2,512]{1,0:T(2,128)} %bitcast.9, s32[16]{0:T(128)S(1)} %iota_xor_fusion), kind=kLoop, calls=%fused_computation | loop fusion | flops 24576 | bytes 12352 | tf_op jit(solution)/shard_map/reduce_or | solution.py:69
  0.8 0.5 collective-permute-start.1
  1.4 0.1 pad_add_fusion.where
  1.4 0.0 copy-start
  1.4 1.2 %copy-done = bf16[512,1024]{1,0:T(8,128)(2,1)S(1)} copy-done((bf16[512,1024]{1,0:T(8,128)(2,1)S(1)}, bf16[512,1024]{1,0:T(8,128)(2,1)}, u32[]{:S(2)}) %copy-start) | copy-done | bytes 1048600
  2.7 0.0 copy-start.1
  2.7 1.7 %shard_map.46 = (bf16[2048,512]{1,0:T(8,128)(2,1)S(1)}, f32[2048,256]{1,0:T(8,128)S(1)}) custom-call(s32[3]{0:T(128)S(1)} %pad_add_fusion.where, bf16[512,1024]{1,0:T(8,128)(2,1)S(1)} %copy-done, bf16[16,512]{1,0:T(8,128)(2,1)S(1)} %convert_element_type.3.flags), custom_call_target="tpu_custom_call" | custom-call | tf_op jit(solution)/shard_map/pallas_call | solution.py:206
  4.4 0.0 collective-permute-done.1.flags
  4.4 0.0 collective-permute-done.tok_b
  4.4 1.7 %shard_map.47 = (f32[4,480,128]{2,1,0:T(8,128)S(1)}, bf16[4,480,128]{2,1,0:T(8,128)(2,1)S(1)}, bf16[2048,512]{1,0:T(8,128)(2,1)S(1)}) custom-call(s32[3]{0:T(128)S(1)} %pad_add_fusion.where, bf16[512,1024]{1,0:T(8,128)(2,1)S(1)} %collective-permute-done.tok_b, bf16[16,512]{1,0:T(8,128)(2,1)S(1)} %collective-permute-done.1.flags, ...), custom_call_target="tpu_custom_call" | custom-call | tf_op jit(solution)/shard_map/pallas_call | solution.py:206
  6.1 2.3 %collective-permute-start.6 = (bf16[4,480,128]{2,1,0:T(8,128)(2,1)S(1)}, bf16[4,480,128]{2,1,0:T(8,128)(2,1)S(1)}, u32[]{:S(2)}, u32[]{:S(2)}) collective-permute-start(bf16[4,480,128]{2,1,0:T(8,128)(2,1)S(1)} %get-tuple-element.32), channel_id=1, source_target_pairs={{0,2},{1,3},{2,0},{3,1},{4,6},{5,7},{6,4},{7,5},{8,10},{9,11},{10,... | collective-permute-start | bytes 1474568 | tf_op jit(solution)/shard_map/ppermute | solution.py:216
  8.5 0.0 copy-done.1
  8.5 1.5 %shard_map.48 = (f32[2,704,128]{2,1,0:T(8,128)S(1)}, bf16[2,704,128]{2,1,0:T(8,128)(2,1)S(1)}) custom-call(s32[3]{0:T(128)S(1)} %pad_add_fusion.where, bf16[2048,512]{1,0:T(8,128)(2,1)S(1)} %get-tuple-element.34.lhs_a, bf16[512,1024]{1,0:T(8,128)(2,1)S(1)} %copy-done.1, bf16[2048,512]{1,0:T(8,128)(2,1)S(1)} %get-tuple-element.35.lhs_b, ...), custom_call_target="tpu_custom_call" | custom-call | tf_op jit(solution)/shard_map/pallas_call | solution.py:206
  10.0 1.4 %collective-permute-start.2 = (bf16[2,704,128]{2,1,0:T(8,128)(2,1)S(1)}, bf16[2,704,128]{2,1,0:T(8,128)(2,1)S(1)}, u32[]{:S(2)}, u32[]{:S(2)}) collective-permute-start(bf16[2,704,128]{2,1,0:T(8,128)(2,1)S(1)} %get-tuple-element.37), channel_id=1, source_target_pairs={{0,4},{4,0},{8,12},{12,8},{1,5},{5,1},{9,13},{13,9},{2,6},{6,2},{1... | collective-permute-start | bytes 1081352 | tf_op jit(solution)/shard_map/ppermute | solution.py:216
  11.4 1.5 %shard_map.49 = (f32[4,320,128]{2,1,0:T(8,128)S(1)}, bf16[4,320,128]{2,1,0:T(8,128)(2,1)S(1)}) custom-call(s32[3]{0:T(128)S(1)} %pad_add_fusion.where, bf16[2048,512]{1,0:T(8,128)(2,1)S(1)} %get-tuple-element.34.lhs_a, bf16[512,1024]{1,0:T(8,128)(2,1)S(1)} %copy-done.1, bf16[2048,512]{1,0:T(8,128)(2,1)S(1)} %get-tuple-element.35.lhs_b, ...), custom_call_target="tpu_custom_call" | custom-call | tf_op jit(solution)/shard_map/pallas_call | solution.py:206
  12.9 0.3 collective-permute-start.12
  13.2 6.4 %collective-permute-done.6.got = bf16[4,480,128]{2,1,0:T(8,128)(2,1)S(1)} collective-permute-done((bf16[4,480,128]{2,1,0:T(8,128)(2,1)S(1)}, bf16[4,480,128]{2,1,0:T(8,128)(2,1)S(1)}, u32[]{:S(2)}, u32[]{:S(2)}) %collective-permute-start.6) | collective-permute-done | bytes 491552 | tf_op jit(solution)/shard_map/ppermute | solution.py:216
  19.6 0.1 shard_map.53
  19.7 1.3 %collective-permute-start.7 = (bf16[2,480,128]{2,1,0:T(8,128)(2,1)S(1)}, bf16[2,480,128]{2,1,0:T(8,128)(2,1)S(1)}, u32[]{:S(2)}, u32[]{:S(2)}) collective-permute-start(bf16[2,480,128]{2,1,0:T(8,128)(2,1)S(1)} %get-tuple-element.46), channel_id=1, source_target_pairs={{0,4},{4,0},{8,12},{12,8},{1,5},{5,1},{9,13},{13,9},{2,6},{6,2},{1... | collective-permute-start | bytes 737288 | tf_op jit(solution)/shard_map/ppermute | solution.py:216
  21.0 0.0 collective-permute-done.2.got
  21.0 0.1 shard_map.50
  21.1 2.4 %collective-permute-start.3 = (bf16[704,128]{1,0:T(8,128)(2,1)S(1)}, bf16[704,128]{1,0:T(8,128)(2,1)S(1)}, u32[]{:S(2)}, u32[]{:S(2)}) collective-permute-start(bf16[704,128]{1,0:T(8,128)(2,1)S(1)} %get-tuple-element.42), channel_id=1, source_target_pairs={{0,8},{4,12},{8,0},{12,4},{1,9},{5,13},{9,1},{13,5},{2,10},{6,14},... | collective-permute-start | bytes 540680 | tf_op jit(solution)/shard_map/ppermute | solution.py:216
  23.5 3.2 %collective-permute-done.12.got = bf16[4,320,128]{2,1,0:T(8,128)(2,1)S(1)} collective-permute-done((bf16[4,320,128]{2,1,0:T(8,128)(2,1)S(1)}, bf16[4,320,128]{2,1,0:T(8,128)(2,1)S(1)}, u32[]{:S(2)}, u32[]{:S(2)}) %collective-permute-start.12) | collective-permute-done | bytes 327712 | tf_op jit(solution)/shard_map/ppermute | solution.py:216
  26.6 0.1 shard_map.57
  26.7 0.0 copy-start.2
  26.7 0.0 copy-start.3
  26.7 1.3 %collective-permute-start.13 = (bf16[2,320,128]{2,1,0:T(8,128)(2,1)S(1)}, bf16[2,320,128]{2,1,0:T(8,128)(2,1)S(1)}, u32[]{:S(2)}, u32[]{:S(2)}) collective-permute-start(bf16[2,320,128]{2,1,0:T(8,128)(2,1)S(1)} %get-tuple-element.53), channel_id=1, source_target_pairs={{0,4},{4,0},{8,12},{12,8},{1,5},{5,1},{9,13},{13,9},{2,6},{6,2},{1... | collective-permute-start | bytes 491528 | tf_op jit(solution)/shard_map/ppermute | solution.py:216
  28.0 0.0 collective-permute-done.7.got
  28.1 3.4 %collective-permute-start.8 = (bf16[480,128]{1,0:T(8,128)(2,1)S(1)}, bf16[480,128]{1,0:T(8,128)(2,1)S(1)}, u32[]{:S(2)}, u32[]{:S(2)}) collective-permute-start(bf16[480,128]{1,0:T(8,128)(2,1)S(1)} %get-tuple-element.48), channel_id=1, source_target_pairs={{0,8},{4,12},{8,0},{12,4},{1,9},{5,13},{9,1},{13,5},{2,10},{6,14},... | collective-permute-start | bytes 368648 | tf_op jit(solution)/shard_map/ppermute | solution.py:216
  31.4 0.0 collective-permute-done.3.refs_1_
  31.5 1.3 %collective-permute-start.4 = (bf16[704,128]{1,0:T(8,128)(2,1)S(1)}, bf16[704,128]{1,0:T(8,128)(2,1)S(1)}, u32[]{:S(2)}, u32[]{:S(2)}) collective-permute-start(bf16[704,128]{1,0:T(8,128)(2,1)S(1)} %shard_map.51.refs_0_), channel_id=1, source_target_pairs={{0,2},{1,3},{2,0},{3,1},{4,6},{5,7},{6,4},{7,5},{8,10},{9,11},{10,... | collective-permute-start | bytes 540680 | tf_op jit(solution)/shard_map/ppermute | solution.py:216
  32.8 2.6 %collective-permute-done.13.got = bf16[2,320,128]{2,1,0:T(8,128)(2,1)S(1)} collective-permute-done((bf16[2,320,128]{2,1,0:T(8,128)(2,1)S(1)}, bf16[2,320,128]{2,1,0:T(8,128)(2,1)S(1)}, u32[]{:S(2)}, u32[]{:S(2)}) %collective-permute-start.13) | collective-permute-done | bytes 163872 | tf_op jit(solution)/shard_map/ppermute | solution.py:216
  35.4 0.1 collective-permute-start.14
  35.5 0.1 collective-permute-done.8.refs_1_
  35.7 1.3 %collective-permute-start.10 = (bf16[480,128]{1,0:T(8,128)(2,1)S(1)}, bf16[480,128]{1,0:T(8,128)(2,1)S(1)}, u32[]{:S(2)}, u32[]{:S(2)}) collective-permute-start(bf16[480,128]{1,0:T(8,128)(2,1)S(1)} %shard_map.55.refs_2_), channel_id=1, source_target_pairs={{0,2},{1,3},{2,0},{3,1},{4,6},{5,7},{6,4},{7,5},{8,10},{9,11},{10,... | collective-permute-start | bytes 368648 | tf_op jit(solution)/shard_map/ppermute | solution.py:216
  37.0 0.0 collective-permute-done.4.refs_1_
  37.0 6.1 %collective-permute-start.5 = (bf16[704,128]{1,0:T(8,128)(2,1)S(1)}, bf16[704,128]{1,0:T(8,128)(2,1)S(1)}, u32[]{:S(2)}, u32[]{:S(2)}) collective-permute-start(bf16[704,128]{1,0:T(8,128)(2,1)S(1)} %shard_map.52.refs_0_), channel_id=1, source_target_pairs={{0,1},{1,0},{2,3},{3,2},{4,5},{5,4},{6,7},{7,6},{8,9},{9,8},{10,11... | collective-permute-start | bytes 540680 | tf_op jit(solution)/shard_map/ppermute | solution.py:216
  43.1 0.0 collective-permute-done.14.refs_1_
  43.2 1.5 %collective-permute-start.16 = (bf16[320,128]{1,0:T(8,128)(2,1)S(1)}, bf16[320,128]{1,0:T(8,128)(2,1)S(1)}, u32[]{:S(2)}, u32[]{:S(2)}) collective-permute-start(bf16[320,128]{1,0:T(8,128)(2,1)S(1)} %shard_map.59.refs_0_), channel_id=1, source_target_pairs={{0,2},{1,3},{2,0},{3,1},{4,6},{5,7},{6,4},{7,5},{8,10},{9,11},{10,... | collective-permute-start | bytes 245768 | tf_op jit(solution)/shard_map/ppermute | solution.py:216
  44.7 0.8 %collective-permute-start.9 = (bf16[480,128]{1,0:T(8,128)(2,1)S(1)}, bf16[480,128]{1,0:T(8,128)(2,1)S(1)}, u32[]{:S(2)}, u32[]{:S(2)}) collective-permute-start(bf16[480,128]{1,0:T(8,128)(2,1)S(1)} %shard_map.55.refs_2_), channel_id=1, source_target_pairs={{0,1},{1,0},{2,3},{3,2},{4,5},{5,4},{6,7},{7,6},{8,9},{9,8},{10,11... | collective-permute-start | bytes 368648 | tf_op jit(solution)/shard_map/ppermute | solution.py:216
  45.5 0.0 collective-permute-done.10.refs_4_
  45.5 1.1 %collective-permute-start.11 = (bf16[480,128]{1,0:T(8,128)(2,1)S(1)}, bf16[480,128]{1,0:T(8,128)(2,1)S(1)}, u32[]{:S(2)}, u32[]{:S(2)}) collective-permute-start(bf16[480,128]{1,0:T(8,128)(2,1)S(1)} %collective-permute-done.10.refs_4_), channel_id=1, source_target_pairs={{0,1},{1,0},{2,3},{3,2},{4,5},{5,4},{6,7},{7,6},{8,9},{9,8},{10,11... | collective-permute-start | bytes 368648 | tf_op jit(solution)/shard_map/ppermute | solution.py:216
  46.6 0.0 collective-permute-start.15
  46.6 0.7 %collective-permute-done.16.refs_2_ = bf16[320,128]{1,0:T(8,128)(2,1)S(1)} collective-permute-done((bf16[320,128]{1,0:T(8,128)(2,1)S(1)}, bf16[320,128]{1,0:T(8,128)(2,1)S(1)}, u32[]{:S(2)}, u32[]{:S(2)}) %collective-permute-start.16) | collective-permute-done | bytes 81952 | tf_op jit(solution)/shard_map/ppermute | solution.py:216
  47.4 0.9 %collective-permute-start.17 = (bf16[320,128]{1,0:T(8,128)(2,1)S(1)}, bf16[320,128]{1,0:T(8,128)(2,1)S(1)}, u32[]{:S(2)}, u32[]{:S(2)}) collective-permute-start(bf16[320,128]{1,0:T(8,128)(2,1)S(1)} %collective-permute-done.16.refs_2_), channel_id=1, source_target_pairs={{0,1},{1,0},{2,3},{3,2},{4,5},{5,4},{6,7},{7,6},{8,9},{9,8},{10,11... | collective-permute-start | bytes 245768 | tf_op jit(solution)/shard_map/ppermute | solution.py:216
  48.3 0.0 collective-permute-done.5.refs_1_
  48.3 0.0 collective-permute-done.9.refs_3_
  48.3 0.0 collective-permute-done.11.refs_5_
  48.3 1.2 %shard_map.56 = (bf16[1024,1024]{1,0:T(8,128)(2,1)S(1)}, f32[32,128]{1,0:T(8,128)S(1)}) custom-call(s32[3]{0:T(128)S(1)} %pad_add_fusion.where, bf16[704,128]{1,0:T(8,128)(2,1)S(1)} %shard_map.52.refs_0_, bf16[704,128]{1,0:T(8,128)(2,1)S(1)} %collective-permute-done.5.refs_1_, bf16[480,128]{1,0:T(8,128)(2,1)S(1)} %shard_map.55.refs_2_, ...), custom_call_target="tpu_custom_call" | custom-call | tf_op jit(solution)/shard_map/pallas_call | solution.py:206
  49.5 0.0 collective-permute-done.15.refs_1_
  49.5 0.0 collective-permute-done.17.refs_3_
  49.5 0.0 copy-done.2
  49.5 0.0 copy-done.3
  49.5 3.4 %shard_map.60 = (f32[128,1024]{1,0:T(8,128)}, bf16[1024,1024]{1,0:T(8,128)(2,1)S(1)}) custom-call(s32[3]{0:T(128)S(1)} %pad_add_fusion.where, f32[128,1024]{1,0:T(8,128)S(1)} %bitcast.7, s32[128,1024]{1,0:T(8,128)S(1)} %bitcast.8, bf16[1024,1024]{1,0:T(8,128)(2,1)S(1)} %get-tuple-element.49.old, ...), custom_call_target="tpu_custom_call", output_to_operand_aliasing={{1}: (3, {})} | custom-call | tf_op jit(solution)/shard_map/pallas_call | solution.py:206
  (8 shorter events, 0.2 us)
Async XLA Ops:
  0.0 4.4 %collective-permute-start = (bf16[512,1024]{1,0:T(8,128)(2,1)}, bf16[512,1024]{1,0:T(8,128)(2,1)S(1)}, u32[]{:S(2)}, u32[]{:S(2)}) collective-permute-start(bf16[512,1024]{1,0:T(8,128)(2,1)} %tok_a.3), channel_id=1, source_target_pairs={{0,1},{1,0},{2,3},{3,2},{4,5},{5,4},{6,7},{7,6},{8,9},{9,8},{10,11... | collective-permute-start | bytes 3145736 | tf_op jit(solution)/shard_map/ppermute | solution.py:216
  0.8 3.5 %collective-permute-start.1 = (bf16[16,512]{1,0:T(8,128)(2,1)S(1)}, bf16[16,512]{1,0:T(8,128)(2,1)S(1)}, u32[]{:S(2)}, u32[]{:S(2)}) collective-permute-start(bf16[16,512]{1,0:T(8,128)(2,1)S(1)} %convert_element_type.3.flags), channel_id=1, source_target_pairs={{0,1},{1,0},{2,3},{3,2},{4,5},{5,4},{6,7},{7,6},{8,9},{9,8},{10,11... | collective-permute-start | bytes 49160 | tf_op jit(solution)/shard_map/ppermute | solution.py:216
  1.4 1.2 %copy-start = (bf16[512,1024]{1,0:T(8,128)(2,1)S(1)}, bf16[512,1024]{1,0:T(8,128)(2,1)}, u32[]{:S(2)}) copy-start(bf16[512,1024]{1,0:T(8,128)(2,1)} %tok_a.3) | copy-start | bytes 3145732
  2.7 5.8 %copy-start.1 = (bf16[512,1024]{1,0:T(8,128)(2,1)S(1)}, bf16[512,1024]{1,0:T(8,128)(2,1)}, u32[]{:S(2)}) copy-start(bf16[512,1024]{1,0:T(8,128)(2,1)} %tok_a.3) | copy-start | bytes 3145732
  6.1 13.5 %collective-permute-start.6 = (bf16[4,480,128]{2,1,0:T(8,128)(2,1)S(1)}, bf16[4,480,128]{2,1,0:T(8,128)(2,1)S(1)}, u32[]{:S(2)}, u32[]{:S(2)}) collective-permute-start(bf16[4,480,128]{2,1,0:T(8,128)(2,1)S(1)} %get-tuple-element.32), channel_id=1, source_target_pairs={{0,2},{1,3},{2,0},{3,1},{4,6},{5,7},{6,4},{7,5},{8,10},{9,11},{10,... | collective-permute-start | bytes 1474568 | tf_op jit(solution)/shard_map/ppermute | solution.py:216
  10.0 11.0 %collective-permute-start.2 = (bf16[2,704,128]{2,1,0:T(8,128)(2,1)S(1)}, bf16[2,704,128]{2,1,0:T(8,128)(2,1)S(1)}, u32[]{:S(2)}, u32[]{:S(2)}) collective-permute-start(bf16[2,704,128]{2,1,0:T(8,128)(2,1)S(1)} %get-tuple-element.37), channel_id=1, source_target_pairs={{0,4},{4,0},{8,12},{12,8},{1,5},{5,1},{9,13},{13,9},{2,6},{6,2},{1... | collective-permute-start | bytes 1081352 | tf_op jit(solution)/shard_map/ppermute | solution.py:216
  12.9 13.7 %collective-permute-start.12 = (bf16[4,320,128]{2,1,0:T(8,128)(2,1)S(1)}, bf16[4,320,128]{2,1,0:T(8,128)(2,1)S(1)}, u32[]{:S(2)}, u32[]{:S(2)}) collective-permute-start(bf16[4,320,128]{2,1,0:T(8,128)(2,1)S(1)} %get-tuple-element.39), channel_id=1, source_target_pairs={{0,2},{1,3},{2,0},{3,1},{4,6},{5,7},{6,4},{7,5},{8,10},{9,11},{10,... | collective-permute-start | bytes 983048 | tf_op jit(solution)/shard_map/ppermute | solution.py:216
  19.7 8.3 %collective-permute-start.7 = (bf16[2,480,128]{2,1,0:T(8,128)(2,1)S(1)}, bf16[2,480,128]{2,1,0:T(8,128)(2,1)S(1)}, u32[]{:S(2)}, u32[]{:S(2)}) collective-permute-start(bf16[2,480,128]{2,1,0:T(8,128)(2,1)S(1)} %get-tuple-element.46), channel_id=1, source_target_pairs={{0,4},{4,0},{8,12},{12,8},{1,5},{5,1},{9,13},{13,9},{2,6},{6,2},{1... | collective-permute-start | bytes 737288 | tf_op jit(solution)/shard_map/ppermute | solution.py:216
  21.1 10.3 %collective-permute-start.3 = (bf16[704,128]{1,0:T(8,128)(2,1)S(1)}, bf16[704,128]{1,0:T(8,128)(2,1)S(1)}, u32[]{:S(2)}, u32[]{:S(2)}) collective-permute-start(bf16[704,128]{1,0:T(8,128)(2,1)S(1)} %get-tuple-element.42), channel_id=1, source_target_pairs={{0,8},{4,12},{8,0},{12,4},{1,9},{5,13},{9,1},{13,5},{2,10},{6,14},... | collective-permute-start | bytes 540680 | tf_op jit(solution)/shard_map/ppermute | solution.py:216
  26.7 22.8 %copy-start.2 = (f32[1,128,1024]{2,1,0:T(8,128)S(1)}, f32[1,128,1024]{2,1,0:T(8,128)}, u32[]{:S(2)}) copy-start(f32[1,128,1024]{2,1,0:T(8,128)} %param.6) | copy-start | bytes 1572868
  26.7 22.8 %copy-start.3 = (s32[1,128,1024]{2,1,0:T(8,128)S(1)}, s32[1,128,1024]{2,1,0:T(8,128)}, u32[]{:S(2)}) copy-start(s32[1,128,1024]{2,1,0:T(8,128)} %param.7) | copy-start | bytes 1572868
  26.7 8.7 %collective-permute-start.13 = (bf16[2,320,128]{2,1,0:T(8,128)(2,1)S(1)}, bf16[2,320,128]{2,1,0:T(8,128)(2,1)S(1)}, u32[]{:S(2)}, u32[]{:S(2)}) collective-permute-start(bf16[2,320,128]{2,1,0:T(8,128)(2,1)S(1)} %get-tuple-element.53), channel_id=1, source_target_pairs={{0,4},{4,0},{8,12},{12,8},{1,5},{5,1},{9,13},{13,9},{2,6},{6,2},{1... | collective-permute-start | bytes 491528 | tf_op jit(solution)/shard_map/ppermute | solution.py:216
  28.1 7.6 %collective-permute-start.8 = (bf16[480,128]{1,0:T(8,128)(2,1)S(1)}, bf16[480,128]{1,0:T(8,128)(2,1)S(1)}, u32[]{:S(2)}, u32[]{:S(2)}) collective-permute-start(bf16[480,128]{1,0:T(8,128)(2,1)S(1)} %get-tuple-element.48), channel_id=1, source_target_pairs={{0,8},{4,12},{8,0},{12,4},{1,9},{5,13},{9,1},{13,5},{2,10},{6,14},... | collective-permute-start | bytes 368648 | tf_op jit(solution)/shard_map/ppermute | solution.py:216
  31.5 5.5 %collective-permute-start.4 = (bf16[704,128]{1,0:T(8,128)(2,1)S(1)}, bf16[704,128]{1,0:T(8,128)(2,1)S(1)}, u32[]{:S(2)}, u32[]{:S(2)}) collective-permute-start(bf16[704,128]{1,0:T(8,128)(2,1)S(1)} %shard_map.51.refs_0_), channel_id=1, source_target_pairs={{0,2},{1,3},{2,0},{3,1},{4,6},{5,7},{6,4},{7,5},{8,10},{9,11},{10,... | collective-permute-start | bytes 540680 | tf_op jit(solution)/shard_map/ppermute | solution.py:216
  35.4 7.7 %collective-permute-start.14 = (bf16[320,128]{1,0:T(8,128)(2,1)S(1)}, bf16[320,128]{1,0:T(8,128)(2,1)S(1)}, u32[]{:S(2)}, u32[]{:S(2)}) collective-permute-start(bf16[320,128]{1,0:T(8,128)(2,1)S(1)} %get-tuple-element.55), channel_id=1, source_target_pairs={{0,8},{4,12},{8,0},{12,4},{1,9},{5,13},{9,1},{13,5},{2,10},{6,14},... | collective-permute-start | bytes 245768 | tf_op jit(solution)/shard_map/ppermute | solution.py:216
  35.7 9.8 %collective-permute-start.10 = (bf16[480,128]{1,0:T(8,128)(2,1)S(1)}, bf16[480,128]{1,0:T(8,128)(2,1)S(1)}, u32[]{:S(2)}, u32[]{:S(2)}) collective-permute-start(bf16[480,128]{1,0:T(8,128)(2,1)S(1)} %shard_map.55.refs_2_), channel_id=1, source_target_pairs={{0,2},{1,3},{2,0},{3,1},{4,6},{5,7},{6,4},{7,5},{8,10},{9,11},{10,... | collective-permute-start | bytes 368648 | tf_op jit(solution)/shard_map/ppermute | solution.py:216
  37.0 11.3 %collective-permute-start.5 = (bf16[704,128]{1,0:T(8,128)(2,1)S(1)}, bf16[704,128]{1,0:T(8,128)(2,1)S(1)}, u32[]{:S(2)}, u32[]{:S(2)}) collective-permute-start(bf16[704,128]{1,0:T(8,128)(2,1)S(1)} %shard_map.52.refs_0_), channel_id=1, source_target_pairs={{0,1},{1,0},{2,3},{3,2},{4,5},{5,4},{6,7},{7,6},{8,9},{9,8},{10,11... | collective-permute-start | bytes 540680 | tf_op jit(solution)/shard_map/ppermute | solution.py:216
  43.2 4.2 %collective-permute-start.16 = (bf16[320,128]{1,0:T(8,128)(2,1)S(1)}, bf16[320,128]{1,0:T(8,128)(2,1)S(1)}, u32[]{:S(2)}, u32[]{:S(2)}) collective-permute-start(bf16[320,128]{1,0:T(8,128)(2,1)S(1)} %shard_map.59.refs_0_), channel_id=1, source_target_pairs={{0,2},{1,3},{2,0},{3,1},{4,6},{5,7},{6,4},{7,5},{8,10},{9,11},{10,... | collective-permute-start | bytes 245768 | tf_op jit(solution)/shard_map/ppermute | solution.py:216
  44.7 3.6 %collective-permute-start.9 = (bf16[480,128]{1,0:T(8,128)(2,1)S(1)}, bf16[480,128]{1,0:T(8,128)(2,1)S(1)}, u32[]{:S(2)}, u32[]{:S(2)}) collective-permute-start(bf16[480,128]{1,0:T(8,128)(2,1)S(1)} %shard_map.55.refs_2_), channel_id=1, source_target_pairs={{0,1},{1,0},{2,3},{3,2},{4,5},{5,4},{6,7},{7,6},{8,9},{9,8},{10,11... | collective-permute-start | bytes 368648 | tf_op jit(solution)/shard_map/ppermute | solution.py:216
  45.5 2.8 %collective-permute-start.11 = (bf16[480,128]{1,0:T(8,128)(2,1)S(1)}, bf16[480,128]{1,0:T(8,128)(2,1)S(1)}, u32[]{:S(2)}, u32[]{:S(2)}) collective-permute-start(bf16[480,128]{1,0:T(8,128)(2,1)S(1)} %collective-permute-done.10.refs_4_), channel_id=1, source_target_pairs={{0,1},{1,0},{2,3},{3,2},{4,5},{5,4},{6,7},{7,6},{8,9},{9,8},{10,11... | collective-permute-start | bytes 368648 | tf_op jit(solution)/shard_map/ppermute | solution.py:216
  46.6 2.9 %collective-permute-start.15 = (bf16[320,128]{1,0:T(8,128)(2,1)S(1)}, bf16[320,128]{1,0:T(8,128)(2,1)S(1)}, u32[]{:S(2)}, u32[]{:S(2)}) collective-permute-start(bf16[320,128]{1,0:T(8,128)(2,1)S(1)} %shard_map.59.refs_0_), channel_id=1, source_target_pairs={{0,1},{1,0},{2,3},{3,2},{4,5},{5,4},{6,7},{7,6},{8,9},{9,8},{10,11... | collective-permute-start | bytes 245768 | tf_op jit(solution)/shard_map/ppermute | solution.py:216
  47.4 2.2 %collective-permute-start.17 = (bf16[320,128]{1,0:T(8,128)(2,1)S(1)}, bf16[320,128]{1,0:T(8,128)(2,1)S(1)}, u32[]{:S(2)}, u32[]{:S(2)}) collective-permute-start(bf16[320,128]{1,0:T(8,128)(2,1)S(1)} %collective-permute-done.16.refs_2_), channel_id=1, source_target_pairs={{0,1},{1,0},{2,3},{3,2},{4,5},{5,4},{6,7},{7,6},{8,9},{9,8},{10,11... | collective-permute-start | bytes 245768 | tf_op jit(solution)/shard_map/ppermute | solution.py:216

commit v5 on v4

--- a/solution.py
+++ b/solution.py
@@ -56,12 +56,15 @@
     return weights[None]
 
 
-def count(panels):
-    return sum(4 * j + 3 for j in panels)
+EXTRA = 16
 
 
 def blocks_of(panels):
-    return [(k, c) for j in panels for c in (2 * j, 2 * j + 1) for k in range(c + 1)]
+    return [(k, c) for j in panels for c in (2 * j, 2 * j + 1) for k in range(2 * j + 1)]
+
+
+def rows_of(panels, size):
+    return size * len(blocks_of(panels)) + EXTRA + MORE.get((panels, size), 0)
 
 
 def flags_of(z, routes):
@@ -90,23 +93,42 @@
                         preferred_element_type=jnp.float32)
 
 
-def pack(total, j, base, mode, experts, halves, keep, send):
+def pack(totals, panels, mode, experts, where, keep, send):
     group = 2 * experts * PIECE
-    for side in range(2):
-        for k in range(2 * j + side + 1):
-            for s in range(2):
-                for e in range(experts):
-                    first = group * k + experts * PIECE * s + PIECE * e
-                    value = total[first : first + PIECE, BLK * side : BLK * (side + 1)]
-                    if mode == "z":
-                        out = keep if e % 2 == 0 else send
-                        at = pl.multiple_of(halves[s] + base, PIECE)
-                        out[e // 2, pl.ds(at, PIECE), :] = value.astype(out.dtype)
-                    else:
-                        out = (keep, send)[s]
-                        out[e, base : base + PIECE, :] = value.astype(out.dtype)
-            base += 2 * PIECE if mode == "z" else PIECE
-    return base
+    size = 2 * PIECE if mode == "z" else PIECE
+    halves = (PIECE * where[1], PIECE * (1 - where[1]))
+    col = lax.broadcasted_iota(jnp.int32, (PIECE, BLK), 1)
+    row = lax.broadcasted_iota(jnp.int32, (PIECE, BLK), 0) + 64 * where[2]
+    end = size * len(blocks_of(panels))
+    for e in range(experts):
+        lines = []
+        for s in range(2):
+            if mode == "z":
+                out, lead, shift = (keep, send)[e % 2], e // 2, halves[s]
+            else:
+                out, lead, shift = (keep, send)[s], e, 0
+            base, lines_s = 0, []
+            for total, j in zip(totals, panels):
+                for side in range(2):
+                    for k in range(2 * j + 1):
+                        first = group * k + experts * PIECE * s + PIECE * e
+                        value = total[first : first + PIECE, BLK * side : BLK * (side + 1)]
+                        if side == 0 and k == 2 * j:
+                            below = total[first + group : first + group + PIECE, BLK : 2 * BLK]
+                            at = row + halves[s]
+                            value = jnp.where(col >= at, value, below)
+                            lines_s.append(jnp.sum(jnp.where(col == at, below, 0.0), axis=0, keepdims=True))
+                        spot = pl.multiple_of(shift + base, PIECE) if mode == "z" else base
+                        out[lead, pl.ds(spot, PIECE), :] = value.astype(out.dtype)
+                        base += size
+            lines.append(lines_s)
+        if mode == "z":
+            slabs = [((keep, send)[e % 2], e // 2, [a + b for a, b in zip(*lines)])]
+        else:
+            slabs = [(keep, e, lines[0]), (send, e, lines[1])]
+        for out, lead, slab in slabs:
+            slab = slab + [jnp.zeros((out.shape[1] - end - len(slab), BLK), jnp.float32)]
+            out[lead, end:, :] = jnp.concatenate(slab, axis=0).astype(out.dtype)
 
 
 def first_kernel(panel, experts, where, tok_b, flags, part, keep, send, lhs_b, turned):
@@ -116,18 +138,17 @@
         lift(where, experts, turned, flags, lhs_b, lanes)
     total = part[...] + jnp.dot(lhs_b[0 : part.shape[0], :], tok_b[:, 256 * panel : 256 * panel + 256],
                                 preferred_element_type=jnp.float32)
-    pack(total, panel, 0, "x", experts, None, keep, send)
+    pack([total], (panel,), "x", experts, where, keep, send)
 
 
 def gram_kernel(panels, mode, experts, where, lhs_a, tok_a, lhs_b, tok_b, keep, send):
     group = 2 * experts * PIECE
-    halves = (PIECE * where[1], PIECE * (1 - where[1]))
-    base = 0
+    totals = []
     for j in panels:
         used, cols = slice(0, group * (2 * j + 2)), slice(256 * j, 256 * j + 256)
         total = jnp.dot(lhs_a[used, :], tok_a[:, cols], preferred_element_type=jnp.float32)
-        total = total + jnp.dot(lhs_b[used, :], tok_b[:, cols], preferred_element_type=jnp.float32)
-        base = pack(total, j, base, mode, experts, halves, keep, send)
+        totals.append(total + jnp.dot(lhs_b[used, :], tok_b[:, cols], preferred_element_type=jnp.float32))
+    pack(totals, panels, mode, experts, where, keep, send)
 
 
 def pair_kernel(keep, got, own, *outs):
@@ -156,19 +177,35 @@
     else:
         ats = [64 * a for a in (core, 1 - core)]
     square = jnp.zeros((PIECE, BLK), jnp.float32)
+    end = size * len(blocks_of(panels))
     for at, piece in zip(ats, pieces):
         base = 0
         for k, c in blocks_of(panels):
             gram[pl.ds(pl.multiple_of(at + BLK * k, PIECE), size), BLK * c : BLK * (c + 1)] = piece[
                 base : base + size, :]
             for part in range(0, size, PIECE):
-                value = piece[base + part : base + part + PIECE, :].astype(jnp.float32)
-                square = square + value * value * (1.0 if k == c else 2.0)
+                if k < c:
+                    value = piece[base + part : base + part + PIECE, :].astype(jnp.float32)
+                    square = square + 2.0 * value * value
             base += size
     for k, c in blocks_of(panels):
         if k < c:
             gram[BLK * c : BLK * (c + 1), BLK * k : BLK * (k + 1)] = gram[
                 BLK * k : BLK * (k + 1), BLK * c : BLK * (c + 1)].T
+    lines = sum(piece[end : end + EXTRA, :].astype(jnp.float32) for piece in pieces)
+    col = lax.broadcasted_iota(jnp.int32, (BLK, BLK), 1)
+    row = lax.broadcasted_iota(jnp.int32, (BLK, BLK), 0)
+    for i, j in enumerate(panels):
+        first, second = slice(256 * j, 256 * j + BLK), slice(256 * j + BLK, 256 * j + 256)
+        mixed = gram[first, first].astype(jnp.float32)
+        turned = mixed.T
+        upper = jnp.where(col >= row, mixed, turned)
+        lower = jnp.where(col < row, mixed, jnp.where(col > row, turned, lines[i : i + 1, :]))
+        gram[first, first] = upper.astype(gram.dtype)
+        gram[second, second] = lower.astype(gram.dtype)
+        both = upper * upper + lower * lower
+        for part in range(0, BLK, PIECE):
+            square = square + both[part : part + PIECE, :]
     return square
 
 
@@ -228,7 +265,7 @@
     chunk_a, chunk_z, chunk_b = plan
     panel, = chunk_a
     lifted, turned = ((2 * width, toks), bf16), pltpu.VMEM((width, toks), bf16)
-    dims = (experts, PIECE * count(chunk_a), BLK)
+    dims = (experts, rows_of(chunk_a, PIECE), BLK)
     flags = flags_of(z, routes)
     other, other_flags = over_core(tokens), over_core(flags)
     lhs, part = call(
@@ -242,13 +279,12 @@
 
 
     def gram(panels, mode, at):
-        blocks = count(panels)
-        dims = (2, 2 * PIECE * blocks, BLK) if mode == "z" else (experts, PIECE * blocks, BLK)
+        dims = (2 if mode == "z" else experts,) + flat(panels, mode)
         return call(functools.partial(gram_kernel, panels, mode, experts),
                     [(dims, f32), (dims, bf16)], at, lhs, tokens, other_lhs, other)
 
     def flat(panels, mode=""):
-        return ((2 if mode == "z" else 1) * PIECE * count(panels), BLK)
+        return (rows_of(panels, 2 * PIECE if mode == "z" else PIECE), BLK)
 
     def summed(*parts):
         return call(sum_kernel, [(parts[0].shape, bf16)], *parts, smem=False)[0]
@@ -294,6 +330,7 @@
     return lax.optimization_barrier((value, earlier))[0]
 
 
+MORE = {((0, 1), PIECE): 48}
 PLAN = ((3,), (2,), (0, 1))
 
 

time: 53.2 us -> 52.3 us (0.983)
  starting transfers between devices: 26 us -> 24.8 us
    ppermute x18, starting transfers between devices: 26 us -> 24.8 us  [over(): return lambda a: lax.ppermute(a, axis, [(i, i ^ bit) for i in range(4)])]
  transfers between devices with their start and end apart: 18 -> 18, of which waited for: 5 -> 4; matrix products, arithmetic and copies ran while one was open for 2% -> 2% of each run, Pallas kernels for 12% -> 12%
where the time goes in v5:
time: 52.3 us; the launch traced here: 52.1 us
  starting transfers between devices  24.8 us (47%)
  waiting for transfers between devices  13.4 us (26%)
  Pallas kernels  11.6 us (22%)
  local copies, waits for them, and re-layouts  1.24 us (2%)
  other arithmetic  0.85 us (2%)
    ppermute x18, starting transfers between devices, over(): return lambda a: lax.ppermute(a, axis, [(i, i ^ bit) for i in range(4)])  24.8 us
    ppermute x18, waiting for transfers between devices, over(): return lambda a: lax.ppermute(a, axis, [(i, i ^ bit) for i in range(4)])  13.4 us
    pallas_call x15, Pallas kernels, call(): pl.pallas_call(kernel, in_specs=[SMEM if smem and i == 0 else VMEM for i...  11.6 us
    unnamed x8, local copies, waits for them, and re-layouts  1.24 us
  transfers between devices with their start and end apart: 18, of which 4 were waited for; matrix products, arithmetic and copies ran while one was open for 2% of the time, Pallas kernels for 12%

profile of v5, /device:TPU:1, one launch (start us, length us, event | category | flops | bytes accessed | tf_op | source)
XLA Modules:
  0.0 52.1 jit_solution(8091973142493748082)
XLA Ops:
  0.0 0.1 collective-permute-start
  0.1 0.8 %compare_reduce_fusion = pred[16,512]{1,0:T(8,128)(4,1)S(1)} fusion(s32[2,512]{1,0:T(2,128)} %bitcast.9, s32[16]{0:T(128)S(1)} %iota_xor_fusion), kind=kLoop, calls=%fused_computation | loop fusion | flops 24576 | bytes 12352 | tf_op jit(solution)/shard_map/reduce_or | solution.py:72
  0.8 0.5 collective-permute-start.1
  1.4 0.1 pad_add_fusion.where
  1.4 0.0 copy-start
  1.4 1.2 %copy-done = bf16[512,1024]{1,0:T(8,128)(2,1)S(1)} copy-done((bf16[512,1024]{1,0:T(8,128)(2,1)S(1)}, bf16[512,1024]{1,0:T(8,128)(2,1)}, u32[]{:S(2)}) %copy-start) | copy-done | bytes 1048600
  2.7 0.0 copy-start.1
  2.7 1.7 %shard_map.46 = (bf16[2048,512]{1,0:T(8,128)(2,1)S(1)}, f32[2048,256]{1,0:T(8,128)S(1)}) custom-call(s32[3]{0:T(128)S(1)} %pad_add_fusion.where, bf16[512,1024]{1,0:T(8,128)(2,1)S(1)} %copy-done, bf16[16,512]{1,0:T(8,128)(2,1)S(1)} %convert_element_type.3.flags), custom_call_target="tpu_custom_call" | custom-call | tf_op jit(solution)/shard_map/pallas_call | solution.py:243
  4.4 0.0 collective-permute-done.1.flags
  4.4 0.0 collective-permute-done.tok_b
  4.4 1.7 %shard_map.47 = (f32[4,464,128]{2,1,0:T(8,128)S(1)}, bf16[4,464,128]{2,1,0:T(8,128)(2,1)S(1)}, bf16[2048,512]{1,0:T(8,128)(2,1)S(1)}) custom-call(s32[3]{0:T(128)S(1)} %pad_add_fusion.where, bf16[512,1024]{1,0:T(8,128)(2,1)S(1)} %collective-permute-done.tok_b, bf16[16,512]{1,0:T(8,128)(2,1)S(1)} %collective-permute-done.1.flags, ...), custom_call_target="tpu_custom_call" | custom-call | tf_op jit(solution)/shard_map/pallas_call | solution.py:243
  6.2 2.3 %collective-permute-start.6 = (bf16[4,464,128]{2,1,0:T(8,128)(2,1)S(1)}, bf16[4,464,128]{2,1,0:T(8,128)(2,1)S(1)}, u32[]{:S(2)}, u32[]{:S(2)}) collective-permute-start(bf16[4,464,128]{2,1,0:T(8,128)(2,1)S(1)} %get-tuple-element.32), channel_id=1, source_target_pairs={{0,2},{1,3},{2,0},{3,1},{4,6},{5,7},{6,4},{7,5},{8,10},{9,11},{10,... | collective-permute-start | bytes 1425416 | tf_op jit(solution)/shard_map/ppermute | solution.py:253
  8.5 0.0 copy-done.1
  8.5 1.6 %shard_map.48 = (f32[2,656,128]{2,1,0:T(8,128)S(1)}, bf16[2,656,128]{2,1,0:T(8,128)(2,1)S(1)}) custom-call(s32[3]{0:T(128)S(1)} %pad_add_fusion.where, bf16[2048,512]{1,0:T(8,128)(2,1)S(1)} %get-tuple-element.34.lhs_a, bf16[512,1024]{1,0:T(8,128)(2,1)S(1)} %copy-done.1, bf16[2048,512]{1,0:T(8,128)(2,1)S(1)} %get-tuple-element.35.lhs_b, ...), custom_call_target="tpu_custom_call" | custom-call | tf_op jit(solution)/shard_map/pallas_call | solution.py:243
  10.0 1.4 %collective-permute-start.2 = (bf16[2,656,128]{2,1,0:T(8,128)(2,1)S(1)}, bf16[2,656,128]{2,1,0:T(8,128)(2,1)S(1)}, u32[]{:S(2)}, u32[]{:S(2)}) collective-permute-start(bf16[2,656,128]{2,1,0:T(8,128)(2,1)S(1)} %get-tuple-element.37), channel_id=1, source_target_pairs={{0,4},{4,0},{8,12},{12,8},{1,5},{5,1},{9,13},{13,9},{2,6},{6,2},{1... | collective-permute-start | bytes 1007624 | tf_op jit(solution)/shard_map/ppermute | solution.py:253
  11.4 1.5 %shard_map.49 = (f32[4,320,128]{2,1,0:T(8,128)S(1)}, bf16[4,320,128]{2,1,0:T(8,128)(2,1)S(1)}) custom-call(s32[3]{0:T(128)S(1)} %pad_add_fusion.where, bf16[2048,512]{1,0:T(8,128)(2,1)S(1)} %get-tuple-element.34.lhs_a, bf16[512,1024]{1,0:T(8,128)(2,1)S(1)} %copy-done.1, bf16[2048,512]{1,0:T(8,128)(2,1)S(1)} %get-tuple-element.35.lhs_b, ...), custom_call_target="tpu_custom_call" | custom-call | tf_op jit(solution)/shard_map/pallas_call | solution.py:243
  12.9 0.3 collective-permute-start.12
  13.3 6.0 %collective-permute-done.6.got = bf16[4,464,128]{2,1,0:T(8,128)(2,1)S(1)} collective-permute-done((bf16[4,464,128]{2,1,0:T(8,128)(2,1)S(1)}, bf16[4,464,128]{2,1,0:T(8,128)(2,1)S(1)}, u32[]{:S(2)}, u32[]{:S(2)}) %collective-permute-start.6) | collective-permute-done | bytes 475168 | tf_op jit(solution)/shard_map/ppermute | solution.py:253
  19.3 0.1 shard_map.53
  19.4 1.3 %collective-permute-start.7 = (bf16[2,464,128]{2,1,0:T(8,128)(2,1)S(1)}, bf16[2,464,128]{2,1,0:T(8,128)(2,1)S(1)}, u32[]{:S(2)}, u32[]{:S(2)}) collective-permute-start(bf16[2,464,128]{2,1,0:T(8,128)(2,1)S(1)} %get-tuple-element.46), channel_id=1, source_target_pairs={{0,4},{4,0},{8,12},{12,8},{1,5},{5,1},{9,13},{13,9},{2,6},{6,2},{1... | collective-permute-start | bytes 712712 | tf_op jit(solution)/shard_map/ppermute | solution.py:253
  20.6 0.0 collective-permute-done.2.got
  20.7 0.1 shard_map.50
  20.7 2.4 %collective-permute-start.3 = (bf16[656,128]{1,0:T(8,128)(2,1)S(1)}, bf16[656,128]{1,0:T(8,128)(2,1)S(1)}, u32[]{:S(2)}, u32[]{:S(2)}) collective-permute-start(bf16[656,128]{1,0:T(8,128)(2,1)S(1)} %get-tuple-element.42), channel_id=1, source_target_pairs={{0,8},{4,12},{8,0},{12,4},{1,9},{5,13},{9,1},{13,5},{2,10},{6,14},... | collective-permute-start | bytes 503816 | tf_op jit(solution)/shard_map/ppermute | solution.py:253
  23.1 3.2 %collective-permute-done.12.got = bf16[4,320,128]{2,1,0:T(8,128)(2,1)S(1)} collective-permute-done((bf16[4,320,128]{2,1,0:T(8,128)(2,1)S(1)}, bf16[4,320,128]{2,1,0:T(8,128)(2,1)S(1)}, u32[]{:S(2)}, u32[]{:S(2)}) %collective-permute-start.12) | collective-permute-done | bytes 327712 | tf_op jit(solution)/shard_map/ppermute | solution.py:253
  26.3 0.1 shard_map.57
  26.4 0.0 copy-start.2
  26.4 0.0 copy-start.3
  26.4 1.3 %collective-permute-start.13 = (bf16[2,320,128]{2,1,0:T(8,128)(2,1)S(1)}, bf16[2,320,128]{2,1,0:T(8,128)(2,1)S(1)}, u32[]{:S(2)}, u32[]{:S(2)}) collective-permute-start(bf16[2,320,128]{2,1,0:T(8,128)(2,1)S(1)} %get-tuple-element.53), channel_id=1, source_target_pairs={{0,4},{4,0},{8,12},{12,8},{1,5},{5,1},{9,13},{13,9},{2,6},{6,2},{1... | collective-permute-start | bytes 491528 | tf_op jit(solution)/shard_map/ppermute | solution.py:253
  27.7 0.0 collective-permute-done.7.got
  27.7 0.1 shard_map.54
  27.7 2.4 %collective-permute-start.8 = (bf16[464,128]{1,0:T(8,128)(2,1)S(1)}, bf16[464,128]{1,0:T(8,128)(2,1)S(1)}, u32[]{:S(2)}, u32[]{:S(2)}) collective-permute-start(bf16[464,128]{1,0:T(8,128)(2,1)S(1)} %get-tuple-element.48), channel_id=1, source_target_pairs={{0,8},{4,12},{8,0},{12,4},{1,9},{5,13},{9,1},{13,5},{2,10},{6,14},... | collective-permute-start | bytes 356360 | tf_op jit(solution)/shard_map/ppermute | solution.py:253
  30.1 0.0 collective-permute-done.3.refs_1_
  30.2 1.3 %collective-permute-start.4 = (bf16[656,128]{1,0:T(8,128)(2,1)S(1)}, bf16[656,128]{1,0:T(8,128)(2,1)S(1)}, u32[]{:S(2)}, u32[]{:S(2)}) collective-permute-start(bf16[656,128]{1,0:T(8,128)(2,1)S(1)} %shard_map.51.refs_0_), channel_id=1, source_target_pairs={{0,2},{1,3},{2,0},{3,1},{4,6},{5,7},{6,4},{7,5},{8,10},{9,11},{10,... | collective-permute-start | bytes 503816 | tf_op jit(solution)/shard_map/ppermute | solution.py:253
  31.4 3.5 %collective-permute-done.13.got = bf16[2,320,128]{2,1,0:T(8,128)(2,1)S(1)} collective-permute-done((bf16[2,320,128]{2,1,0:T(8,128)(2,1)S(1)}, bf16[2,320,128]{2,1,0:T(8,128)(2,1)S(1)}, u32[]{:S(2)}, u32[]{:S(2)}) %collective-permute-start.13) | collective-permute-done | bytes 163872 | tf_op jit(solution)/shard_map/ppermute | solution.py:253
  35.0 0.1 collective-permute-start.14
  35.1 0.0 collective-permute-done.8.refs_1_
  35.1 1.3 %collective-permute-start.10 = (bf16[464,128]{1,0:T(8,128)(2,1)S(1)}, bf16[464,128]{1,0:T(8,128)(2,1)S(1)}, u32[]{:S(2)}, u32[]{:S(2)}) collective-permute-start(bf16[464,128]{1,0:T(8,128)(2,1)S(1)} %shard_map.55.refs_2_), channel_id=1, source_target_pairs={{0,2},{1,3},{2,0},{3,1},{4,6},{5,7},{6,4},{7,5},{8,10},{9,11},{10,... | collective-permute-start | bytes 356360 | tf_op jit(solution)/shard_map/ppermute | solution.py:253
  36.4 0.0 collective-permute-done.4.refs_1_
  36.5 5.8 %collective-permute-start.5 = (bf16[656,128]{1,0:T(8,128)(2,1)S(1)}, bf16[656,128]{1,0:T(8,128)(2,1)S(1)}, u32[]{:S(2)}, u32[]{:S(2)}) collective-permute-start(bf16[656,128]{1,0:T(8,128)(2,1)S(1)} %shard_map.52.refs_0_), channel_id=1, source_target_pairs={{0,1},{1,0},{2,3},{3,2},{4,5},{5,4},{6,7},{7,6},{8,9},{9,8},{10,11... | collective-permute-start | bytes 503816 | tf_op jit(solution)/shard_map/ppermute | solution.py:253
  42.3 0.0 collective-permute-done.14.refs_1_
  42.3 1.5 %collective-permute-start.16 = (bf16[320,128]{1,0:T(8,128)(2,1)S(1)}, bf16[320,128]{1,0:T(8,128)(2,1)S(1)}, u32[]{:S(2)}, u32[]{:S(2)}) collective-permute-start(bf16[320,128]{1,0:T(8,128)(2,1)S(1)} %shard_map.59.refs_0_), channel_id=1, source_target_pairs={{0,2},{1,3},{2,0},{3,1},{4,6},{5,7},{6,4},{7,5},{8,10},{9,11},{10,... | collective-permute-start | bytes 245768 | tf_op jit(solution)/shard_map/ppermute | solution.py:253
  43.8 0.8 %collective-permute-start.9 = (bf16[464,128]{1,0:T(8,128)(2,1)S(1)}, bf16[464,128]{1,0:T(8,128)(2,1)S(1)}, u32[]{:S(2)}, u32[]{:S(2)}) collective-permute-start(bf16[464,128]{1,0:T(8,128)(2,1)S(1)} %shard_map.55.refs_2_), channel_id=1, source_target_pairs={{0,1},{1,0},{2,3},{3,2},{4,5},{5,4},{6,7},{7,6},{8,9},{9,8},{10,11... | collective-permute-start | bytes 356360 | tf_op jit(solution)/shard_map/ppermute | solution.py:253
  44.6 0.0 collective-permute-done.10.refs_4_
  44.7 1.2 %collective-permute-start.11 = (bf16[464,128]{1,0:T(8,128)(2,1)S(1)}, bf16[464,128]{1,0:T(8,128)(2,1)S(1)}, u32[]{:S(2)}, u32[]{:S(2)}) collective-permute-start(bf16[464,128]{1,0:T(8,128)(2,1)S(1)} %collective-permute-done.10.refs_4_), channel_id=1, source_target_pairs={{0,1},{1,0},{2,3},{3,2},{4,5},{5,4},{6,7},{7,6},{8,9},{9,8},{10,11... | collective-permute-start | bytes 356360 | tf_op jit(solution)/shard_map/ppermute | solution.py:253
  45.9 0.0 collective-permute-start.15
  45.9 0.7 %collective-permute-done.16.refs_2_ = bf16[320,128]{1,0:T(8,128)(2,1)S(1)} collective-permute-done((bf16[320,128]{1,0:T(8,128)(2,1)S(1)}, bf16[320,128]{1,0:T(8,128)(2,1)S(1)}, u32[]{:S(2)}, u32[]{:S(2)}) %collective-permute-start.16) | collective-permute-done | bytes 81952 | tf_op jit(solution)/shard_map/ppermute | solution.py:253
  46.6 0.9 %collective-permute-start.17 = (bf16[320,128]{1,0:T(8,128)(2,1)S(1)}, bf16[320,128]{1,0:T(8,128)(2,1)S(1)}, u32[]{:S(2)}, u32[]{:S(2)}) collective-permute-start(bf16[320,128]{1,0:T(8,128)(2,1)S(1)} %collective-permute-done.16.refs_2_), channel_id=1, source_target_pairs={{0,1},{1,0},{2,3},{3,2},{4,5},{5,4},{6,7},{7,6},{8,9},{9,8},{10,11... | collective-permute-start | bytes 245768 | tf_op jit(solution)/shard_map/ppermute | solution.py:253
  47.4 0.0 collective-permute-done.5.refs_1_
  47.4 0.0 collective-permute-done.9.refs_3_
  47.5 0.0 collective-permute-done.11.refs_5_
  47.5 1.2 %shard_map.56 = (bf16[1024,1024]{1,0:T(8,128)(2,1)S(1)}, f32[32,128]{1,0:T(8,128)S(1)}) custom-call(s32[3]{0:T(128)S(1)} %pad_add_fusion.where, bf16[656,128]{1,0:T(8,128)(2,1)S(1)} %shard_map.52.refs_0_, bf16[656,128]{1,0:T(8,128)(2,1)S(1)} %collective-permute-done.5.refs_1_, bf16[464,128]{1,0:T(8,128)(2,1)S(1)} %shard_map.55.refs_2_, ...), custom_call_target="tpu_custom_call" | custom-call | tf_op jit(solution)/shard_map/pallas_call | solution.py:243
  48.7 0.0 collective-permute-done.15.refs_1_
  48.7 0.0 collective-permute-done.17.refs_3_
  48.7 0.0 copy-done.2
  48.7 0.0 copy-done.3
  48.7 3.4 %shard_map.60 = (f32[128,1024]{1,0:T(8,128)}, bf16[1024,1024]{1,0:T(8,128)(2,1)S(1)}) custom-call(s32[3]{0:T(128)S(1)} %pad_add_fusion.where, f32[128,1024]{1,0:T(8,128)S(1)} %bitcast.7, s32[128,1024]{1,0:T(8,128)S(1)} %bitcast.8, bf16[1024,1024]{1,0:T(8,128)(2,1)S(1)} %get-tuple-element.49.old, ...), custom_call_target="tpu_custom_call", output_to_operand_aliasing={{1}: (3, {})} | custom-call | tf_op jit(solution)/shard_map/pallas_call | solution.py:243
  (7 shorter events, 0.2 us)
Async XLA Ops:
  0.0 4.4 %collective-permute-start = (bf16[512,1024]{1,0:T(8,128)(2,1)}, bf16[512,1024]{1,0:T(8,128)(2,1)S(1)}, u32[]{:S(2)}, u32[]{:S(2)}) collective-permute-start(bf16[512,1024]{1,0:T(8,128)(2,1)} %tok_a.3), channel_id=1, source_target_pairs={{0,1},{1,0},{2,3},{3,2},{4,5},{5,4},{6,7},{7,6},{8,9},{9,8},{10,11... | collective-permute-start | bytes 3145736 | tf_op jit(solution)/shard_map/ppermute | solution.py:253
  0.8 3.5 %collective-permute-start.1 = (bf16[16,512]{1,0:T(8,128)(2,1)S(1)}, bf16[16,512]{1,0:T(8,128)(2,1)S(1)}, u32[]{:S(2)}, u32[]{:S(2)}) collective-permute-start(bf16[16,512]{1,0:T(8,128)(2,1)S(1)} %convert_element_type.3.flags), channel_id=1, source_target_pairs={{0,1},{1,0},{2,3},{3,2},{4,5},{5,4},{6,7},{7,6},{8,9},{9,8},{10,11... | collective-permute-start | bytes 49160 | tf_op jit(solution)/shard_map/ppermute | solution.py:253
  1.4 1.2 %copy-start = (bf16[512,1024]{1,0:T(8,128)(2,1)S(1)}, bf16[512,1024]{1,0:T(8,128)(2,1)}, u32[]{:S(2)}) copy-start(bf16[512,1024]{1,0:T(8,128)(2,1)} %tok_a.3) | copy-start | bytes 3145732
  2.7 5.8 %copy-start.1 = (bf16[512,1024]{1,0:T(8,128)(2,1)S(1)}, bf16[512,1024]{1,0:T(8,128)(2,1)}, u32[]{:S(2)}) copy-start(bf16[512,1024]{1,0:T(8,128)(2,1)} %tok_a.3) | copy-start | bytes 3145732
  6.2 13.1 %collective-permute-start.6 = (bf16[4,464,128]{2,1,0:T(8,128)(2,1)S(1)}, bf16[4,464,128]{2,1,0:T(8,128)(2,1)S(1)}, u32[]{:S(2)}, u32[]{:S(2)}) collective-permute-start(bf16[4,464,128]{2,1,0:T(8,128)(2,1)S(1)} %get-tuple-element.32), channel_id=1, source_target_pairs={{0,2},{1,3},{2,0},{3,1},{4,6},{5,7},{6,4},{7,5},{8,10},{9,11},{10,... | collective-permute-start | bytes 1425416 | tf_op jit(solution)/shard_map/ppermute | solution.py:253
  10.0 10.6 %collective-permute-start.2 = (bf16[2,656,128]{2,1,0:T(8,128)(2,1)S(1)}, bf16[2,656,128]{2,1,0:T(8,128)(2,1)S(1)}, u32[]{:S(2)}, u32[]{:S(2)}) collective-permute-start(bf16[2,656,128]{2,1,0:T(8,128)(2,1)S(1)} %get-tuple-element.37), channel_id=1, source_target_pairs={{0,4},{4,0},{8,12},{12,8},{1,5},{5,1},{9,13},{13,9},{2,6},{6,2},{1... | collective-permute-start | bytes 1007624 | tf_op jit(solution)/shard_map/ppermute | solution.py:253
  12.9 13.4 %collective-permute-start.12 = (bf16[4,320,128]{2,1,0:T(8,128)(2,1)S(1)}, bf16[4,320,128]{2,1,0:T(8,128)(2,1)S(1)}, u32[]{:S(2)}, u32[]{:S(2)}) collective-permute-start(bf16[4,320,128]{2,1,0:T(8,128)(2,1)S(1)} %get-tuple-element.39), channel_id=1, source_target_pairs={{0,2},{1,3},{2,0},{3,1},{4,6},{5,7},{6,4},{7,5},{8,10},{9,11},{10,... | collective-permute-start | bytes 983048 | tf_op jit(solution)/shard_map/ppermute | solution.py:253
  19.4 8.3 %collective-permute-start.7 = (bf16[2,464,128]{2,1,0:T(8,128)(2,1)S(1)}, bf16[2,464,128]{2,1,0:T(8,128)(2,1)S(1)}, u32[]{:S(2)}, u32[]{:S(2)}) collective-permute-start(bf16[2,464,128]{2,1,0:T(8,128)(2,1)S(1)} %get-tuple-element.46), channel_id=1, source_target_pairs={{0,4},{4,0},{8,12},{12,8},{1,5},{5,1},{9,13},{13,9},{2,6},{6,2},{1... | collective-permute-start | bytes 712712 | tf_op jit(solution)/shard_map/ppermute | solution.py:253
  20.7 9.4 %collective-permute-start.3 = (bf16[656,128]{1,0:T(8,128)(2,1)S(1)}, bf16[656,128]{1,0:T(8,128)(2,1)S(1)}, u32[]{:S(2)}, u32[]{:S(2)}) collective-permute-start(bf16[656,128]{1,0:T(8,128)(2,1)S(1)} %get-tuple-element.42), channel_id=1, source_target_pairs={{0,8},{4,12},{8,0},{12,4},{1,9},{5,13},{9,1},{13,5},{2,10},{6,14},... | collective-permute-start | bytes 503816 | tf_op jit(solution)/shard_map/ppermute | solution.py:253
  26.4 22.3 %copy-start.2 = (f32[1,128,1024]{2,1,0:T(8,128)S(1)}, f32[1,128,1024]{2,1,0:T(8,128)}, u32[]{:S(2)}) copy-start(f32[1,128,1024]{2,1,0:T(8,128)} %param.6) | copy-start | bytes 1572868
  26.4 22.3 %copy-start.3 = (s32[1,128,1024]{2,1,0:T(8,128)S(1)}, s32[1,128,1024]{2,1,0:T(8,128)}, u32[]{:S(2)}) copy-start(s32[1,128,1024]{2,1,0:T(8,128)} %param.7) | copy-start | bytes 1572868
  26.4 8.5 %collective-permute-start.13 = (bf16[2,320,128]{2,1,0:T(8,128)(2,1)S(1)}, bf16[2,320,128]{2,1,0:T(8,128)(2,1)S(1)}, u32[]{:S(2)}, u32[]{:S(2)}) collective-permute-start(bf16[2,320,128]{2,1,0:T(8,128)(2,1)S(1)} %get-tuple-element.53), channel_id=1, source_target_pairs={{0,4},{4,0},{8,12},{12,8},{1,5},{5,1},{9,13},{13,9},{2,6},{6,2},{1... | collective-permute-start | bytes 491528 | tf_op jit(solution)/shard_map/ppermute | solution.py:253
  27.7 7.3 %collective-permute-start.8 = (bf16[464,128]{1,0:T(8,128)(2,1)S(1)}, bf16[464,128]{1,0:T(8,128)(2,1)S(1)}, u32[]{:S(2)}, u32[]{:S(2)}) collective-permute-start(bf16[464,128]{1,0:T(8,128)(2,1)S(1)} %get-tuple-element.48), channel_id=1, source_target_pairs={{0,8},{4,12},{8,0},{12,4},{1,9},{5,13},{9,1},{13,5},{2,10},{6,14},... | collective-permute-start | bytes 356360 | tf_op jit(solution)/shard_map/ppermute | solution.py:253
  30.2 6.2 %collective-permute-start.4 = (bf16[656,128]{1,0:T(8,128)(2,1)S(1)}, bf16[656,128]{1,0:T(8,128)(2,1)S(1)}, u32[]{:S(2)}, u32[]{:S(2)}) collective-permute-start(bf16[656,128]{1,0:T(8,128)(2,1)S(1)} %shard_map.51.refs_0_), channel_id=1, source_target_pairs={{0,2},{1,3},{2,0},{3,1},{4,6},{5,7},{6,4},{7,5},{8,10},{9,11},{10,... | collective-permute-start | bytes 503816 | tf_op jit(solution)/shard_map/ppermute | solution.py:253
  35.0 7.3 %collective-permute-start.14 = (bf16[320,128]{1,0:T(8,128)(2,1)S(1)}, bf16[320,128]{1,0:T(8,128)(2,1)S(1)}, u32[]{:S(2)}, u32[]{:S(2)}) collective-permute-start(bf16[320,128]{1,0:T(8,128)(2,1)S(1)} %get-tuple-element.55), channel_id=1, source_target_pairs={{0,8},{4,12},{8,0},{12,4},{1,9},{5,13},{9,1},{13,5},{2,10},{6,14},... | collective-permute-start | bytes 245768 | tf_op jit(solution)/shard_map/ppermute | solution.py:253
  35.1 9.5 %collective-permute-start.10 = (bf16[464,128]{1,0:T(8,128)(2,1)S(1)}, bf16[464,128]{1,0:T(8,128)(2,1)S(1)}, u32[]{:S(2)}, u32[]{:S(2)}) collective-permute-start(bf16[464,128]{1,0:T(8,128)(2,1)S(1)} %shard_map.55.refs_2_), channel_id=1, source_target_pairs={{0,2},{1,3},{2,0},{3,1},{4,6},{5,7},{6,4},{7,5},{8,10},{9,11},{10,... | collective-permute-start | bytes 356360 | tf_op jit(solution)/shard_map/ppermute | solution.py:253
  36.5 11.0 %collective-permute-start.5 = (bf16[656,128]{1,0:T(8,128)(2,1)S(1)}, bf16[656,128]{1,0:T(8,128)(2,1)S(1)}, u32[]{:S(2)}, u32[]{:S(2)}) collective-permute-start(bf16[656,128]{1,0:T(8,128)(2,1)S(1)} %shard_map.52.refs_0_), channel_id=1, source_target_pairs={{0,1},{1,0},{2,3},{3,2},{4,5},{5,4},{6,7},{7,6},{8,9},{9,8},{10,11... | collective-permute-start | bytes 503816 | tf_op jit(solution)/shard_map/ppermute | solution.py:253
  42.3 4.3 %collective-permute-start.16 = (bf16[320,128]{1,0:T(8,128)(2,1)S(1)}, bf16[320,128]{1,0:T(8,128)(2,1)S(1)}, u32[]{:S(2)}, u32[]{:S(2)}) collective-permute-start(bf16[320,128]{1,0:T(8,128)(2,1)S(1)} %shard_map.59.refs_0_), channel_id=1, source_target_pairs={{0,2},{1,3},{2,0},{3,1},{4,6},{5,7},{6,4},{7,5},{8,10},{9,11},{10,... | collective-permute-start | bytes 245768 | tf_op jit(solution)/shard_map/ppermute | solution.py:253
  43.8 3.6 %collective-permute-start.9 = (bf16[464,128]{1,0:T(8,128)(2,1)S(1)}, bf16[464,128]{1,0:T(8,128)(2,1)S(1)}, u32[]{:S(2)}, u32[]{:S(2)}) collective-permute-start(bf16[464,128]{1,0:T(8,128)(2,1)S(1)} %shard_map.55.refs_2_), channel_id=1, source_target_pairs={{0,1},{1,0},{2,3},{3,2},{4,5},{5,4},{6,7},{7,6},{8,9},{9,8},{10,11... | collective-permute-start | bytes 356360 | tf_op jit(solution)/shard_map/ppermute | solution.py:253
  44.7 2.8 %collective-permute-start.11 = (bf16[464,128]{1,0:T(8,128)(2,1)S(1)}, bf16[464,128]{1,0:T(8,128)(2,1)S(1)}, u32[]{:S(2)}, u32[]{:S(2)}) collective-permute-start(bf16[464,128]{1,0:T(8,128)(2,1)S(1)} %collective-permute-done.10.refs_4_), channel_id=1, source_target_pairs={{0,1},{1,0},{2,3},{3,2},{4,5},{5,4},{6,7},{7,6},{8,9},{9,8},{10,11... | collective-permute-start | bytes 356360 | tf_op jit(solution)/shard_map/ppermute | solution.py:253
  45.9 2.8 %collective-permute-start.15 = (bf16[320,128]{1,0:T(8,128)(2,1)S(1)}, bf16[320,128]{1,0:T(8,128)(2,1)S(1)}, u32[]{:S(2)}, u32[]{:S(2)}) collective-permute-start(bf16[320,128]{1,0:T(8,128)(2,1)S(1)} %shard_map.59.refs_0_), channel_id=1, source_target_pairs={{0,1},{1,0},{2,3},{3,2},{4,5},{5,4},{6,7},{7,6},{8,9},{9,8},{10,11... | collective-permute-start | bytes 245768 | tf_op jit(solution)/shard_map/ppermute | solution.py:253
  46.6 2.1 %collective-permute-start.17 = (bf16[320,128]{1,0:T(8,128)(2,1)S(1)}, bf16[320,128]{1,0:T(8,128)(2,1)S(1)}, u32[]{:S(2)}, u32[]{:S(2)}) collective-permute-start(bf16[320,128]{1,0:T(8,128)(2,1)S(1)} %collective-permute-done.16.refs_2_), channel_id=1, source_target_pairs={{0,1},{1,0},{2,3},{3,2},{4,5},{5,4},{6,7},{7,6},{8,9},{9,8},{10,11... | collective-permute-start | bytes 245768 | tf_op jit(solution)/shard_map/ppermute | solution.py:253
